TPU v7x, 32 devices: a whole 2x2x4 slice. The times are simulated.
32 devices in a mesh: section: 2 (over x), dp: 8 (over z, core), tensor: 2 (over y).
Axes of the slice: x: 2, y: 2, z: 4, core: 2. Of those that a mesh axis runs over, the one named last changes fastest.
Arguments:
- ends_in: bfloat16 [2, 2, 2048, 2048], P('section', None, ('dp', 'tensor')), may hold values from -6 to 6
- pieces: int32 [2, 2], replicated, may hold values from 0 to 1792, as said below
- w_query: bfloat16 [2, 2048, 2048], P('section', 'dp', 'tensor'), may hold values from -0.125 to 0.125
- w_keyval: bfloat16 [2, 2048, 256], P('section', ('dp', 'tensor')), may hold values from -0.125 to 0.125
- w_output: bfloat16 [2, 2048, 2048], P('section', 'tensor', 'dp'), may hold values from -1.5 to 1.5
- w_hidden: bfloat16 [2, 2048, 8192], P('section', 'dp', 'tensor'), may hold values from -0.125 to 0.125
- w_project: bfloat16 [2, 8192, 2048], P('section', 'tensor', 'dp'), may hold values from -0.0625 to 0.0625
- norm_params: bfloat16 [2, 4, 2048], P('section', None, ('dp', 'tensor')), as said below
Outputs:
- ends_out: float32 [2, 2, 2048, 2048], P('section', None, ('dp', 'tensor'))
- grad_query: float32 [2, 2048, 2048], P('section', 'dp', 'tensor')
- grad_keyval: float32 [2, 2048, 256], P('section', ('dp', 'tensor'))
- grad_output: float32 [2, 2048, 2048], P('section', 'tensor', 'dp')
- grad_hidden: float32 [2, 2048, 8192], P('section', 'dp', 'tensor')
- grad_project: float32 [2, 8192, 2048], P('section', 'tensor', 'dp')
- grad_norms: float32 [2, 3, 2048], P('section', None, ('dp', 'tensor'))
- grad_shift: float32 [2, 2048], P('section', ('dp', 'tensor'))
Inputs may be any that keep to these rules, and one draw needn't show every extreme that they name: Each sequence has 2 picture pieces of 256 positions; the j-th starts between j * (1024) and (j + 1) * 1024 - 256. `norm_params`: gains in rows 0 and 2 lie between 0.5 and 1.5.
All inputs are finite; a program needn't handle non-finite values.
Results may differ from a plain program's by a relative error of at most 0.02.
Values may be sent and summed in bfloat16 or wider, within the bound.
No kernel may reach another device: no remote copies, remote signals or barrier semaphores. Data moves between devices by JAX's collectives and lax.ppermute only.
A program may use at most 384 MiB of HBM per device.

v0:
```python
import jax
import jax.numpy as jnp
from jax import lax
from jax.sharding import PartitionSpec as P

SPAN = 256
MICRO = 2


EPSILON = 1e-05
NEGATIVE = -1000000000.0


def in_blocks(array, dim, devices):
    shape = array.shape
    blocks = array.reshape(*shape[:dim], devices, shape[dim] // devices, *shape[dim + 1 :])
    return jnp.moveaxis(blocks, dim, 0)


def sum_at_owner(array, axis, dim):
    devices = lax.axis_size(axis)
    blocks = lax.all_to_all(in_blocks(array, dim, devices), axis, 0, 0, tiled=True)
    return jnp.sum(blocks.astype(jnp.float32), axis=0)


def from_behind(block, axis, distance):
    devices = range(lax.axis_size(axis))
    route = [(i - distance, i) for i in devices if i - distance in devices]
    return lax.ppermute(block, axis, route)


def layer_norm(values, scale_row, shift_row):
    centered = values - jnp.mean(values, -1, keepdims=True)
    spread = jnp.mean(centered * centered, -1, keepdims=True)
    return centered * lax.rsqrt(spread + EPSILON) * scale_row + shift_row


def gelu_tanh(values):
    return jax.nn.gelu(values, approximate=True)


def spread_rows(values):
    return lax.all_gather(values, "tensor", axis=1, tiled=True)


def collect_rows(terms):
    return lax.psum_scatter(
        terms.astype(jnp.bfloat16), "tensor", scatter_dimension=1, tiled=True
    ).astype(jnp.float32)


def spread_grads(values):
    return lax.all_gather(values, "tensor", axis=1, tiled=True)


def collect_grads(terms):
    return lax.psum_scatter(
        terms.astype(jnp.bfloat16), "tensor", scatter_dimension=1, tiled=True
    ).astype(jnp.float32)


def allowed_keys(starts, query_start, query_rows, length):
    query_pos = query_start + jnp.arange(query_rows, dtype=jnp.int32)
    key_pos = jnp.arange(length, dtype=jnp.int32)
    causal = key_pos[None, :] <= query_pos[:, None]
    query_in = (query_pos[None, None, :] >= starts[:, :, None]) & (
        query_pos[None, None, :] < starts[:, :, None] + SPAN
    )
    key_in = (key_pos[None, None, :] >= starts[:, :, None]) & (
        key_pos[None, None, :] < starts[:, :, None] + SPAN
    )
    shared_piece = jnp.any(query_in[:, :, :, None] & key_in[:, :, None, :], axis=1)
    return causal[None] | shared_piece


def scores_of(queries, keyval_all, allowed):
    head_size = keyval_all.shape[-1] // 2
    queries_four = queries.reshape(queries.shape[0], queries.shape[1], -1, head_size)
    keys_part = keyval_all[..., :head_size]
    scores = jnp.einsum(
        "sqhd,skd->shqk", queries_four, keys_part, preferred_element_type=jnp.float32
    ) * head_size ** (-0.5)
    return (jnp.where(allowed[:, None], scores, NEGATIVE), queries_four)


def attend_forward(queries, keyval_all, allowed):
    head_size = keyval_all.shape[-1] // 2
    scores, queries_four = scores_of(queries, keyval_all, allowed)
    peak = jnp.max(scores, -1, keepdims=True)
    log_total = peak + jnp.log(jnp.sum(jnp.exp(scores - peak), -1, keepdims=True))
    probs = jnp.exp(scores - log_total).astype(jnp.bfloat16)
    values_part = keyval_all[..., head_size:]
    attended = jnp.einsum(
        "shqk,skd->sqhd", probs, values_part, preferred_element_type=jnp.float32
    ).astype(jnp.bfloat16)
    return (log_total, attended.reshape(queries.shape))


def attend_backward(queries, keyval_all, log_total, grad_attended, allowed):
    head_size = keyval_all.shape[-1] // 2
    scores, queries_four = scores_of(queries, keyval_all, allowed)
    probs = jnp.exp(scores - log_total)
    keys_part = keyval_all[..., :head_size]
    values_part = keyval_all[..., head_size:]
    grad_four = grad_attended.reshape(queries_four.shape)
    grad_probs = jnp.einsum(
        "sqhd,skd->shqk", grad_four, values_part, preferred_element_type=jnp.float32
    )
    grad_values = jnp.einsum(
        "shqk,sqhd->skd", probs.astype(jnp.bfloat16), grad_four, preferred_element_type=jnp.float32
    )
    weighted = jnp.sum(probs * grad_probs, -1, keepdims=True)
    grad_scores = (probs * (grad_probs - weighted) * head_size ** (-0.5)).astype(jnp.bfloat16)
    grad_queries = jnp.einsum(
        "shqk,skd->sqhd", grad_scores, keys_part, preferred_element_type=jnp.float32
    )
    grad_queries = grad_queries.astype(jnp.bfloat16).reshape(queries.shape)
    grad_keys = jnp.einsum(
        "shqk,sqhd->skd", grad_scores, queries_four, preferred_element_type=jnp.float32
    )
    return (grad_queries, jnp.concatenate([grad_keys, grad_values], -1))


def layer_forward(inputs, weights, allowed):
    query_mat, keyval_mat, output_mat, hidden_mat, project_mat, norm_table = weights
    normed_local = layer_norm(inputs, norm_table[0], norm_table[1]).astype(jnp.bfloat16)
    keyval_local = jnp.einsum(
        "srd,de->sre", normed_local, keyval_mat, preferred_element_type=jnp.float32
    ).astype(jnp.bfloat16)
    keyval_all = lax.all_gather(keyval_local, ("dp", "tensor"), axis=1, tiled=True)
    normed_rows = spread_rows(normed_local)
    queries = jnp.einsum(
        "sqd,de->sqe", normed_rows, query_mat, preferred_element_type=jnp.float32
    ).astype(jnp.bfloat16)
    log_total, attended = attend_forward(queries, keyval_all, allowed)
    middle = inputs + collect_rows(
        jnp.einsum("sqe,ed->sqd", attended, output_mat, preferred_element_type=jnp.float32)
    )
    mixed_local = layer_norm(middle, norm_table[2], norm_table[3]).astype(jnp.bfloat16)
    mixed_rows = spread_rows(mixed_local)
    hidden_pre = jnp.einsum(
        "sqd,df->sqf", mixed_rows, hidden_mat, preferred_element_type=jnp.float32
    )
    hidden_act = gelu_tanh(hidden_pre).astype(jnp.bfloat16)
    outputs = middle + collect_rows(
        jnp.einsum("sqf,fd->sqd", hidden_act, project_mat, preferred_element_type=jnp.float32)
    )
    saved = (
        normed_local,
        normed_rows,
        keyval_all,
        queries,
        log_total,
        attended,
        middle,
        mixed_rows,
        hidden_pre,
        hidden_act,
    )
    return (outputs, saved)


def input_backward(inputs, grad_out, weights, allowed, saved):
    query_mat, keyval_mat, output_mat, hidden_mat, project_mat, norm_table = weights
    (
        normed_local,
        normed_rows,
        keyval_all,
        queries,
        log_total,
        attended,
        middle,
        mixed_rows,
        hidden_pre,
        hidden_act,
    ) = saved
    grad_branch = spread_grads(grad_out.astype(jnp.bfloat16))
    grad_act = jnp.einsum(
        "sqd,fd->sqf", grad_branch, project_mat, preferred_element_type=jnp.float32
    )
    grad_pre = jax.vjp(gelu_tanh, hidden_pre)[1](grad_act)[0].astype(jnp.bfloat16)
    grad_mixed = collect_grads(
        jnp.einsum("sqf,df->sqd", grad_pre, hidden_mat, preferred_element_type=jnp.float32)
    )
    second_pull = jax.vjp(layer_norm, middle, norm_table[2], norm_table[3])[1]
    grad_mid_norm, grad_gain_two, grad_bias_two = second_pull(grad_mixed)
    grad_middle = grad_out + grad_mid_norm
    grad_attn_rows = spread_grads(grad_middle.astype(jnp.bfloat16))
    grad_attended = jnp.einsum(
        "sqd,ed->sqe", grad_attn_rows, output_mat, preferred_element_type=jnp.float32
    ).astype(jnp.bfloat16)
    grad_queries, keyval_terms = attend_backward(
        queries, keyval_all, log_total, grad_attended, allowed
    )
    grad_keyval = sum_at_owner(keyval_terms.astype(jnp.bfloat16), ("dp", "tensor"), 1).astype(
        jnp.bfloat16
    )
    grad_normed = collect_grads(
        jnp.einsum("sqe,de->sqd", grad_queries, query_mat, preferred_element_type=jnp.float32)
    )
    grad_normed = grad_normed + jnp.einsum(
        "sre,de->srd", grad_keyval, keyval_mat, preferred_element_type=jnp.float32
    )
    first_pull = jax.vjp(layer_norm, inputs, norm_table[0], norm_table[1])[1]
    grad_in_norm, grad_gain_one, grad_bias_one = first_pull(grad_normed)
    grad_inputs = grad_middle + grad_in_norm
    grad_table = jnp.stack([grad_gain_one, grad_bias_one, grad_gain_two, grad_bias_two])
    pairs = (
        (normed_rows, grad_queries),
        (attended, grad_attn_rows),
        (mixed_rows, grad_pre),
        (hidden_act, grad_branch),
        (normed_local, grad_keyval),
    )
    return (grad_inputs, grad_table, pairs)


def weight_products(pairs):
    grad_querymat = jnp.einsum(
        "sqd,sqe->de", pairs[0][0], pairs[0][1], preferred_element_type=jnp.float32
    )
    grad_outmat = jnp.einsum(
        "sqe,sqd->ed", pairs[1][0], pairs[1][1], preferred_element_type=jnp.float32
    )
    grad_hidmat = jnp.einsum(
        "sqd,sqf->df", pairs[2][0], pairs[2][1], preferred_element_type=jnp.float32
    )
    grad_projmat = jnp.einsum(
        "sqf,sqd->fd", pairs[3][0], pairs[3][1], preferred_element_type=jnp.float32
    )
    grad_keyvalmat = jnp.einsum(
        "srd,sre->de", pairs[4][0], pairs[4][1], preferred_element_type=jnp.float32
    )
    return (grad_querymat, grad_outmat, grad_hidmat, grad_projmat, grad_keyvalmat)


def local(ends_in, pieces, w_query, w_keyval, w_output, w_hidden, w_project, norm_params):
    section_index = lax.axis_index("section")
    per_batch = ends_in.shape[1] // MICRO
    rows_local = ends_in.shape[2]
    width = ends_in.shape[3]
    local_ends = ends_in[0].reshape(MICRO, per_batch, rows_local, width)
    starts_all = pieces.reshape(MICRO, per_batch, pieces.shape[1])
    gathered = (
        lax.all_gather(w_query, "dp", axis=1, tiled=True),
        lax.all_gather(w_output, "dp", axis=2, tiled=True),
        lax.all_gather(w_hidden, "dp", axis=1, tiled=True),
        lax.all_gather(w_project, "dp", axis=2, tiled=True),
    )
    shared = (
        lax.all_gather(w_keyval, ("dp", "tensor"), axis=1, tiled=True),
        lax.all_gather(norm_params, ("dp", "tensor"), axis=2, tiled=True),
    )
    weights = (
        gathered[0][0],
        shared[0][0],
        gathered[1][0],
        gathered[2][0],
        gathered[3][0],
        shared[1][0].astype(jnp.float32),
    )
    query_rows = rows_local * lax.axis_size("tensor")
    query_start = lax.axis_index("dp") * query_rows
    length = query_rows * lax.axis_size("dp")
    incoming = jnp.zeros((per_batch, rows_local, width), jnp.bfloat16)
    stored = []
    layer_outs = []
    saved_list = []
    for tick_now in range(MICRO + 1):
        batch_clip = jnp.clip(tick_now - section_index, 0, MICRO - 1)
        starts = lax.dynamic_index_in_dim(starts_all, batch_clip, 0, keepdims=False)
        allowed = allowed_keys(starts, query_start, query_rows, length)
        own_rows = local_ends[min(tick_now, MICRO - 1)]
        inputs_now = jnp.where(section_index == 0, own_rows, incoming)
        stored.append(inputs_now)
        outputs, saved_now = layer_forward(inputs_now.astype(jnp.float32), weights, allowed)
        layer_outs.append(outputs)
        saved_list.append(saved_now)
        if tick_now < MICRO:
            incoming = from_behind(outputs.astype(jnp.bfloat16), "section", 1)
    stored_stack = jnp.stack(stored)
    saved_stack = tuple((jnp.stack(items) for items in zip(*saved_list)))
    totals = tuple(
        (
            jnp.zeros((1,) + arr.shape, jnp.float32)
            for arr in (weights[0], weights[2], weights[3], weights[4], weights[1])
        )
    )
    table_total = jnp.zeros((1,) + weights[5].shape, jnp.float32)
    received = jnp.zeros((per_batch, rows_local, width), jnp.bfloat16)
    input_grads = []
    for tick_now in range(MICRO + 1):
        batch_index = tick_now - 1 + section_index
        valid = ((batch_index >= 0) & (batch_index < MICRO)).astype(jnp.float32)
        batch_clip = jnp.clip(batch_index, 0, MICRO - 1)
        source_tick = jnp.clip(tick_now - 1 + 2 * section_index, 0, MICRO)
        inputs_now = lax.dynamic_index_in_dim(stored_stack, source_tick, 0, keepdims=False).astype(
            jnp.float32
        )
        starts = lax.dynamic_index_in_dim(starts_all, batch_clip, 0, keepdims=False)
        allowed = allowed_keys(starts, query_start, query_rows, length)
        fed_back = local_ends[min(tick_now, MICRO - 1)]
        grad_now = jnp.where(section_index == 1, fed_back, received).astype(jnp.float32)
        saved_now = tuple(
            (lax.dynamic_index_in_dim(item, source_tick, 0, keepdims=False) for item in saved_stack)
        )
        grad_inputs, grad_table, pairs = input_backward(
            inputs_now, grad_now, weights, allowed, saved_now
        )
        input_grads.append(grad_inputs)
        table_total = table_total + grad_table[None] * valid
        if tick_now < MICRO:
            received = from_behind(grad_inputs.astype(jnp.bfloat16), "section", -1)
        products = weight_products(pairs)
        totals = tuple((total + term[None] * valid for total, term in zip(totals, products)))
    large_part = (
        lax.psum_scatter(
            totals[0].astype(jnp.bfloat16), "dp", scatter_dimension=1, tiled=True
        ).astype(jnp.float32),
        lax.psum_scatter(
            totals[1].astype(jnp.bfloat16), "dp", scatter_dimension=2, tiled=True
        ).astype(jnp.float32),
        lax.psum_scatter(
            totals[2].astype(jnp.bfloat16), "dp", scatter_dimension=1, tiled=True
        ).astype(jnp.float32),
        lax.psum_scatter(
            totals[3].astype(jnp.bfloat16), "dp", scatter_dimension=2, tiled=True
        ).astype(jnp.float32),
    )
    small_part = (
        lax.psum_scatter(totals[4], ("dp", "tensor"), scatter_dimension=1, tiled=True),
        lax.psum_scatter(table_total, ("dp", "tensor"), scatter_dimension=2, tiled=True),
    )
    norm_totals = small_part[1]
    result_rows = [
        jnp.where(section_index == 0, input_grads[index + 1], layer_outs[index + 1])
        for index in range(MICRO)
    ]
    ends_out = jnp.stack(result_rows).reshape(1, MICRO * per_batch, rows_local, width)
    return (
        ends_out,
        large_part[0],
        small_part[0],
        large_part[1],
        large_part[2],
        large_part[3],
        norm_totals[:, :3],
        norm_totals[:, 3],
    )


def solution(mesh):
    placed = (
        P("section", None, ("dp", "tensor"), None),
        P(),
        P("section", "dp", "tensor"),
        P("section", ("dp", "tensor"), None),
        P("section", "tensor", "dp"),
        P("section", "dp", "tensor"),
        P("section", "tensor", "dp"),
        P("section", None, ("dp", "tensor")),
    )
    return jax.shard_map(
        local,
        mesh=mesh,
        in_specs=placed,
        out_specs=(
            P("section", None, ("dp", "tensor"), None),
            P("section", "dp", "tensor"),
            P("section", ("dp", "tensor"), None),
            P("section", "tensor", "dp"),
            P("section", "dp", "tensor"),
            P("section", "tensor", "dp"),
            P("section", None, ("dp", "tensor")),
            P("section", ("dp", "tensor")),
        ),
        check_vma=False,
    )
```

profile of v0, /device:TPU:0, one launch (start us, length us, event | category | flops | bytes accessed | tf_op | source)
XLA Modules:
  0.0 2126.4 jit_solution(3505118352944656290)
XLA Ops:
  8.0 34.1 %all_gather.65 = bf16[1,4,2048]{2,1,0:T(4,128)(2,1)S(1)} all-gather(bf16[1,4,128]{2,1,0:T(4,128)(2,1)} %param.15), channel_id=1, replica_groups=mesh['section'=2,'dp'=8,'tensor'=2] {'dp','tensor'}, dimensions={2}, use_global_device_ids=true | all-gather | bytes 17408 | tf_op jit(solution)/shard_map/all_gather | solution.py:252
  61.6 11.8 all-gather.29.cloned.1.call-done
  73.4 48.8 %all-gather.31.cloned.1.call-done = bf16[1,2048,1024]{2,1,0:T(8,128)(2,1)} async-done(((bf16[1,256,1024]{2,1,0:T(8,128)(2,1)}), bf16[1,2048,1024]{2,1,0:T(8,128)(2,1)}) %all-gather.31.cloned.1.call-update) | async-done | bytes 4194320 | tf_op jit(solution)/shard_map/all_gather | solution.py:245
  125.9 35.6 %all-gather.59.cloned.1.call-done = bf16[2048,256]{1,0:T(8,128)(2,1)} async-done(((bf16[128,256]{1,0:T(8,128)(2,1)}), bf16[2048,256]{1,0:T(8,128)(2,1)}) %all-gather.59.cloned.1.call-update) | async-done | bytes 1048592 | tf_op jit(solution)/shard_map/all_gather | solution.py:130
  170.1 9.4 exponential_reduce_fusion.2
  187.7 22.0 %all-gather.33.cloned.1.call-done = bf16[1,1024,2048]{2,1,0:T(8,128)(2,1)} async-done(((bf16[1,1024,256]{2,1,0:T(8,128)(2,1)}), bf16[1,1024,2048]{2,1,0:T(8,128)(2,1)}) %all-gather.33.cloned.1.call-update) | async-done | bytes 4194320 | tf_op jit(solution)/shard_map/all_gather | solution.py:246
  214.2 18.7 reduce-scatter.21.cloned.1.call-done
  240.2 19.7 all-gather.35.cloned.1.call-done
  260.0 152.8 %all-gather.37.cloned.1.call-done = bf16[1,2048,4096]{2,1,0:T(8,128)(2,1)} async-done(((bf16[1,256,4096]{2,1,0:T(8,128)(2,1)}), bf16[1,2048,4096]{2,1,0:T(8,128)(2,1)}) %all-gather.37.cloned.1.call-update) | async-done | bytes 16777232 | tf_op jit(solution)/shard_map/all_gather | solution.py:247
  412.8 12.6 fusion.30
  425.4 139.2 %all-gather.25.cloned.1.call-done = bf16[1,4096,2048]{2,1,0:T(8,128)(2,1)} async-done(((bf16[1,4096,256]{2,1,0:T(8,128)(2,1)}), bf16[1,4096,2048]{2,1,0:T(8,128)(2,1)}) %all-gather.25.cloned.1.call-update) | async-done | bytes 16777232 | tf_op jit(solution)/shard_map/all_gather | solution.py:248
  564.6 12.9 fusion.205
  577.6 18.6 reduce-scatter.23.cloned.1.call-done
  600.8 11.1 collective-permute-done
  618.0 18.3 all-gather.39.cloned.1.call-done
  640.8 36.1 %all-gather.61.cloned.1.call-done = bf16[2048,256]{1,0:T(8,128)(2,1)} async-done(((bf16[128,256]{1,0:T(8,128)(2,1)}), bf16[2048,256]{1,0:T(8,128)(2,1)}) %all-gather.61.cloned.1.call-update) | async-done | bytes 1048592 | tf_op jit(solution)/shard_map/all_gather | solution.py:130
  676.9 9.6 fusion.45
  686.5 9.2 exponential_reduce_fusion.1
  695.7 10.3 fusion.248
  709.6 18.9 reduce-scatter.25.cloned.1.call-done
  734.2 21.4 %all-gather.41.cloned.1.call-done = bf16[1,256,2048]{2,1,0:T(8,128)(2,1)} async-done(((bf16[1,128,2048]{2,1,0:T(8,128)(2,1)}), bf16[1,256,2048]{2,1,0:T(8,128)(2,1)}) %all-gather.41.cloned.1.call-update) | async-done | bytes 1048592 | tf_op jit(solution)/shard_map/all_gather | solution.py:43
  766.0 11.7 fusion.202
  777.8 20.4 reduce-scatter.27.cloned.1.call-done
  802.9 11.1 collective-permute-done.1
  820.0 18.3 all-gather.43.cloned.1.call-done
  842.1 36.9 %all-gather.63.cloned.1.call-done = bf16[2048,256]{1,0:T(8,128)(2,1)} async-done(((bf16[128,256]{1,0:T(8,128)(2,1)}), bf16[2048,256]{1,0:T(8,128)(2,1)}) %all-gather.63.cloned.1.call-update) | async-done | bytes 1048592 | tf_op jit(solution)/shard_map/all_gather | solution.py:130
  896.5 10.3 fusion.251
  909.1 19.3 reduce-scatter.29.cloned.1.call-done
  935.4 20.3 all-gather.45.cloned.1.call-done
  955.7 12.7 fusion.26
  968.4 9.4 pad_maximum_fusion
  978.5 12.0 fusion.74
  990.5 12.0 fusion.196
  1013.2 9.8 reduce-scatter.31.cloned.1.call-done
  1041.0 9.3 all-gather.47.cloned.1.call-done
  1054.2 14.8 fusion.16
  1070.6 14.6 fusion.19
  1111.1 18.0 all-to-all-done
  1143.5 14.5 collective-permute-done.2
  1158.9 20.8 all-gather.49.cloned.1.call-done
  1179.6 12.2 fusion.81
  1191.9 12.1 fusion.193
  1204.1 20.6 reduce-scatter.35.cloned.1.call-done
  1255.8 14.9 fusion.12
  1272.2 14.8 fusion.15
  1312.0 19.1 all-to-all-done.1
  1346.1 14.5 collective-permute-done.3
  1361.5 20.7 all-gather.53.cloned.1.call-done
  1382.2 12.2 fusion.88
  1394.4 12.1 fusion.190
  1408.9 18.2 reduce-scatter.39.cloned.1.call-done
  1444.6 9.6 all-gather.55.cloned.1.call-done
  1458.8 15.2 fusion.8
  1475.5 14.5 fusion.11
  1517.2 13.0 fusion.199
  1581.2 13.2 fusion.232
  1594.4 13.2 fusion.230
  1607.6 30.4 %fusion.1 = bf16[1,4096,2048]{2,1,0:T(8,128)(2,1)} fusion(f32[4096,2048]{1,0:T(8,128)} %fusion.230, f32[4096,2048]{1,0:T(8,128)} %fusion.232, f32[]{:T(128)S(6)} %convert_element_type.649, f32[]{:T(128)S(6)} %convert_element_type.648, f32[]{:T(128)S(6)} %convert_element_type.647, bf16[3,1,256,4096]{3,2,1,0:T(8,128)(2,1)} %copy-done.12, s32[]{:T(128)S(6)} %min.35, ...), kind=kOutput, calls=%fused_computation.3 | convolution fusion | flops 4345298944 | bytes 87031824 | tf_op jit(solution)/shard_map/sqf,sqd->fd/dot_general | solution.py:228
  1640.9 13.5 fusion.357
  1654.4 13.3 fusion.355
  1667.7 30.1 %fusion = bf16[1,2048,4096]{2,1,0:T(8,128)(2,1)} fusion(f32[2048,4096]{1,0:T(8,128)} %fusion.355, f32[2048,4096]{1,0:T(8,128)} %fusion.357, f32[]{:T(128)S(6)} %convert_element_type.649, f32[]{:T(128)S(6)} %convert_element_type.648, f32[]{:T(128)S(6)} %convert_element_type.647, bf16[256,4096]{1,0:T(8,128)(2,1)} %fusion.88, ...), kind=kOutput, calls=%fused_computation.2 | convolution fusion | flops 4345298944 | bytes 87031824 | tf_op jit(solution)/shard_map/sqd,sqf->df/dot_general | solution.py:225
  1719.3 166.7 %reduce-scatter.53.cloned.1.call-done = bf16[1,4096,256]{2,1,0:T(8,128)(2,1)} async-done(((bf16[1,4096,2048]{2,1,0:T(8,128)(2,1)}), bf16[1,4096,256]{2,1,0:T(8,128)(2,1)}) %reduce-scatter.53.cloned.1.call-update) | async-done | bytes 2097168 | tf_op jit(solution)/shard_map/reduce_scatter | solution.py:326
  1889.9 165.0 %reduce-scatter.51.cloned.1.call-done = bf16[1,256,4096]{2,1,0:T(8,128)(2,1)} async-done(((bf16[1,2048,4096]{2,1,0:T(8,128)(2,1)}), bf16[1,256,4096]{2,1,0:T(8,128)(2,1)}) %reduce-scatter.51.cloned.1.call-update) | async-done | bytes 2097168 | tf_op jit(solution)/shard_map/reduce_scatter | solution.py:323
  2059.0 60.7 %reduce-scatter.47.cloned.1.call-done = f32[1,128,256]{2,1,0:T(8,128)} async-done(((f32[1,2048,256]{2,1,0:T(8,128)}), f32[1,128,256]{2,1,0:T(8,128)}) %reduce-scatter.47.cloned.1.call-update) | async-done | bytes 131088 | tf_op jit(solution)/shard_map/reduce_scatter | solution.py:331
  (583 shorter events, 412.7 us)
Async XLA Ops:
  7.2 46.6 %copy-start.98 = (s32[2,2]{1,0:T(2,128)S(1)}, s32[2,2]{1,0:T(2,128)}, u32[]{:S(2)}) copy-start(s32[2,2]{1,0:T(2,128)} %param.9) | copy-start | bytes 52
  7.2 43.8 %all-gather.27.cloned.1.call-start = ((), (), s32[]{:S(2)}) async-start(), calls=%async_computation.22 | async-start | bytes 1114112 | tf_op jit(solution)/shard_map/all_gather | solution.py:251
  7.9 65.4 %all-gather.29.cloned.1.call-start = ((), (), s32[]{:S(2)}) async-start(), calls=%async_computation.23 | async-start | bytes 1572864 | tf_op jit(solution)/shard_map/all_gather | solution.py:43
  43.3 552.8 %copy-start.10 = (bf16[1,1,128,2048]{3,2,1,0:T(8,128)(2,1)}, bf16[1,1,128,2048]{3,2,1,0:T(8,128)(2,1)S(1)}, u32[]{:S(2)}) copy-start(bf16[1,1,128,2048]{3,2,1,0:T(8,128)(2,1)S(1)} %get-tuple-element.65) | copy-start | bytes 1572868
  43.7 770.9 %copy-start.82 = (f32[1,1,2048]{2,1,0:T(1,128)}, f32[1,1,2048]{2,1,0:T(1,128)S(1)}, u32[]{:S(2)}) copy-start(f32[1,1,2048]{2,1,0:T(1,128)S(1)} %get-tuple-element.90) | copy-start | bytes 24580
  43.7 1500.3 %copy-start.68 = (f32[1,1,2048]{2,1,0:T(1,128)}, f32[1,1,2048]{2,1,0:T(1,128)S(1)}, u32[]{:S(2)}) copy-start(f32[1,1,2048]{2,1,0:T(1,128)S(1)} %get-tuple-element.89) | copy-start | bytes 24580
  44.9 77.2 %all-gather.31.cloned.1.call-start = ((), (), s32[]{:S(2)}) async-start(), calls=%async_computation.24 | async-start | bytes 4718592 | tf_op jit(solution)/shard_map/all_gather | solution.py:245
  45.7 115.9 %all-gather.59.cloned.1.call-start = ((), (), s32[]{:S(2)}) async-start(), calls=%async_computation.55 | async-start | bytes 1114112 | tf_op jit(solution)/shard_map/all_gather | solution.py:130
  53.1 156.6 %all-gather.33.cloned.1.call-start = ((), (), s32[]{:S(2)}) async-start(), calls=%async_computation.25 | async-start | bytes 4718592 | tf_op jit(solution)/shard_map/all_gather | solution.py:246
  53.7 179.1 %reduce-scatter.21.cloned.1.call-start = ((), (), s32[]{:S(2)}) async-start(), calls=%async_computation.26 | async-start | bytes 1572864 | tf_op jit(solution)/shard_map/reduce_scatter | solution.py:47
  125.9 44.2 %copy-start.47 = (bf16[256,1024]{1,0:T(8,128)(2,1)}, bf16[256,1024]{1,0:T(8,128)(2,1)S(1)}, u32[]{:S(2)}) copy-start(bf16[256,1024]{1,0:T(8,128)(2,1)S(1)} %fusion.260) | copy-start | bytes 1572868
  187.7 46.5 %copy-start.79 = (bf16[128,8,256]{2,0,1:T(8,128)(2,1)}, bf16[128,8,256]{2,0,1:T(8,128)(2,1)S(1)}, u32[]{:S(2)}) copy-start(bf16[128,8,256]{2,0,1:T(8,128)(2,1)S(1)} %fusion.245) | copy-start | bytes 1572868
  214.2 45.8 %all-gather.35.cloned.1.call-start = ((), (), s32[]{:S(2)}) async-start(), calls=%async_computation.27 | async-start | bytes 1572864 | tf_op jit(solution)/shard_map/all_gather | solution.py:43
  238.5 174.3 %all-gather.37.cloned.1.call-start = ((), (), s32[]{:S(2)}) async-start(), calls=%async_computation.28 | async-start | bytes 18874368 | tf_op jit(solution)/shard_map/all_gather | solution.py:247
  239.3 325.3 %all-gather.25.cloned.1.call-start = ((), (), s32[]{:S(2)}) async-start(), calls=%async_computation.21 | async-start | bytes 18874368 | tf_op jit(solution)/shard_map/all_gather | solution.py:248
  240.0 356.1 %reduce-scatter.23.cloned.1.call-start = ((), (), s32[]{:S(2)}) async-start(), calls=%async_computation.29 | async-start | bytes 1572864 | tf_op jit(solution)/shard_map/reduce_scatter | solution.py:47
  425.4 170.8 %copy-start.38 = (bf16[1,128,2048]{2,1,0:T(8,128)(2,1)S(1)}, bf16[1,128,2048]{2,1,0:T(8,128)(2,1)}, u32[]{:S(2)}) copy-start(bf16[1,128,2048]{2,1,0:T(8,128)(2,1)} %reduce-scatter.21.cloned.1.call-done) | copy-start | bytes 1572868
  425.4 186.6 %copy-start.19 = (bf16[1,2,128,2048]{3,2,1,0:T(8,128)(2,1)S(1)}, bf16[1,2,128,2048]{3,2,1,0:T(8,128)(2,1)}, u32[]{:S(2)}) copy-start(bf16[1,2,128,2048]{3,2,1,0:T(8,128)(2,1)} %param.8) | copy-start | bytes 3145732
  577.5 36.3 %copy-start.27 = (bf16[1,2048,256]{2,1,0:T(8,128)(2,1)S(1)}, bf16[1,2048,256]{2,1,0:T(8,128)(2,1)}, u32[]{:S(2)}) copy-start(bf16[1,2048,256]{2,1,0:T(8,128)(2,1)} %all-gather.27.cloned.1.call-done) | copy-start | bytes 3145732
  577.5 58.7 %all-gather.39.cloned.1.call-start = ((), (), s32[]{:S(2)}) async-start(), calls=%async_computation.30 | async-start | bytes 1572864 | tf_op jit(solution)/shard_map/all_gather | solution.py:43
  597.4 14.5 collective-permute-start
  612.2 186.0 %copy-start.3 = (bf16[1,128,2048]{2,1,0:T(8,128)(2,1)}, bf16[1,128,2048]{2,1,0:T(8,128)(2,1)S(1)}, u32[]{:S(2)}) copy-start(bf16[1,128,2048]{2,1,0:T(8,128)(2,1)S(1)} %get-tuple-element.61) | copy-start | bytes 1572868
  613.8 63.1 %all-gather.61.cloned.1.call-start = ((), (), s32[]{:S(2)}) async-start(), calls=%async_computation.56 | async-start | bytes 1114112 | tf_op jit(solution)/shard_map/all_gather | solution.py:130
  615.8 112.7 %reduce-scatter.25.cloned.1.call-start = ((), (), s32[]{:S(2)}) async-start(), calls=%async_computation.31 | async-start | bytes 1572864 | tf_op jit(solution)/shard_map/reduce_scatter | solution.py:47
  709.1 46.5 %all-gather.41.cloned.1.call-start = ((), (), s32[]{:S(2)}) async-start(), calls=%async_computation.32 | async-start | bytes 1572864 | tf_op jit(solution)/shard_map/all_gather | solution.py:43
  734.1 64.0 %reduce-scatter.27.cloned.1.call-start = ((), (), s32[]{:S(2)}) async-start(), calls=%async_computation.33 | async-start | bytes 1572864 | tf_op jit(solution)/shard_map/reduce_scatter | solution.py:47
  766.0 32.2 %copy-start.23 = (bf16[1,128,2048]{2,1,0:T(8,128)(2,1)S(1)}, bf16[1,128,2048]{2,1,0:T(8,128)(2,1)}, u32[]{:S(2)}) copy-start(bf16[1,128,2048]{2,1,0:T(8,128)(2,1)} %reduce-scatter.25.cloned.1.call-done) | copy-start | bytes 1572868
  777.7 60.6 %all-gather.43.cloned.1.call-start = ((), (), s32[]{:S(2)}) async-start(), calls=%async_computation.34 | async-start | bytes 1572864 | tf_op jit(solution)/shard_map/all_gather | solution.py:43
  799.5 14.5 collective-permute-start.1
  814.2 117.8 %copy-start.7 = (bf16[1,128,2048]{2,1,0:T(8,128)(2,1)}, bf16[1,128,2048]{2,1,0:T(8,128)(2,1)S(1)}, u32[]{:S(2)}) copy-start(bf16[1,128,2048]{2,1,0:T(8,128)(2,1)S(1)} %get-tuple-element.57) | copy-start | bytes 1572868
  815.8 63.1 %all-gather.63.cloned.1.call-start = ((), (), s32[]{:S(2)}) async-start(), calls=%async_computation.57 | async-start | bytes 1114112 | tf_op jit(solution)/shard_map/all_gather | solution.py:130
  817.9 110.6 %reduce-scatter.29.cloned.1.call-start = ((), (), s32[]{:S(2)}) async-start(), calls=%async_computation.35 | async-start | bytes 1572864 | tf_op jit(solution)/shard_map/reduce_scatter | solution.py:47
  909.1 46.6 %all-gather.45.cloned.1.call-start = ((), (), s32[]{:S(2)}) async-start(), calls=%async_computation.36 | async-start | bytes 1572864 | tf_op jit(solution)/shard_map/all_gather | solution.py:43
  934.2 44.3 %all-gather.57.cloned.1.call-start = ((), (), s32[]{:S(2)}) async-start(), calls=%async_computation.54 | async-start | bytes 1572864 | tf_op jit(solution)/shard_map/all_gather | solution.py:53
  935.1 87.8 %reduce-scatter.31.cloned.1.call-start = ((), (), s32[]{:S(2)}) async-start(), calls=%async_computation.37 | async-start | bytes 1572864 | tf_op jit(solution)/shard_map/reduce_scatter | solution.py:57
  1002.5 47.8 %all-gather.47.cloned.1.call-start = ((), (), s32[]{:S(2)}) async-start(), calls=%async_computation.38 | async-start | bytes 1572864 | tf_op jit(solution)/shard_map/all_gather | solution.py:53
  1100.5 28.6 %all-to-all-start = ((bf16[16,1,128,256]{2,3,1,0:T(8,128)(2,1)}), bf16[16,1,128,256]{2,3,1,0:T(8,128)(2,1)}, u32[]{:S(2)}, u32[]{:S(2)}) async-start(bf16[16,1,128,256]{2,3,1,0:T(8,128)(2,1)} %maximum_bitcast_fusion.1), calls=%async_computation.7 | async-start | bytes 2097152 | tf_op jit(solution)/shard_map/all_to_all | solution.py:22
  1105.3 32.5 %reduce-scatter.33.cloned.1.call-start = ((), (), s32[]{:S(2)}) async-start(), calls=%async_computation.39 | async-start | bytes 1572864 | tf_op jit(solution)/shard_map/reduce_scatter | solution.py:57
  1110.1 69.6 %all-gather.49.cloned.1.call-start = ((), (), s32[]{:S(2)}) async-start(), calls=%async_computation.40 | async-start | bytes 1572864 | tf_op jit(solution)/shard_map/all_gather | solution.py:53
  1110.3 31.9 %copy-start.13 = (bf16[3,1,128,2048]{3,2,1,0:T(8,128)(2,1)}, bf16[3,1,128,2048]{3,2,1,0:T(8,128)(2,1)S(1)}, u32[]{:S(2)}) copy-start(bf16[3,1,128,2048]{3,2,1,0:T(8,128)(2,1)S(1)} %pad_maximum_fusion.7) | copy-start | bytes 4718596
  1142.2 15.8 collective-permute-start.2
  1158.8 65.8 %reduce-scatter.35.cloned.1.call-start = ((), (), s32[]{:S(2)}) async-start(), calls=%async_computation.41 | async-start | bytes 1572864 | tf_op jit(solution)/shard_map/reduce_scatter | solution.py:57
  1191.9 32.8 %copy-start.1 = (f32[3,1,128,2048]{3,2,1,0:T(8,128)S(1)}, f32[3,1,128,2048]{3,2,1,0:T(8,128)}, u32[]{:S(2)}) copy-start(f32[3,1,128,2048]{3,2,1,0:T(8,128)} %copy-done) | copy-start | bytes 9437188
  1191.9 32.8 %copy-start.108 = (f32[128]{0:T(128)S(1)}, f32[128]{0:T(128)}, u32[]{:S(2)}) copy-start(f32[128]{0:T(128)} %copy-done.107) | copy-start | bytes 1540
  1204.0 48.0 %all-gather.51.cloned.1.call-start = ((), (), s32[]{:S(2)}) async-start(), calls=%async_computation.42 | async-start | bytes 1572864 | tf_op jit(solution)/shard_map/all_gather | solution.py:53
  1302.4 28.6 %all-to-all-start.1 = ((bf16[16,1,128,256]{2,3,1,0:T(8,128)(2,1)}), bf16[16,1,128,256]{2,3,1,0:T(8,128)(2,1)}, u32[]{:S(2)}, u32[]{:S(2)}) async-start(bf16[16,1,128,256]{2,3,1,0:T(8,128)(2,1)} %maximum_bitcast_fusion.2), calls=%async_computation.10 | async-start | bytes 2097152 | tf_op jit(solution)/shard_map/all_to_all | solution.py:22
  1307.2 32.5 %reduce-scatter.37.cloned.1.call-start = ((), (), s32[]{:S(2)}) async-start(), calls=%async_computation.43 | async-start | bytes 1572864 | tf_op jit(solution)/shard_map/reduce_scatter | solution.py:57
  1307.3 32.4 %copy-start.14 = (bf16[3,1,128,2048]{3,2,1,0:T(8,128)(2,1)S(1)}, bf16[3,1,128,2048]{3,2,1,0:T(8,128)(2,1)}, u32[]{:S(2)}) copy-start(bf16[3,1,128,2048]{3,2,1,0:T(8,128)(2,1)} %copy-done.13) | copy-start | bytes 4718596
  1311.9 70.3 %all-gather.53.cloned.1.call-start = ((), (), s32[]{:S(2)}) async-start(), calls=%async_computation.44 | async-start | bytes 1572864 | tf_op jit(solution)/shard_map/all_gather | solution.py:53
  1344.8 15.8 collective-permute-start.3
  1361.4 65.7 %reduce-scatter.39.cloned.1.call-start = ((), (), s32[]{:S(2)}) async-start(), calls=%async_computation.45 | async-start | bytes 1572864 | tf_op jit(solution)/shard_map/reduce_scatter | solution.py:57
  1394.4 32.7 %copy-start.2 = (f32[3,1,128,2048]{3,2,1,0:T(8,128)S(1)}, f32[3,1,128,2048]{3,2,1,0:T(8,128)}, u32[]{:S(2)}) copy-start(f32[3,1,128,2048]{3,2,1,0:T(8,128)} %copy-done) | copy-start | bytes 9437188
  1394.4 32.7 %copy-start.106 = (f32[128]{0:T(128)S(1)}, f32[128]{0:T(128)}, u32[]{:S(2)}) copy-start(f32[128]{0:T(128)} %copy-done.105) | copy-start | bytes 1540
  1406.5 47.7 %all-gather.55.cloned.1.call-start = ((), (), s32[]{:S(2)}) async-start(), calls=%async_computation.46 | async-start | bytes 1572864 | tf_op jit(solution)/shard_map/all_gather | solution.py:53
  1432.7 109.5 %reduce-scatter.41.cloned.1.call-start = ((), (), s32[]{:S(2)}) async-start(), calls=%async_computation.47 | async-start | bytes 1572864 | tf_op jit(solution)/shard_map/reduce_scatter | solution.py:57
  1436.3 94.0 %copy-start.41 = (bf16[3,1,256,1024]{2,3,1,0:T(8,128)(2,1)}, bf16[3,1,256,1024]{2,3,1,0:T(8,128)(2,1)S(1)}, u32[]{:S(2)}) copy-start(bf16[3,1,256,1024]{2,3,1,0:T(8,128)(2,1)S(1)} %pad_maximum_fusion.9) | copy-start | bytes 4718596
  1511.7 29.1 %all-to-all-start.2 = ((bf16[16,1,128,256]{2,3,1,0:T(8,128)(2,1)}), bf16[16,1,128,256]{2,3,1,0:T(8,128)(2,1)}, u32[]{:S(2)}, u32[]{:S(2)}) async-start(bf16[16,1,128,256]{2,3,1,0:T(8,128)(2,1)} %maximum_bitcast_fusion.3), calls=%async_computation.13 | async-start | bytes 2097152 | tf_op jit(solution)/shard_map/all_to_all | solution.py:22
  1516.8 186.1 %reduce-scatter.43.cloned.1.call-start = ((), (), s32[]{:S(2)}) async-start(), calls=%async_computation.48 | async-start | bytes 1572864 | tf_op jit(solution)/shard_map/reduce_scatter | solution.py:47
  1530.2 176.6 %reduce-scatter.55.cloned.1.call-start = ((), (), s32[]{:S(2)}) async-start(), calls=%async_computation.58 | async-start | bytes 1114112
  1554.5 154.7 %reduce-scatter.49.cloned.1.call-start = ((), (), s32[]{:S(2)}) async-start(), calls=%async_computation.51 | async-start | bytes 4718592 | tf_op jit(solution)/shard_map/reduce_scatter | solution.py:320
  1563.6 153.6 %reduce-scatter.45.cloned.1.call-start = ((), (), s32[]{:S(2)}) async-start(), calls=%async_computation.49 | async-start | bytes 4718592 | tf_op jit(solution)/shard_map/reduce_scatter | solution.py:317
  1574.9 311.0 %reduce-scatter.53.cloned.1.call-start = ((), (), s32[]{:S(2)}) async-start(), calls=%async_computation.53 | async-start | bytes 18874368 | tf_op jit(solution)/shard_map/reduce_scatter | solution.py:326
  1638.1 416.9 %reduce-scatter.51.cloned.1.call-start = ((), (), s32[]{:S(2)}) async-start(), calls=%async_computation.52 | async-start | bytes 18874368 | tf_op jit(solution)/shard_map/reduce_scatter | solution.py:323
  1698.0 421.7 %reduce-scatter.47.cloned.1.call-start = ((), (), s32[]{:S(2)}) async-start(), calls=%async_computation.50 | async-start | bytes 2228224 | tf_op jit(solution)/shard_map/reduce_scatter | solution.py:331
  (131 other events, 1227.3 us)
Sparse Core Ops, SparseCore 0:
  10.2 40.6 all-gather.26
  53.1 20.2 all-gather.28
  75.0 47.1 all-gather.30
  124.8 36.6 all-gather.58
  163.0 46.7 all-gather.32
  214.3 18.5 reduce-scatter.20
  238.6 21.2 all-gather.34
  261.7 151.0 all-gather.36
  414.5 150.0 all-gather.24
  577.6 18.4 reduce-scatter.22
  613.9 22.3 all-gather.38
  638.9 37.9 all-gather.60
  709.2 19.2 reduce-scatter.24
  734.3 21.2 all-gather.40
  777.8 20.3 reduce-scatter.26
  815.9 22.3 all-gather.42
  840.9 37.9 all-gather.62
  909.2 19.2 reduce-scatter.28
  934.3 21.2 all-gather.44
  957.1 21.2 all-gather.56
  1002.6 20.3 reduce-scatter.30
  1029.0 21.2 all-gather.46
  1110.2 27.5 reduce-scatter.32
  1159.0 20.6 all-gather.48
  1204.1 20.5 reduce-scatter.34
  1230.6 21.2 all-gather.50
  1312.0 27.5 reduce-scatter.36
  1361.5 20.6 all-gather.52
  1406.6 20.4 reduce-scatter.38
  1432.8 21.2 all-gather.54
  1498.1 20.3 reduce-scatter.40
  1530.3 23.3 reduce-scatter.42
  1557.2 57.3 reduce-scatter.54
  1617.0 49.0 reduce-scatter.48
  1669.0 48.1 reduce-scatter.44
  1719.5 166.4 reduce-scatter.52
  1888.3 166.5 reduce-scatter.50
  2059.7 59.9 reduce-scatter.46
where the time goes:
time: 2130 us
  waiting for transfers between devices  1310 us (62%)
  matrix products  515 us (24%)
  other arithmetic  181 us (8%)
  local copies, waits for them, and re-layouts  46.3 us (2%)
  blocking collectives  34.1 us (2%)
  starting transfers between devices  27.7 us (1%)
    reduce_scatter x1, waiting for transfers between devices, local(): lax.psum_scatter(totals[3].astype(jnp.bfloat16), 'dp', scatter_dimension=...  167 us
    reduce_scatter x1, waiting for transfers between devices, local(): lax.psum_scatter(totals[2].astype(jnp.bfloat16), 'dp', scatter_dimension=...  165 us
    all_gather x1, waiting for transfers between devices, local(): lax.all_gather(w_hidden, 'dp', axis=1, tiled=True)  153 us
    all_gather x1, waiting for transfers between devices, local(): lax.all_gather(w_project, 'dp', axis=2, tiled=True)  139 us
    all_gather x6, waiting for transfers between devices, spread_rows(): return lax.all_gather(values, 'tensor', axis=1, tiled=True)  110 us
    all_gather x3, waiting for transfers between devices, layer_forward(): lax.all_gather(keyval_local, ('dp', 'tensor'), axis=1, tiled=True)  109 us
    reduce_scatter x6, waiting for transfers between devices, collect_rows(): lax.psum_scatter(terms.astype(jnp.bfloat16), 'tensor', scatter_dimension=...  96 us
    all_gather x6, waiting for transfers between devices, spread_grads(): return lax.all_gather(values, 'tensor', axis=1, tiled=True)  69.9 us
  transfers between devices with their start and end apart: 45, of which 40 were waited for; matrix products, arithmetic and copies ran while one was open for 17% of the time, Pallas kernels for 0%

commit v1 on v0

v1 whole, which is shorter than its diff:
```python
import jax
import jax.numpy as jnp
from jax import lax
from jax.sharding import PartitionSpec as P

SPAN = 256
EPSILON = 1e-05
NEGATIVE = -1000000000.0
BF16 = jnp.bfloat16
F32 = jnp.float32


def dot(left, right, dims):
    return lax.dot_general(left, right, ((dims[0], dims[1]), ((), ())), preferred_element_type=F32)


def swap_quad(block, offset):
    size = lax.axis_size("section") * lax.axis_size("tensor")
    return lax.ppermute(block, ("section", "tensor"), [(i, i ^ offset) for i in range(size)])


def swap_dp(block, offset):
    return lax.ppermute(block, "dp", [(i, i ^ offset) for i in range(lax.axis_size("dp"))])


def quad_size():
    return lax.axis_size("section") * lax.axis_size("tensor")


def spread(block):
    return jnp.concatenate([block] + [swap_quad(block, k) for k in range(1, quad_size())], 0)


def collect(partial):
    rows = partial.shape[0] // quad_size()
    total = partial[:rows].astype(F32)
    for k in range(1, quad_size()):
        total = total + swap_quad(partial[k * rows : (k + 1) * rows], k).astype(F32)
    return total


def gather_dp(block):
    count = lax.axis_size("dp")
    far = [block] + [swap_dp(block, 2 * j) for j in range(1, count // 2)]
    near = swap_dp(jnp.stack(far), 1)
    return jnp.stack(far), near


def scatter_dp(near_even, near_odd):
    halves = near_even + swap_dp(near_odd.astype(BF16), 1).astype(F32)
    total = halves[0]
    for j in range(1, halves.shape[0]):
        total = total + swap_dp(halves[j].astype(BF16), 2 * j).astype(F32)
    return total


def scatter_all(blocks, wire):
    sections, count, tensors = blocks.shape[:3]
    me_s, me_d, me_t = lax.axis_index("section"), lax.axis_index("dp"), lax.axis_index("tensor")

    def pick(s, t):
        one = lax.dynamic_index_in_dim(blocks, me_s ^ s, 0, keepdims=False)
        return lax.dynamic_index_in_dim(one, me_t ^ t, 1, keepdims=False)

    total = pick(0, 0)
    for k in range(1, sections * tensors):
        total = total + swap_quad(pick(k // tensors, k % tensors).astype(wire), k).astype(F32)
    pairs = total.reshape((count // 2, 2) + total.shape[1:])
    core = me_d % 2
    kept = lax.dynamic_index_in_dim(pairs, core, 1, keepdims=False)
    given = lax.dynamic_index_in_dim(pairs, 1 - core, 1, keepdims=False)
    kept = kept + swap_dp(given.astype(wire), 1).astype(F32)
    place = me_d // 2
    result = lax.dynamic_index_in_dim(kept, place, 0, keepdims=False)
    for j in range(1, count // 2):
        piece = lax.dynamic_index_in_dim(kept, place ^ j, 0, keepdims=False)
        result = result + swap_dp(piece.astype(wire), 2 * j).astype(F32)
    return result


def gather_all(block):
    sections, count, tensors = (lax.axis_size(a) for a in ("section", "dp", "tensor"))
    me_s, me_d, me_t = lax.axis_index("section"), lax.axis_index("dp"), lax.axis_index("tensor")
    even, odd = gather_dp(block)
    mine = jnp.stack([even, odd], 1).reshape((count,) + block.shape)
    parts = [mine] + [swap_quad(mine, k) for k in range(1, sections * tensors)]
    whole = jnp.zeros((sections, count, tensors) + block.shape, block.dtype)
    for k, part in enumerate(parts):
        for j in range(count):
            index = (me_s ^ (k // tensors), me_d ^ j, me_t ^ (k % tensors)) + (0,) * block.ndim
            whole = lax.dynamic_update_slice(whole, part[j][None, None, None], index)
    return whole


def layer_norm(values, scale_row, shift_row):
    centered = values - jnp.mean(values, -1, keepdims=True)
    spread_of = jnp.mean(centered * centered, -1, keepdims=True)
    return centered * lax.rsqrt(spread_of + EPSILON) * scale_row + shift_row


def gelu_tanh(values):
    return jax.nn.gelu(values, approximate=True)


def allowed_keys(starts, query_pos, key_pos):
    causal = key_pos[None, :] <= query_pos[:, None]
    query_in = (query_pos[None, :] >= starts[:, None]) & (query_pos[None, :] < starts[:, None] + SPAN)
    key_in = (key_pos[None, :] >= starts[:, None]) & (key_pos[None, :] < starts[:, None] + SPAN)
    return causal | jnp.any(query_in[:, :, None] & key_in[:, None, :], axis=0)


def scores_of(queries, keys, allowed):
    head = keys.shape[-1]
    scores = jnp.einsum("sqhd,skd->shqk", queries, keys, preferred_element_type=F32) * head**-0.5
    return jnp.where(allowed[:, None], scores, NEGATIVE)


def attend_forward(queries, keyval, allowed):
    head = keyval.shape[-1] // 2
    four = queries.reshape(allowed.shape[0], allowed.shape[1], -1, head)
    scores = scores_of(four, keyval[..., :head], allowed)
    peak = jnp.max(scores, -1, keepdims=True)
    log_total = peak + jnp.log(jnp.sum(jnp.exp(scores - peak), -1, keepdims=True))
    probs = jnp.exp(scores - log_total).astype(BF16)
    out = jnp.einsum("shqk,skd->sqhd", probs, keyval[..., head:], preferred_element_type=F32)
    return log_total, out.astype(BF16).reshape(queries.shape)


def attend_backward(queries, keyval, log_total, grad_out, allowed):
    head = keyval.shape[-1] // 2
    shape = (allowed.shape[0], allowed.shape[1], -1, head)
    four, grad_four = queries.reshape(shape), grad_out.reshape(shape)
    keys, values = keyval[..., :head], keyval[..., head:]
    probs = jnp.exp(scores_of(four, keys, allowed) - log_total)
    grad_probs = jnp.einsum("sqhd,skd->shqk", grad_four, values, preferred_element_type=F32)
    grad_values = jnp.einsum(
        "shqk,sqhd->skd", probs.astype(BF16), grad_four, preferred_element_type=F32
    )
    weighted = jnp.sum(probs * grad_probs, -1, keepdims=True)
    grad_scores = (probs * (grad_probs - weighted) * head**-0.5).astype(BF16)
    grad_queries = jnp.einsum("shqk,skd->sqhd", grad_scores, keys, preferred_element_type=F32)
    grad_keys = jnp.einsum("shqk,sqhd->skd", grad_scores, four, preferred_element_type=F32)
    return grad_queries.astype(BF16).reshape(queries.shape), jnp.concatenate(
        [grad_keys, grad_values], -1
    )


def gather_keyval(block):
    even, odd = gather_dp(block)
    mine = jnp.concatenate([even, odd], 0)
    parts = [mine] + [swap_quad(mine, k) for k in range(1, quad_size())]
    return jnp.stack(parts).reshape(lax.axis_size("section"), -1, block.shape[-1])


def scatter_keyval(partial, rows):
    count = lax.axis_size("dp")
    blocks = partial.reshape(quad_size(), count * rows, partial.shape[-1])
    total = blocks[0]
    for k in range(1, quad_size()):
        total = total + swap_quad(blocks[k].astype(BF16), k).astype(F32)
    halves = total.reshape(2, count // 2, rows, partial.shape[-1])
    return scatter_dp(halves[0], halves[1])


def layer_forward(inputs, weights, allowed):
    query_mat, keyval_mat, output_mat, hidden_mat, project_mat, norms = weights
    normed = layer_norm(inputs, norms[0], norms[1]).astype(BF16)
    keyval = gather_keyval(dot(normed, keyval_mat, ((1,), (0,))).astype(BF16))
    normed_all = spread(normed)
    queries = dot(normed_all, query_mat, ((1,), (0,))).astype(BF16)
    log_total, attended = attend_forward(queries, keyval, allowed)
    middle = inputs + collect(dot(attended, output_mat, ((1,), (0,))).astype(BF16))
    mixed_all = spread(layer_norm(middle, norms[2], norms[3]).astype(BF16))
    hidden_pre = dot(mixed_all, hidden_mat, ((1,), (0,)))
    hidden_act = gelu_tanh(hidden_pre).astype(BF16)
    outputs = middle + collect(dot(hidden_act, project_mat, ((1,), (0,))).astype(BF16))
    saved = (normed, normed_all, keyval, queries, log_total, attended)
    return outputs, saved + (middle, mixed_all, hidden_pre, hidden_act)


def layer_backward(inputs, grad_out, weights, allowed, saved):
    query_mat, keyval_mat, output_mat, hidden_mat, project_mat, norms = weights
    normed, normed_all, keyval, queries, log_total, attended = saved[:6]
    middle, mixed_all, hidden_pre, hidden_act = saved[6:]
    rows = inputs.shape[0]
    grad_branch = spread(grad_out.astype(BF16))
    grad_project = dot(hidden_act, grad_branch, ((0,), (0,))).astype(BF16)
    grad_act = dot(grad_branch, project_mat, ((1,), (1,)))
    grad_pre = jax.vjp(gelu_tanh, hidden_pre)[1](grad_act)[0].astype(BF16)
    grad_hidden = dot(mixed_all, grad_pre, ((0,), (0,))).astype(BF16)
    grad_mixed = collect(dot(grad_pre, hidden_mat, ((1,), (1,))).astype(BF16))
    pull = jax.vjp(layer_norm, middle, norms[2], norms[3])[1]
    grad_mid, grad_gain_two, grad_bias_two = pull(grad_mixed)
    grad_middle = grad_out + grad_mid
    grad_rows = spread(grad_middle.astype(BF16))
    grad_output = dot(attended, grad_rows, ((0,), (0,))).astype(BF16)
    grad_attended = dot(grad_rows, output_mat, ((1,), (1,))).astype(BF16)
    grad_queries, grad_kv = attend_backward(queries, keyval, log_total, grad_attended, allowed)
    grad_query = dot(normed_all, grad_queries, ((0,), (0,))).astype(BF16)
    grad_keyval = scatter_keyval(grad_kv, rows).astype(BF16)
    grad_keyval_mat = dot(normed, grad_keyval, ((0,), (0,)))
    grad_normed = collect(dot(grad_queries, query_mat, ((1,), (1,))).astype(BF16))
    grad_normed = grad_normed + dot(grad_keyval, keyval_mat, ((1,), (1,)))
    pull = jax.vjp(layer_norm, inputs, norms[0], norms[1])[1]
    grad_in, grad_gain_one, grad_bias_one = pull(grad_normed)
    table = jnp.stack([grad_gain_one, grad_bias_one, grad_gain_two, grad_bias_two])
    grads = (grad_query, grad_output, grad_hidden, grad_project)
    return grad_middle + grad_in, grads, grad_keyval_mat, table


CUT = (1, 0, 1, 0)


def local(ends_in, pieces, w_query, w_keyval, w_output, w_hidden, w_project, norm_params):
    section = lax.axis_index("section")
    tensor = lax.axis_index("tensor")
    place = lax.axis_index("dp")
    first = section == 0
    count, tensors = lax.axis_size("dp"), lax.axis_size("tensor")
    rows, width = ends_in.shape[2:]

    given = lax.dynamic_index_in_dim(ends_in[0], 1 - section, 0, keepdims=False)
    kept = lax.dynamic_index_in_dim(ends_in[0], section, 0, keepdims=False)
    taken = lax.ppermute(given, "section", [(0, 1), (1, 0)])
    inputs = jnp.where(first, kept, taken).astype(F32)
    cotangent = jnp.where(first, taken, kept).astype(F32)

    depth = w_keyval.shape[1]
    columns = w_keyval.shape[2]
    table = jnp.pad(norm_params[0].reshape(-1), (0, 16 * columns - 4 * depth))
    small = gather_all(jnp.concatenate([w_keyval[0], table.reshape(16, columns)], 0))
    keyval_mats = small[..., :depth, :].reshape(2, width, columns)
    norms = small[..., depth:, :].reshape(2, count * tensors, 16 * columns)
    norms = norms[..., : 4 * depth].reshape(2, count * tensors, 4, depth)
    norms = jnp.swapaxes(norms, 1, 2).reshape(2, 4, width).astype(F32)

    large = (w_query[0], w_output[0], w_hidden[0], w_project[0])

    def quarter(array, cut, index):
        size = array.shape[cut] // 2
        return lax.dynamic_slice_in_dim(array, index * size, size, cut)

    mats = []
    for layer in range(2):
        mine = []
        for array, cut in zip(large, CUT):
            moved = lax.ppermute(
                quarter(array, cut, 1 - section), "section", [(layer, 1 - layer)]
            )
            shard = jnp.where(section == layer, quarter(array, cut, section), moved)
            mine.append(lax.all_gather(shard, "dp", axis=1 - cut, tiled=True))
        mats.append((mine[0], keyval_mats[layer], mine[1], mine[2], mine[3], norms[layer]))

    row = jnp.arange(rows, dtype=jnp.int32)
    turn = tensor ^ jnp.arange(tensors, dtype=jnp.int32)
    query_pos = ((place * tensors + turn)[:, None] * rows + row).reshape(-1)
    order = jnp.concatenate([jnp.arange(0, count, 2), jnp.arange(1, count, 2)]).astype(jnp.int32)
    where = (place ^ order)[None, :] * tensors + turn[:, None]
    key_pos = (where[:, :, None] * rows + row).reshape(-1)
    allowed = jnp.stack(
        [
            allowed_keys(
                lax.dynamic_index_in_dim(pieces, section ^ k, 0, keepdims=False),
                query_pos,
                key_pos,
            )
            for k in range(2)
        ]
    )

    between, saved_one = layer_forward(inputs, mats[0], allowed)
    between = between.astype(BF16).astype(F32)
    outputs, saved_two = layer_forward(between, mats[1], allowed)
    grad_between, grads_two, kv_two, table_two = layer_backward(
        between, cotangent, mats[1], allowed, saved_two
    )
    grad_between = grad_between.astype(BF16).astype(F32)
    grad_inputs, grads_one, kv_one, table_one = layer_backward(
        inputs, grad_between, mats[0], allowed, saved_one
    )

    results = []
    for index, cut in enumerate(CUT):
        halves = []
        for layer, grads in ((1, grads_two), (0, grads_one)):
            own = lax.psum_scatter(grads[index], "dp", scatter_dimension=1 - cut, tiled=True)
            moved = lax.ppermute(own, "section", [(1 - layer, layer)])
            pair = (own, moved) if layer == 0 else (moved, own)
            halves.append(jnp.concatenate(pair, cut).astype(F32))
        results.append(jnp.where(first, halves[1], halves[0])[None])

    kv_blocks = jnp.stack([kv_one, kv_two]).reshape(2, count, tensors, depth, -1)
    kv_result = scatter_all(kv_blocks, BF16)
    tables = jnp.stack([table_one, table_two]).reshape(2, 4, count, tensors, depth)
    table_result = scatter_all(jnp.moveaxis(tables, 1, 3), F32)

    given = jnp.where(first, outputs, grad_inputs).astype(BF16)
    kept = jnp.where(first, grad_inputs, outputs)
    taken = lax.ppermute(given, "section", [(0, 1), (1, 0)]).astype(F32)
    ends_out = jnp.where(first, jnp.stack([kept, taken]), jnp.stack([taken, kept]))
    return (
        ends_out[None],
        results[0],
        kv_result[None],
        results[1],
        results[2],
        results[3],
        table_result[None, :3],
        table_result[None, 3],
    )


def solution(mesh):
    placed = (
        P("section", None, ("dp", "tensor"), None),
        P(),
        P("section", "dp", "tensor"),
        P("section", ("dp", "tensor"), None),
        P("section", "tensor", "dp"),
        P("section", "dp", "tensor"),
        P("section", "tensor", "dp"),
        P("section", None, ("dp", "tensor")),
    )
    return jax.shard_map(
        local,
        mesh=mesh,
        in_specs=placed,
        out_specs=(
            P("section", None, ("dp", "tensor"), None),
            P("section", "dp", "tensor"),
            P("section", ("dp", "tensor"), None),
            P("section", "tensor", "dp"),
            P("section", "dp", "tensor"),
            P("section", "tensor", "dp"),
            P("section", None, ("dp", "tensor")),
            P("section", ("dp", "tensor")),
        ),
        check_vma=False,
    )
```

time: 2130 us -> 1220 us (0.57)
  waiting for transfers between devices: 1310 us -> 574 us
  matrix products: 515 us -> 316 us
  starting transfers between devices: 27.7 us -> 166 us
  other arithmetic: 181 us -> 73.1 us
  blocking collectives: 34.1 us -> 0 us
    all_gather x20 -> x8, waiting for transfers between devices: 656 us -> 0.11 us  [local(): mine.append(lax.all_gather(shard, 'dp', axis=1 - cut, tiled=True))]
    reduce_scatter x17 -> x8, waiting for transfers between devices: 557 us -> 58.2 us  [local(): lax.psum_scatter(grads[index], 'dp', scatter_dimension=1 - cut, tiled=True)]
    ppermute x4 -> x115, waiting for transfers between devices: 51.2 us -> 515 us  [the longest x69 385 us: swap_quad(): lax.ppermute(block, ('section', 'tensor'), [(i, i ^ offset) for i in rang...]
    dot_general x66 -> x42, matrix products: 515 us -> 316 us  [the longest x30 156 us: dot(): lax.dot_general(left, right, ((dims[0], dims[1]), ((), ())), preferred_el...]
    ppermute x4 -> x115, starting transfers between devices: 9.37 us -> 164 us  [the longest x69 82.7 us: swap_quad(): lax.ppermute(block, ('section', 'tensor'), [(i, i ^ offset) for i in rang...]
    convert_element_type x20 -> x12, other arithmetic: 72.6 us -> 4.08 us  [the longest x2 1.3 us: layer_forward(): mixed_all = spread(layer_norm(middle, norms[2], norms[3]).astype(BF16))]
    all_to_all x3 -> x0, waiting for transfers between devices: 37.1 us -> none  [sum_at_owner(): lax.all_to_all(in_blocks(array, dim, devices), axis, 0, 0, tiled=True)]
    all_gather x1 -> x0, blocking collectives: 34.1 us -> none  [local(): lax.all_gather(norm_params, ('dp', 'tensor'), axis=2, tiled=True)]
  transfers between devices with their start and end apart: 45 -> 131, of which waited for: 40 -> 72; matrix products, arithmetic and copies ran while one was open for 17% -> 36% of each run, Pallas kernels for 0% -> 0%
where the time goes in v1:
time: 1220 us; the launch traced here: 1210 us
  waiting for transfers between devices  574 us (47%)
  matrix products  316 us (26%)
  starting transfers between devices  166 us (14%)
  other arithmetic  73.1 us (6%)
  local copies, waits for them, and re-layouts  62.8 us (5%)
  between operations  16.4 us (1%)
    ppermute x69, waiting for transfers between devices, swap_quad(): lax.ppermute(block, ('section', 'tensor'), [(i, i ^ offset) for i in rang...  385 us
    dot_general x30, matrix products, dot(): lax.dot_general(left, right, ((dims[0], dims[1]), ((), ())), preferred_el...  156 us
    ppermute x69, starting transfers between devices, swap_quad(): lax.ppermute(block, ('section', 'tensor'), [(i, i ^ offset) for i in rang...  82.7 us
    reduce_scatter x8, waiting for transfers between devices, local(): lax.psum_scatter(grads[index], 'dp', scatter_dimension=1 - cut, tiled=True)  58.2 us
    ppermute x8, waiting for transfers between devices, local(): lax.ppermute(quarter(array, cut, 1 - section), 'section', [(layer, 1 - la...  51.7 us
    dot_general x2, matrix products, attend_backward(): jnp.einsum('shqk,sqhd->skd', grad_scores, four, preferred_element_type=F32)  51 us
    dot_general x2, matrix products, attend_backward(): jnp.einsum('shqk,skd->sqhd', grad_scores, keys, preferred_element_type=F32)  50.5 us
    ppermute x28, waiting for transfers between devices, swap_dp(): lax.ppermute(block, 'dp', [(i, i ^ offset) for i in range(lax.axis_size('...  43.5 us
  transfers between devices with their start and end apart: 131, of which 72 were waited for; matrix products, arithmetic and copies ran while one was open for 36% of the time, Pallas kernels for 0%

profile of v1, /device:TPU:0, one launch (start us, length us, event | category | flops | bytes accessed | tf_op | source)
XLA Modules:
  0.0 1207.9 jit_solution(1163771699254967210)
XLA Ops:
  9.6 4.9 collective-permute-start.22
  36.8 6.5 collective-permute-start.30
  43.3 17.3 %collective-permute-done.53 = bf16[256,2048]{1,0:T(8,128)(2,1)} collective-permute-done((bf16[256,2048]{1,0:T(8,128)(2,1)S(1)}, bf16[256,2048]{1,0:T(8,128)(2,1)}, u32[]{:S(2)}, u32[]{:S(2)}) %collective-permute-start.53) | collective-permute-done | bytes 1048608 | tf_op jit(solution)/shard_map/ppermute | solution.py:247
  73.3 18.1 %collective-permute-done.31 = bf16[2048,256]{1,0:T(8,128)(2,1)S(1)} collective-permute-done((bf16[2048,256]{1,0:T(8,128)(2,1)S(1)}, bf16[2048,256]{1,0:T(8,128)(2,1)S(1)}, u32[]{:S(2)}, u32[]{:S(2)}) %collective-permute-start.31) | collective-permute-done | bytes 1048608 | tf_op jit(solution)/shard_map/ppermute | solution.py:247
  119.2 23.4 %collective-permute-done.9 = bf16[8,144,256]{2,1,0:T(8,128)(2,1)S(1)} collective-permute-done((bf16[8,144,256]{2,1,0:T(8,128)(2,1)S(1)}, bf16[8,144,256]{2,1,0:T(8,128)(2,1)S(1)}, u32[]{:S(2)}, u32[]{:S(2)}) %collective-permute-start.9) | collective-permute-done | bytes 589856 | tf_op jit(solution)/shard_map/ppermute | solution.py:19
  166.6 10.4 collective-permute-done.13
  186.2 8.2 collective-permute-done.18
  201.1 26.4 %collective-permute-done.17 = bf16[8,128,256]{2,1,0:T(8,128)(2,1)} collective-permute-done((bf16[8,128,256]{2,1,0:T(8,128)(2,1)S(1)}, bf16[8,128,256]{2,1,0:T(8,128)(2,1)}, u32[]{:S(2)}, u32[]{:S(2)}) %collective-permute-start.17) | collective-permute-done | bytes 524320 | tf_op jit(solution)/shard_map/ppermute | solution.py:19
  244.2 5.5 fusion.46
  256.7 21.5 %collective-permute-done.24 = bf16[128,2048]{1,0:T(8,128)(2,1)S(1)} collective-permute-done((bf16[128,2048]{1,0:T(8,128)(2,1)S(1)}, bf16[128,2048]{1,0:T(8,128)(2,1)S(1)}, u32[]{:S(2)}, u32[]{:S(2)}) %collective-permute-start.24) | collective-permute-done | bytes 524320 | tf_op jit(solution)/shard_map/ppermute | solution.py:19
  284.4 12.0 collective-permute-done.29
  296.4 9.3 collective-permute-done.28
  305.8 10.3 fusion.109
  316.1 9.5 convolution_convert_fusion.14
  329.3 21.6 %collective-permute-done.32 = bf16[128,2048]{1,0:T(8,128)(2,1)S(1)} collective-permute-done((bf16[128,2048]{1,0:T(8,128)(2,1)S(1)}, bf16[128,2048]{1,0:T(8,128)(2,1)S(1)}, u32[]{:S(2)}, u32[]{:S(2)}) %collective-permute-start.32) | collective-permute-done | bytes 524320 | tf_op jit(solution)/shard_map/ppermute | solution.py:19
  363.4 4.8 collective-permute-done.36
  376.3 9.1 collective-permute-done.43
  391.1 5.5 collective-permute-done.41
  396.6 8.4 collective-permute-done.40
  415.8 5.5 fusion.47
  428.5 21.5 %collective-permute-done.47 = bf16[128,2048]{1,0:T(8,128)(2,1)S(1)} collective-permute-done((bf16[128,2048]{1,0:T(8,128)(2,1)S(1)}, bf16[128,2048]{1,0:T(8,128)(2,1)S(1)}, u32[]{:S(2)}, u32[]{:S(2)}) %collective-permute-start.47) | collective-permute-done | bytes 524320 | tf_op jit(solution)/shard_map/ppermute | solution.py:19
  460.8 8.4 collective-permute-done.52
  470.8 9.8 collective-permute-done.51
  480.6 7.5 fusion.108
  491.7 9.5 collective-permute-done.2
  501.2 8.7 convolution_convert_fusion
  510.0 11.8 fusion.25
  521.8 9.2 convolution_convert_fusion.12
  534.8 21.2 %collective-permute-done.54 = bf16[128,2048]{1,0:T(8,128)(2,1)S(1)} collective-permute-done((bf16[128,2048]{1,0:T(8,128)(2,1)S(1)}, bf16[128,2048]{1,0:T(8,128)(2,1)S(1)}, u32[]{:S(2)}, u32[]{:S(2)}) %collective-permute-start.54) | collective-permute-done | bytes 524320 | tf_op jit(solution)/shard_map/ppermute | solution.py:19
  563.6 12.3 %collective-permute-done.59 = bf16[128,2048]{1,0:T(8,128)(2,1)S(1)} collective-permute-done((bf16[128,2048]{1,0:T(8,128)(2,1)S(1)}, bf16[128,2048]{1,0:T(8,128)(2,1)S(1)}, u32[]{:S(2)}, u32[]{:S(2)}) %collective-permute-start.59) | collective-permute-done | bytes 524320 | tf_op jit(solution)/shard_map/ppermute | solution.py:19
  576.0 9.4 collective-permute-done.58
  590.5 9.5 fusion.84
  600.0 25.2 %fusion.33 = f32[2,2048,128]{1,2,0:T(8,128)} fusion(bf16[2,256,4,128]{1,3,2,0:T(8,128)(2,1)S(1)} %copy-done.42, f32[2,2048,256,4]{2,1,3,0:T(8,128)} %fusion.84, f32[2,2048,256,4]{2,1,3,0:T(8,128)} %copy-done.7, f32[2,4,256]{2,1,0:T(4,128)S(1)} %bitcast.784, pred[2,256,2048]{1,2,0:T(8,128)(4,1)S(1)} %copy.103), kind=kOutput, calls=%fused_computation.80 | convolution fusion | flops 1119883264 | bytes 37232640 | tf_op jit(solution)/shard_map/shqk,sqhd->skd/dot_general | solution.py:142
  625.2 9.4 convolution_bitcast_fusion.1
  639.3 5.4 copy.120
  651.8 25.1 %fusion.44 = bf16[2,256,4,128]{1,3,2,0:T(8,128)(2,1)} fusion(f32[2,2048,256,4]{2,1,3,0:T(8,128)} %fusion.84, f32[2,2048,256,4]{2,1,3,0:T(8,128)} %copy-done.7, f32[2,4,256]{2,1,0:T(4,128)S(1)} %bitcast.786, pred[2,256,2048]{1,2,0:T(8,128)(4,1)S(1)} %copy.103, bf16[2,2048,256]{2,1,0:T(8,128)(2,1)} %bitcast.691), kind=kOutput, calls=%fused_computation.122 | convolution fusion | flops 1120145408 | bytes 70795264 | tf_op jit(solution)/shard_map/shqk,skd->sqhd/dot_general | solution.py:141
  699.5 11.8 collective-permute-done.60
  718.1 12.3 %collective-permute-done.72 = bf16[128,2048]{1,0:T(8,128)(2,1)S(1)} collective-permute-done((bf16[128,2048]{1,0:T(8,128)(2,1)S(1)}, bf16[128,2048]{1,0:T(8,128)(2,1)S(1)}, u32[]{:S(2)}, u32[]{:S(2)}) %collective-permute-start.72) | collective-permute-done | bytes 524320 | tf_op jit(solution)/shard_map/ppermute | solution.py:19
  730.4 8.8 collective-permute-done.71
  740.8 7.2 convolution_convert_fusion.1
  757.7 12.3 %fusion.18 = bf16[512,2048]{1,0:T(8,128)(2,1)S(1)} fusion(f32[512,2048]{1,0:T(8,128)} %fusion.109, bf16[2048,2048]{1,0:T(8,128)(2,1)} %all-gather.17.cloned.1.call-done, bf16[128,2048]{1,0:T(8,128)(2,1)S(1)} %copy-done.81, bf16[128,2048]{1,0:T(8,128)(2,1)S(1)} %copy-done.83, bf16[128,2048]{1,0:T(8,128)(2,1)} %copy-done.84, bf16[128,2048]{1,0:T(8,128)(2,1)S(1)} %copy-done.20), kind=kOutput, calls=%fused_computation.44 | convolution fusion | flops 4324327424 | bytes 16777216 | tf_op jit(solution)/shard_map/dot_general | solution.py:14
  771.3 8.3 convolution_convert_fusion.10
  783.3 21.7 %collective-permute-done.73 = bf16[128,2048]{1,0:T(8,128)(2,1)S(1)} collective-permute-done((bf16[128,2048]{1,0:T(8,128)(2,1)S(1)}, bf16[128,2048]{1,0:T(8,128)(2,1)S(1)}, u32[]{:S(2)}, u32[]{:S(2)}) %collective-permute-start.73) | collective-permute-done | bytes 524320 | tf_op jit(solution)/shard_map/ppermute | solution.py:19
  811.0 12.3 %collective-permute-done.78 = bf16[128,2048]{1,0:T(8,128)(2,1)S(1)} collective-permute-done((bf16[128,2048]{1,0:T(8,128)(2,1)S(1)}, bf16[128,2048]{1,0:T(8,128)(2,1)S(1)}, u32[]{:S(2)}, u32[]{:S(2)}) %collective-permute-start.78) | collective-permute-done | bytes 524320 | tf_op jit(solution)/shard_map/ppermute | solution.py:19
  823.4 8.6 collective-permute-done.77
  843.0 9.4 fusion.82
  852.4 25.4 %fusion.45 = bf16[2,256,4,128]{1,3,2,0:T(8,128)(2,1)} fusion(f32[2,2048,256,4]{2,1,3,0:T(8,128)} %fusion.82, f32[2,2048,256,4]{2,1,3,0:T(8,128)} %copy-done.6, f32[2,4,256]{2,1,0:T(4,128)S(1)} %bitcast.780, pred[2,256,2048]{1,2,0:T(8,128)(4,1)S(1)} %copy.103, bf16[2,2048,256]{2,1,0:T(8,128)(2,1)} %bitcast.687), kind=kOutput, calls=%fused_computation.123 | convolution fusion | flops 1120145408 | bytes 70795264 | tf_op jit(solution)/shard_map/shqk,skd->sqhd/dot_general | solution.py:141
  884.4 10.2 convolution_convert_fusion.2
  894.7 10.1 convolution_convert_fusion.3
  904.9 25.8 %fusion.32 = f32[2,2048,128]{1,2,0:T(8,128)} fusion(bf16[2,256,4,128]{1,3,2,0:T(8,128)(2,1)} %copy-done.36, f32[2,2048,256,4]{2,1,3,0:T(8,128)} %fusion.82, f32[2,2048,256,4]{2,1,3,0:T(8,128)} %copy-done.6, f32[2,4,256]{2,1,0:T(4,128)S(1)} %bitcast.781, pred[2,256,2048]{1,2,0:T(8,128)(4,1)S(1)} %copy.103), kind=kOutput, calls=%fused_computation.79 | convolution fusion | flops 1119883264 | bytes 37232640 | tf_op jit(solution)/shard_map/shqk,sqhd->skd/dot_general | solution.py:142
  930.7 11.9 convolution_bitcast_fusion
  947.4 5.4 copy.129
  958.9 8.8 convolution_convert_fusion.8
  968.0 12.6 %collective-permute-done.82 = bf16[1024,256]{1,0:T(8,128)(2,1)S(1)} collective-permute-done((bf16[1024,256]{1,0:T(8,128)(2,1)S(1)}, bf16[1024,256]{1,0:T(8,128)(2,1)S(1)}, u32[]{:S(2)}, u32[]{:S(2)}) %collective-permute-start.82) | collective-permute-done | bytes 524320 | tf_op jit(solution)/shard_map/ppermute | solution.py:19
  997.4 5.4 collective-permute-done.87
  1003.7 7.6 collective-permute-done.79
  1016.9 16.6 %collective-permute-done.108 = f32[8,4,128]{2,0,1:T(8,128)S(1)} collective-permute-done((f32[8,4,128]{2,0,1:T(8,128)S(1)}, f32[8,4,128]{2,0,1:T(8,128)S(1)}, u32[]{:S(2)}, u32[]{:S(2)}) %collective-permute-start.108) | collective-permute-done | bytes 16416 | tf_op jit(solution)/shard_map/ppermute | solution.py:19
  1043.5 5.1 collective-permute-done.95
  1052.2 9.6 collective-permute-done.97
  1078.6 6.3 collective-permute-start.103
  1090.6 12.9 %collective-permute-done.103 = bf16[512,256]{1,0:T(8,128)(2,1)} collective-permute-done((bf16[512,256]{1,0:T(8,128)(2,1)}, bf16[512,256]{1,0:T(8,128)(2,1)}, u32[]{:S(2)}, u32[]{:S(2)}) %collective-permute-start.103) | collective-permute-done | bytes 262176 | tf_op jit(solution)/shard_map/ppermute | solution.py:287
  1108.7 5.4 collective-permute-start.105
  1114.1 58.2 %reduce-scatter.17.cloned.1.call-done = bf16[256,2048]{1,0:T(8,128)(2,1)} async-done(((bf16[2048,2048]{1,0:T(8,128)(2,1)}), bf16[256,2048]{1,0:T(8,128)(2,1)}) %reduce-scatter.17.cloned.1.call-update) | async-done | bytes 1048592 | tf_op jit(solution)/shard_map/reduce_scatter | solution.py:286
  1183.7 13.5 %collective-permute-done.104 = bf16[256,2048]{1,0:T(8,128)(2,1)S(1)} collective-permute-done((bf16[256,2048]{1,0:T(8,128)(2,1)}, bf16[256,2048]{1,0:T(8,128)(2,1)S(1)}, u32[]{:S(2)}, u32[]{:S(2)}) %collective-permute-start.104) | collective-permute-done | bytes 1048608 | tf_op jit(solution)/shard_map/ppermute | solution.py:287
  (627 shorter events, 386.1 us)
Async XLA Ops:
  7.2 223.2 %all-gather.11.cloned.1.call-start = ((), (), s32[]{:S(2)}) async-start(), calls=%async_computation.9 | async-start | bytes 2359296 | tf_op jit(solution)/shard_map/all_gather | solution.py:251
  22.0 228.0 %all-gather.13.cloned.1.call-start = ((), (), s32[]{:S(2)}) async-start(), calls=%async_computation.10 | async-start | bytes 2359296 | tf_op jit(solution)/shard_map/all_gather | solution.py:251
  35.3 270.4 %all-gather.15.cloned.1.call-start = ((), (), s32[]{:S(2)}) async-start(), calls=%async_computation.11 | async-start | bytes 9437184 | tf_op jit(solution)/shard_map/all_gather | solution.py:251
  35.5 25.1 %collective-permute-start.53 = (bf16[256,2048]{1,0:T(8,128)(2,1)S(1)}, bf16[256,2048]{1,0:T(8,128)(2,1)}, u32[]{:S(2)}, u32[]{:S(2)}) collective-permute-start(bf16[256,2048]{1,0:T(8,128)(2,1)S(1)} %dynamic-slice_bitcast_fusion), channel_id=1, source_target_pairs={{16,0},{17,1},{18,2},{19,3},{20,4},{21,5},{22,6},{23,7},{24,8},{25... | collective-permute-start | bytes 3145736 | tf_op jit(solution)/shard_map/ppermute | solution.py:247
  36.8 25.8 %collective-permute-start.30 = (bf16[256,2048]{1,0:T(8,128)(2,1)S(1)}, bf16[256,2048]{1,0:T(8,128)(2,1)}, u32[]{:S(2)}, u32[]{:S(2)}) collective-permute-start(bf16[256,2048]{1,0:T(8,128)(2,1)S(1)} %dynamic-slice_bitcast_fusion), channel_id=1, source_target_pairs={{0,16},{1,17},{2,18},{3,19},{4,20},{5,21},{6,22},{7,23},{8,24},{9,... | collective-permute-start | bytes 3145736 | tf_op jit(solution)/shard_map/ppermute | solution.py:247
  66.0 250.1 %all-gather.17.cloned.1.call-start = ((), (), s32[]{:S(2)}) async-start(), calls=%async_computation.12 | async-start | bytes 9437184 | tf_op jit(solution)/shard_map/all_gather | solution.py:251
  98.7 277.6 %all-gather.19.cloned.1.call-start = ((), (), s32[]{:S(2)}) async-start(), calls=%async_computation.13 | async-start | bytes 2359296 | tf_op jit(solution)/shard_map/all_gather | solution.py:251
  99.3 322.4 %all-gather.21.cloned.1.call-start = ((), (), s32[]{:S(2)}) async-start(), calls=%async_computation.14 | async-start | bytes 2359296 | tf_op jit(solution)/shard_map/all_gather | solution.py:251
  112.1 358.8 %all-gather.23.cloned.1.call-start = ((), (), s32[]{:S(2)}) async-start(), calls=%async_computation.15 | async-start | bytes 9437184 | tf_op jit(solution)/shard_map/all_gather | solution.py:251
  113.6 35.5 %collective-permute-start.11 = (bf16[8,144,256]{2,1,0:T(8,128)(2,1)S(1)}, bf16[8,144,256]{2,1,0:T(8,128)(2,1)}, u32[]{:S(2)}, u32[]{:S(2)}) collective-permute-start(bf16[8,144,256]{2,1,0:T(8,128)(2,1)S(1)} %bitcast.694), channel_id=1, source_target_pairs={{0,17},{1,16},{16,1},{17,0},{2,19},{3,18},{18,3},{19,2},{4,21},{5,... | collective-permute-start | bytes 1769480 | tf_op jit(solution)/shard_map/ppermute | solution.py:19
  114.2 28.6 %collective-permute-start.10 = (bf16[8,144,256]{2,1,0:T(8,128)(2,1)S(1)}, bf16[8,144,256]{2,1,0:T(8,128)(2,1)S(1)}, u32[]{:S(2)}, u32[]{:S(2)}) collective-permute-start(bf16[8,144,256]{2,1,0:T(8,128)(2,1)S(1)} %bitcast.695), channel_id=1, source_target_pairs={{0,16},{1,17},{16,0},{17,1},{2,18},{3,19},{18,2},{19,3},{4,20},{5,... | collective-permute-start | bytes 1769480 | tf_op jit(solution)/shard_map/ppermute | solution.py:19
  116.6 25.9 %collective-permute-start.9 = (bf16[8,144,256]{2,1,0:T(8,128)(2,1)S(1)}, bf16[8,144,256]{2,1,0:T(8,128)(2,1)S(1)}, u32[]{:S(2)}, u32[]{:S(2)}) collective-permute-start(bf16[8,144,256]{2,1,0:T(8,128)(2,1)S(1)} %bitcast.696), channel_id=1, source_target_pairs={{0,1},{1,0},{16,17},{17,16},{2,3},{3,2},{18,19},{19,18},{4,5},{5,4... | collective-permute-start | bytes 1769480 | tf_op jit(solution)/shard_map/ppermute | solution.py:19
  143.6 366.4 %all-gather.9.cloned.1.call-start = ((), (), s32[]{:S(2)}) async-start(), calls=%async_computation.8 | async-start | bytes 9437184 | tf_op jit(solution)/shard_map/all_gather | solution.py:251
  180.1 50.2 %collective-permute-start.21 = (bf16[128,2048]{1,0:T(8,128)(2,1)S(1)}, bf16[128,2048]{1,0:T(8,128)(2,1)}, u32[]{:S(2)}, u32[]{:S(2)}) collective-permute-start(bf16[128,2048]{1,0:T(8,128)(2,1)S(1)} %fusion.56), channel_id=1, source_target_pairs={{0,17},{1,16},{16,1},{17,0},{2,19},{3,18},{18,3},{19,2},{4,21},{5,... | collective-permute-start | bytes 1572872 | tf_op jit(solution)/shard_map/ppermute | solution.py:19
  182.7 47.6 %collective-permute-start.20 = (bf16[128,2048]{1,0:T(8,128)(2,1)S(1)}, bf16[128,2048]{1,0:T(8,128)(2,1)}, u32[]{:S(2)}, u32[]{:S(2)}) collective-permute-start(bf16[128,2048]{1,0:T(8,128)(2,1)S(1)} %fusion.56), channel_id=1, source_target_pairs={{0,16},{1,17},{16,0},{17,1},{2,18},{3,19},{18,2},{19,3},{4,20},{5,... | collective-permute-start | bytes 1572872 | tf_op jit(solution)/shard_map/ppermute | solution.py:19
  183.2 47.1 %collective-permute-start.19 = (bf16[128,2048]{1,0:T(8,128)(2,1)S(1)}, bf16[128,2048]{1,0:T(8,128)(2,1)}, u32[]{:S(2)}, u32[]{:S(2)}) collective-permute-start(bf16[128,2048]{1,0:T(8,128)(2,1)S(1)} %fusion.56), channel_id=1, source_target_pairs={{0,1},{1,0},{16,17},{17,16},{2,3},{3,2},{18,19},{19,18},{4,5},{5,4... | collective-permute-start | bytes 1572872 | tf_op jit(solution)/shard_map/ppermute | solution.py:19
  184.2 43.3 %collective-permute-start.17 = (bf16[8,128,256]{2,1,0:T(8,128)(2,1)S(1)}, bf16[8,128,256]{2,1,0:T(8,128)(2,1)}, u32[]{:S(2)}, u32[]{:S(2)}) collective-permute-start(bf16[8,128,256]{2,1,0:T(8,128)(2,1)S(1)} %constant_dynamic-update-slice_fusion), channel_id=1, source_target_pairs={{0,16},{1,17},{16,0},{17,1},{2,18},{3,19},{18,2},{19,3},{4,20},{5,... | collective-permute-start | bytes 1572872 | tf_op jit(solution)/shard_map/ppermute | solution.py:19
  194.5 33.0 %collective-permute-start.16 = (bf16[8,128,256]{2,1,0:T(8,128)(2,1)S(1)}, bf16[8,128,256]{2,1,0:T(8,128)(2,1)}, u32[]{:S(2)}, u32[]{:S(2)}) collective-permute-start(bf16[8,128,256]{2,1,0:T(8,128)(2,1)S(1)} %constant_dynamic-update-slice_fusion), channel_id=1, source_target_pairs={{0,1},{1,0},{16,17},{17,16},{2,3},{3,2},{18,19},{19,18},{4,5},{5,4... | collective-permute-start | bytes 1572872 | tf_op jit(solution)/shard_map/ppermute | solution.py:19
  253.2 25.1 %collective-permute-start.24 = (bf16[128,2048]{1,0:T(8,128)(2,1)S(1)}, bf16[128,2048]{1,0:T(8,128)(2,1)S(1)}, u32[]{:S(2)}, u32[]{:S(2)}) collective-permute-start(bf16[128,2048]{1,0:T(8,128)(2,1)S(1)} %get-tuple-element.84), channel_id=1, source_target_pairs={{0,1},{1,0},{16,17},{17,16},{2,3},{3,2},{18,19},{19,18},{4,5},{5,4... | collective-permute-start | bytes 1572872 | tf_op jit(solution)/shard_map/ppermute | solution.py:19
  281.2 24.6 %collective-permute-start.28 = (bf16[128,2048]{1,0:T(8,128)(2,1)S(1)}, bf16[128,2048]{1,0:T(8,128)(2,1)}, u32[]{:S(2)}, u32[]{:S(2)}) collective-permute-start(bf16[128,2048]{1,0:T(8,128)(2,1)S(1)} %add_convert_fusion.3), channel_id=1, source_target_pairs={{0,16},{1,17},{16,0},{17,1},{2,18},{3,19},{18,2},{19,3},{4,20},{5,... | collective-permute-start | bytes 1572872 | tf_op jit(solution)/shard_map/ppermute | solution.py:19
  284.2 783.7 %reduce-scatter.23.cloned.1.call-start = ((), (), s32[]{:S(2)}) async-start(), calls=%async_computation.23 | async-start | bytes 9437184 | tf_op jit(solution)/shard_map/reduce_scatter | solution.py:286
  325.7 25.1 %collective-permute-start.32 = (bf16[128,2048]{1,0:T(8,128)(2,1)S(1)}, bf16[128,2048]{1,0:T(8,128)(2,1)S(1)}, u32[]{:S(2)}, u32[]{:S(2)}) collective-permute-start(bf16[128,2048]{1,0:T(8,128)(2,1)S(1)} %get-tuple-element.81), channel_id=1, source_target_pairs={{0,1},{1,0},{16,17},{17,16},{2,3},{3,2},{18,19},{19,18},{4,5},{5,4... | collective-permute-start | bytes 1572872 | tf_op jit(solution)/shard_map/ppermute | solution.py:19
  327.7 24.4 %collective-permute-start.33 = (bf16[128,2048]{1,0:T(8,128)(2,1)S(1)}, bf16[128,2048]{1,0:T(8,128)(2,1)S(1)}, u32[]{:S(2)}, u32[]{:S(2)}) collective-permute-start(bf16[128,2048]{1,0:T(8,128)(2,1)S(1)} %get-tuple-element.83), channel_id=1, source_target_pairs={{0,16},{1,17},{16,0},{17,1},{2,18},{3,19},{18,2},{19,3},{4,20},{5,... | collective-permute-start | bytes 1572872 | tf_op jit(solution)/shard_map/ppermute | solution.py:19
  358.7 26.7 %collective-permute-start.43 = (bf16[128,2048]{1,0:T(8,128)(2,1)S(1)}, bf16[128,2048]{1,0:T(8,128)(2,1)}, u32[]{:S(2)}, u32[]{:S(2)}) collective-permute-start(bf16[128,2048]{1,0:T(8,128)(2,1)S(1)} %fusion.53), channel_id=1, source_target_pairs={{0,16},{1,17},{16,0},{17,1},{2,18},{3,19},{18,2},{19,3},{4,20},{5,... | collective-permute-start | bytes 1572872 | tf_op jit(solution)/shard_map/ppermute | solution.py:19
  370.0 26.6 %collective-permute-start.41 = (bf16[8,128,256]{2,1,0:T(8,128)(2,1)S(1)}, bf16[8,128,256]{2,1,0:T(8,128)(2,1)}, u32[]{:S(2)}, u32[]{:S(2)}) collective-permute-start(bf16[8,128,256]{2,1,0:T(8,128)(2,1)S(1)} %constant_dynamic-update-slice_fusion.5), channel_id=1, source_target_pairs={{0,17},{1,16},{16,1},{17,0},{2,19},{3,18},{18,3},{19,2},{4,21},{5,... | collective-permute-start | bytes 1572872 | tf_op jit(solution)/shard_map/ppermute | solution.py:19
  372.4 32.6 %collective-permute-start.40 = (bf16[8,128,256]{2,1,0:T(8,128)(2,1)S(1)}, bf16[8,128,256]{2,1,0:T(8,128)(2,1)}, u32[]{:S(2)}, u32[]{:S(2)}) collective-permute-start(bf16[8,128,256]{2,1,0:T(8,128)(2,1)S(1)} %constant_dynamic-update-slice_fusion.5), channel_id=1, source_target_pairs={{0,16},{1,17},{16,0},{17,1},{2,18},{3,19},{18,2},{19,3},{4,20},{5,... | collective-permute-start | bytes 1572872 | tf_op jit(solution)/shard_map/ppermute | solution.py:19
  374.7 30.3 %collective-permute-start.39 = (bf16[8,128,256]{2,1,0:T(8,128)(2,1)S(1)}, bf16[8,128,256]{2,1,0:T(8,128)(2,1)}, u32[]{:S(2)}, u32[]{:S(2)}) collective-permute-start(bf16[8,128,256]{2,1,0:T(8,128)(2,1)S(1)} %constant_dynamic-update-slice_fusion.5), channel_id=1, source_target_pairs={{0,1},{1,0},{16,17},{17,16},{2,3},{3,2},{18,19},{19,18},{4,5},{5,4... | collective-permute-start | bytes 1572872 | tf_op jit(solution)/shard_map/ppermute | solution.py:19
  424.9 25.1 %collective-permute-start.47 = (bf16[128,2048]{1,0:T(8,128)(2,1)S(1)}, bf16[128,2048]{1,0:T(8,128)(2,1)S(1)}, u32[]{:S(2)}, u32[]{:S(2)}) collective-permute-start(bf16[128,2048]{1,0:T(8,128)(2,1)S(1)} %get-tuple-element.78), channel_id=1, source_target_pairs={{0,1},{1,0},{16,17},{17,16},{2,3},{3,2},{18,19},{19,18},{4,5},{5,4... | collective-permute-start | bytes 1572872 | tf_op jit(solution)/shard_map/ppermute | solution.py:19
  453.7 26.9 %collective-permute-start.51 = (bf16[128,2048]{1,0:T(8,128)(2,1)}, bf16[128,2048]{1,0:T(8,128)(2,1)}, u32[]{:S(2)}, u32[]{:S(2)}) collective-permute-start(bf16[128,2048]{1,0:T(8,128)(2,1)} %add_convert_fusion.1), channel_id=1, source_target_pairs={{0,16},{1,17},{16,0},{17,1},{2,18},{3,19},{18,2},{19,3},{4,20},{5,... | collective-permute-start | bytes 1572872 | tf_op jit(solution)/shard_map/ppermute | solution.py:19
  456.2 24.4 %collective-permute-start.50 = (bf16[128,2048]{1,0:T(8,128)(2,1)}, bf16[128,2048]{1,0:T(8,128)(2,1)}, u32[]{:S(2)}, u32[]{:S(2)}) collective-permute-start(bf16[128,2048]{1,0:T(8,128)(2,1)} %add_convert_fusion.1), channel_id=1, source_target_pairs={{0,1},{1,0},{16,17},{17,16},{2,3},{3,2},{18,19},{19,18},{4,5},{5,4... | collective-permute-start | bytes 1572872 | tf_op jit(solution)/shard_map/ppermute | solution.py:19
  457.7 34.0 %collective-permute-start.3 = (bf16[128,2048]{1,0:T(8,128)(2,1)S(1)}, bf16[128,2048]{1,0:T(8,128)(2,1)}, u32[]{:S(2)}, u32[]{:S(2)}) collective-permute-start(bf16[128,2048]{1,0:T(8,128)(2,1)S(1)} %bitcast_select_fusion.7), channel_id=1, source_target_pairs={{0,17},{1,16},{16,1},{17,0},{2,19},{3,18},{18,3},{19,2},{4,21},{5,... | collective-permute-start | bytes 1572872 | tf_op jit(solution)/shard_map/ppermute | solution.py:19
  457.8 43.4 %collective-permute-start.2 = (bf16[128,2048]{1,0:T(8,128)(2,1)S(1)}, bf16[128,2048]{1,0:T(8,128)(2,1)}, u32[]{:S(2)}, u32[]{:S(2)}) collective-permute-start(bf16[128,2048]{1,0:T(8,128)(2,1)S(1)} %bitcast_select_fusion.7), channel_id=1, source_target_pairs={{0,16},{1,17},{16,0},{17,1},{2,18},{3,19},{18,2},{19,3},{4,20},{5,... | collective-permute-start | bytes 1572872 | tf_op jit(solution)/shard_map/ppermute | solution.py:19
  469.2 32.0 %collective-permute-start.1 = (bf16[128,2048]{1,0:T(8,128)(2,1)S(1)}, bf16[128,2048]{1,0:T(8,128)(2,1)}, u32[]{:S(2)}, u32[]{:S(2)}) collective-permute-start(bf16[128,2048]{1,0:T(8,128)(2,1)S(1)} %bitcast_select_fusion.7), channel_id=1, source_target_pairs={{0,1},{1,0},{16,17},{17,16},{2,3},{3,2},{18,19},{19,18},{4,5},{5,4... | collective-permute-start | bytes 1572872 | tf_op jit(solution)/shard_map/ppermute | solution.py:19
  509.9 567.2 %reduce-scatter.21.cloned.1.call-start = ((), (), s32[]{:S(2)}) async-start(), calls=%async_computation.22 | async-start | bytes 9437184 | tf_op jit(solution)/shard_map/reduce_scatter | solution.py:286
  531.3 24.7 %collective-permute-start.54 = (bf16[128,2048]{1,0:T(8,128)(2,1)S(1)}, bf16[128,2048]{1,0:T(8,128)(2,1)S(1)}, u32[]{:S(2)}, u32[]{:S(2)}) collective-permute-start(bf16[128,2048]{1,0:T(8,128)(2,1)S(1)} %get-tuple-element.68), channel_id=1, source_target_pairs={{0,1},{1,0},{16,17},{17,16},{2,3},{3,2},{18,19},{19,18},{4,5},{5,4... | collective-permute-start | bytes 1572872 | tf_op jit(solution)/shard_map/ppermute | solution.py:19
  560.8 24.5 %collective-permute-start.58 = (bf16[128,2048]{1,0:T(8,128)(2,1)S(1)}, bf16[128,2048]{1,0:T(8,128)(2,1)S(1)}, u32[]{:S(2)}, u32[]{:S(2)}) collective-permute-start(bf16[128,2048]{1,0:T(8,128)(2,1)S(1)} %fusion.86), channel_id=1, source_target_pairs={{0,16},{1,17},{16,0},{17,1},{2,18},{3,19},{18,2},{19,3},{4,20},{5,... | collective-permute-start | bytes 1572872 | tf_op jit(solution)/shard_map/ppermute | solution.py:19
  648.3 33.8 %collective-permute-start.63 = (bf16[1024,256]{1,0:T(8,128)(2,1)}, bf16[1024,256]{1,0:T(8,128)(2,1)S(1)}, u32[]{:S(2)}, u32[]{:S(2)}) collective-permute-start(bf16[1024,256]{1,0:T(8,128)(2,1)} %get-tuple-element.65), channel_id=1, source_target_pairs={{0,1},{1,0},{16,17},{17,16},{2,3},{3,2},{18,19},{19,18},{4,5},{5,4... | collective-permute-start | bytes 1572872 | tf_op jit(solution)/shard_map/ppermute | solution.py:19
  648.9 33.2 %collective-permute-start.65 = (bf16[1024,256]{1,0:T(8,128)(2,1)}, bf16[1024,256]{1,0:T(8,128)(2,1)S(1)}, u32[]{:S(2)}, u32[]{:S(2)}) collective-permute-start(bf16[1024,256]{1,0:T(8,128)(2,1)} %get-tuple-element.66), channel_id=1, source_target_pairs={{0,17},{1,16},{16,1},{17,0},{2,19},{3,18},{18,3},{19,2},{4,21},{5,... | collective-permute-start | bytes 1572872 | tf_op jit(solution)/shard_map/ppermute | solution.py:19
  649.3 34.3 %collective-permute-start.64 = (bf16[1024,256]{1,0:T(8,128)(2,1)}, bf16[1024,256]{1,0:T(8,128)(2,1)}, u32[]{:S(2)}, u32[]{:S(2)}) collective-permute-start(bf16[1024,256]{1,0:T(8,128)(2,1)} %get-tuple-element.67), channel_id=1, source_target_pairs={{0,16},{1,17},{16,0},{17,1},{2,18},{3,19},{18,2},{19,3},{4,20},{5,... | collective-permute-start | bytes 1572872 | tf_op jit(solution)/shard_map/ppermute | solution.py:19
  685.8 25.6 %collective-permute-start.60 = (bf16[128,2048]{1,0:T(8,128)(2,1)S(1)}, bf16[128,2048]{1,0:T(8,128)(2,1)S(1)}, u32[]{:S(2)}, u32[]{:S(2)}) collective-permute-start(bf16[128,2048]{1,0:T(8,128)(2,1)S(1)} %get-tuple-element.62), channel_id=1, source_target_pairs={{0,1},{1,0},{16,17},{17,16},{2,3},{3,2},{18,19},{19,18},{4,5},{5,4... | collective-permute-start | bytes 1572872 | tf_op jit(solution)/shard_map/ppermute | solution.py:19
  686.5 24.9 %collective-permute-start.62 = (bf16[128,2048]{1,0:T(8,128)(2,1)S(1)}, bf16[128,2048]{1,0:T(8,128)(2,1)S(1)}, u32[]{:S(2)}, u32[]{:S(2)}) collective-permute-start(bf16[128,2048]{1,0:T(8,128)(2,1)S(1)} %get-tuple-element.63), channel_id=1, source_target_pairs={{0,17},{1,16},{16,1},{17,0},{2,19},{3,18},{18,3},{19,2},{4,21},{5,... | collective-permute-start | bytes 1572872 | tf_op jit(solution)/shard_map/ppermute | solution.py:19
  687.3 25.3 %collective-permute-start.61 = (bf16[128,2048]{1,0:T(8,128)(2,1)S(1)}, bf16[128,2048]{1,0:T(8,128)(2,1)S(1)}, u32[]{:S(2)}, u32[]{:S(2)}) collective-permute-start(bf16[128,2048]{1,0:T(8,128)(2,1)S(1)} %get-tuple-element.64), channel_id=1, source_target_pairs={{0,16},{1,17},{16,0},{17,1},{2,18},{3,19},{18,2},{19,3},{4,20},{5,... | collective-permute-start | bytes 1572872 | tf_op jit(solution)/shard_map/ppermute | solution.py:19
  748.0 330.6 %reduce-scatter.15.cloned.1.call-start = ((), (), s32[]{:S(2)}) async-start(), calls=%async_computation.19 | async-start | bytes 2359296 | tf_op jit(solution)/shard_map/reduce_scatter | solution.py:286
  753.2 331.7 %reduce-scatter.11.cloned.1.call-start = ((), (), s32[]{:S(2)}) async-start(), calls=%async_computation.17 | async-start | bytes 2359296 | tf_op jit(solution)/shard_map/reduce_scatter | solution.py:286
  757.6 330.1 %reduce-scatter.13.cloned.1.call-start = ((), (), s32[]{:S(2)}) async-start(), calls=%async_computation.18 | async-start | bytes 2359296 | tf_op jit(solution)/shard_map/reduce_scatter | solution.py:286
  779.7 25.3 %collective-permute-start.73 = (bf16[128,2048]{1,0:T(8,128)(2,1)S(1)}, bf16[128,2048]{1,0:T(8,128)(2,1)S(1)}, u32[]{:S(2)}, u32[]{:S(2)}) collective-permute-start(bf16[128,2048]{1,0:T(8,128)(2,1)S(1)} %get-tuple-element.59), channel_id=1, source_target_pairs={{0,1},{1,0},{16,17},{17,16},{2,3},{3,2},{18,19},{19,18},{4,5},{5,4... | collective-permute-start | bytes 1572872 | tf_op jit(solution)/shard_map/ppermute | solution.py:19
  836.2 267.3 %reduce-scatter.9.cloned.1.call-start = ((), (), s32[]{:S(2)}) async-start(), calls=%async_computation.16 | async-start | bytes 2359296 | tf_op jit(solution)/shard_map/reduce_scatter | solution.py:286
  884.0 224.8 %reduce-scatter.19.cloned.1.call-start = ((), (), s32[]{:S(2)}) async-start(), calls=%async_computation.21 | async-start | bytes 9437184 | tf_op jit(solution)/shard_map/reduce_scatter | solution.py:286
  894.7 277.6 %reduce-scatter.17.cloned.1.call-start = ((), (), s32[]{:S(2)}) async-start(), calls=%async_computation.20 | async-start | bytes 9437184 | tf_op jit(solution)/shard_map/reduce_scatter | solution.py:286
  955.4 25.1 %collective-permute-start.82 = (bf16[1024,256]{1,0:T(8,128)(2,1)S(1)}, bf16[1024,256]{1,0:T(8,128)(2,1)S(1)}, u32[]{:S(2)}, u32[]{:S(2)}) collective-permute-start(bf16[1024,256]{1,0:T(8,128)(2,1)S(1)} %get-tuple-element.56), channel_id=1, source_target_pairs={{0,1},{1,0},{16,17},{17,16},{2,3},{3,2},{18,19},{19,18},{4,5},{5,4... | collective-permute-start | bytes 1572872 | tf_op jit(solution)/shard_map/ppermute | solution.py:19
  985.2 26.1 %collective-permute-start.79 = (bf16[128,2048]{1,0:T(8,128)(2,1)S(1)}, bf16[128,2048]{1,0:T(8,128)(2,1)S(1)}, u32[]{:S(2)}, u32[]{:S(2)}) collective-permute-start(bf16[128,2048]{1,0:T(8,128)(2,1)S(1)} %get-tuple-element.53), channel_id=1, source_target_pairs={{0,1},{1,0},{16,17},{17,16},{2,3},{3,2},{18,19},{19,18},{4,5},{5,4... | collective-permute-start | bytes 1572872 | tf_op jit(solution)/shard_map/ppermute | solution.py:19
  986.4 24.9 %collective-permute-start.81 = (bf16[128,2048]{1,0:T(8,128)(2,1)S(1)}, bf16[128,2048]{1,0:T(8,128)(2,1)S(1)}, u32[]{:S(2)}, u32[]{:S(2)}) collective-permute-start(bf16[128,2048]{1,0:T(8,128)(2,1)S(1)} %get-tuple-element.54), channel_id=1, source_target_pairs={{0,17},{1,16},{16,1},{17,0},{2,19},{3,18},{18,3},{19,2},{4,21},{5,... | collective-permute-start | bytes 1572872 | tf_op jit(solution)/shard_map/ppermute | solution.py:19
  986.7 26.2 %collective-permute-start.80 = (bf16[128,2048]{1,0:T(8,128)(2,1)S(1)}, bf16[128,2048]{1,0:T(8,128)(2,1)S(1)}, u32[]{:S(2)}, u32[]{:S(2)}) collective-permute-start(bf16[128,2048]{1,0:T(8,128)(2,1)S(1)} %get-tuple-element.55), channel_id=1, source_target_pairs={{0,16},{1,17},{16,0},{17,1},{2,18},{3,19},{18,2},{19,3},{4,20},{5,... | collective-permute-start | bytes 1572872 | tf_op jit(solution)/shard_map/ppermute | solution.py:19
  996.5 40.9 %collective-permute-start.89 = (bf16[128,2048]{1,0:T(8,128)(2,1)S(1)}, bf16[128,2048]{1,0:T(8,128)(2,1)S(1)}, u32[]{:S(2)}, u32[]{:S(2)}) collective-permute-start(bf16[128,2048]{1,0:T(8,128)(2,1)S(1)} %get-tuple-element.71), channel_id=1, source_target_pairs={{0,1},{1,0},{16,17},{17,16},{2,3},{3,2},{18,19},{19,18},{4,5},{5,4... | collective-permute-start | bytes 1572872 | tf_op jit(solution)/shard_map/ppermute | solution.py:19
  1002.8 37.1 %collective-permute-start.91 = (bf16[128,2048]{1,0:T(8,128)(2,1)S(1)}, bf16[128,2048]{1,0:T(8,128)(2,1)S(1)}, u32[]{:S(2)}, u32[]{:S(2)}) collective-permute-start(bf16[128,2048]{1,0:T(8,128)(2,1)S(1)} %get-tuple-element.72), channel_id=1, source_target_pairs={{0,17},{1,16},{16,1},{17,0},{2,19},{3,18},{18,3},{19,2},{4,21},{5,... | collective-permute-start | bytes 1572872 | tf_op jit(solution)/shard_map/ppermute | solution.py:19
  1011.3 28.7 %collective-permute-start.90 = (bf16[128,2048]{1,0:T(8,128)(2,1)S(1)}, bf16[128,2048]{1,0:T(8,128)(2,1)S(1)}, u32[]{:S(2)}, u32[]{:S(2)}) collective-permute-start(bf16[128,2048]{1,0:T(8,128)(2,1)S(1)} %get-tuple-element.73), channel_id=1, source_target_pairs={{0,16},{1,17},{16,0},{17,1},{2,18},{3,19},{18,2},{19,3},{4,20},{5,... | collective-permute-start | bytes 1572872 | tf_op jit(solution)/shard_map/ppermute | solution.py:19
  1037.4 24.4 %collective-permute-start.97 = (bf16[8,128,256]{2,1,0:T(8,128)(2,1)S(1)}, bf16[8,128,256]{2,1,0:T(8,128)(2,1)S(1)}, u32[]{:S(2)}, u32[]{:S(2)}) collective-permute-start(bf16[8,128,256]{2,1,0:T(8,128)(2,1)S(1)} %get-tuple-element.50), channel_id=1, source_target_pairs={{0,17},{1,16},{16,1},{17,0},{2,19},{3,18},{18,3},{19,2},{4,21},{5,... | collective-permute-start | bytes 1572872 | tf_op jit(solution)/shard_map/ppermute | solution.py:19
  1067.8 111.6 %collective-permute-start.107 = (bf16[2048,256]{1,0:T(8,128)(2,1)}, bf16[2048,256]{1,0:T(8,128)(2,1)}, u32[]{:S(2)}, u32[]{:S(2)}) collective-permute-start(bf16[2048,256]{1,0:T(8,128)(2,1)} %reduce-scatter.23.cloned.1.call-done), channel_id=1, source_target_pairs={{0,16},{1,17},{2,18},{3,19},{4,20},{5,21},{6,22},{7,23},{8,24},{9,... | collective-permute-start | bytes 3145736 | tf_op jit(solution)/shard_map/ppermute | solution.py:287
  1077.1 102.4 %collective-permute-start.106 = (bf16[2048,256]{1,0:T(8,128)(2,1)}, bf16[2048,256]{1,0:T(8,128)(2,1)}, u32[]{:S(2)}, u32[]{:S(2)}) collective-permute-start(bf16[2048,256]{1,0:T(8,128)(2,1)} %reduce-scatter.21.cloned.1.call-done), channel_id=1, source_target_pairs={{16,0},{17,1},{18,2},{19,3},{20,4},{21,5},{22,6},{23,7},{24,8},{25... | collective-permute-start | bytes 3145736 | tf_op jit(solution)/shard_map/ppermute | solution.py:287
  1078.6 24.9 %collective-permute-start.103 = (bf16[512,256]{1,0:T(8,128)(2,1)}, bf16[512,256]{1,0:T(8,128)(2,1)}, u32[]{:S(2)}, u32[]{:S(2)}) collective-permute-start(bf16[512,256]{1,0:T(8,128)(2,1)} %reduce-scatter.15.cloned.1.call-done), channel_id=1, source_target_pairs={{0,16},{1,17},{2,18},{3,19},{4,20},{5,21},{6,22},{7,23},{8,24},{9,... | collective-permute-start | bytes 786440 | tf_op jit(solution)/shard_map/ppermute | solution.py:287
  1087.7 26.4 %collective-permute-start.102 = (bf16[512,256]{1,0:T(8,128)(2,1)}, bf16[512,256]{1,0:T(8,128)(2,1)}, u32[]{:S(2)}, u32[]{:S(2)}) collective-permute-start(bf16[512,256]{1,0:T(8,128)(2,1)} %reduce-scatter.13.cloned.1.call-done), channel_id=1, source_target_pairs={{16,0},{17,1},{18,2},{19,3},{20,4},{21,5},{22,6},{23,7},{24,8},{25... | collective-permute-start | bytes 786440 | tf_op jit(solution)/shard_map/ppermute | solution.py:287
  1103.5 73.7 %collective-permute-start.93 = (bf16[256,512]{1,0:T(8,128)(2,1)}, bf16[256,512]{1,0:T(8,128)(2,1)}, u32[]{:S(2)}, u32[]{:S(2)}) collective-permute-start(bf16[256,512]{1,0:T(8,128)(2,1)} %reduce-scatter.9.cloned.1.call-done), channel_id=1, source_target_pairs={{16,0},{17,1},{18,2},{19,3},{20,4},{21,5},{22,6},{23,7},{24,8},{25... | collective-permute-start | bytes 786440 | tf_op jit(solution)/shard_map/ppermute | solution.py:287
  1108.7 75.0 %collective-permute-start.105 = (bf16[256,2048]{1,0:T(8,128)(2,1)}, bf16[256,2048]{1,0:T(8,128)(2,1)}, u32[]{:S(2)}, u32[]{:S(2)}) collective-permute-start(bf16[256,2048]{1,0:T(8,128)(2,1)} %reduce-scatter.19.cloned.1.call-done), channel_id=1, source_target_pairs={{0,16},{1,17},{2,18},{3,19},{4,20},{5,21},{6,22},{7,23},{8,24},{9,... | collective-permute-start | bytes 3145736 | tf_op jit(solution)/shard_map/ppermute | solution.py:287
  1172.3 24.8 %collective-permute-start.104 = (bf16[256,2048]{1,0:T(8,128)(2,1)}, bf16[256,2048]{1,0:T(8,128)(2,1)S(1)}, u32[]{:S(2)}, u32[]{:S(2)}) collective-permute-start(bf16[256,2048]{1,0:T(8,128)(2,1)} %reduce-scatter.17.cloned.1.call-done), channel_id=1, source_target_pairs={{16,0},{17,1},{18,2},{19,3},{20,4},{21,5},{22,6},{23,7},{24,8},{25... | collective-permute-start | bytes 3145736 | tf_op jit(solution)/shard_map/ppermute | solution.py:287
  (160 other events, 3558.6 us)
Sparse Core Ops, SparseCore 0:
  22.1 32.1 all-gather.10
  55.9 30.3 all-gather.12
  88.4 91.3 all-gather.14
  181.9 81.5 all-gather.16
  264.9 27.2 all-gather.18
  293.7 30.3 all-gather.20
  325.6 86.5 all-gather.22
  413.9 80.9 all-gather.8
  510.1 88.0 reduce-scatter.22
  748.1 88.2 reduce-scatter.20
  838.7 34.1 reduce-scatter.14
  875.0 34.2 reduce-scatter.10
  911.6 34.3 reduce-scatter.12
  948.2 34.3 reduce-scatter.8
  984.8 94.9 reduce-scatter.18
  1081.9 90.3 reduce-scatter.16

commit v2 on v1

v2 whole, which is shorter than its diff:
```python
import functools
import math

import jax
import jax.numpy as jnp
from jax import lax
from jax.experimental import pallas as pl
from jax.experimental.pallas import tpu as pltpu
from jax.sharding import PartitionSpec as P

SPAN = 256
EPSILON = 1e-05
NEGATIVE = -1000000000.0
BF16 = jnp.bfloat16
F32 = jnp.float32
LOG2E = math.log2(math.e)


def dot(left, right, dims):
    return lax.dot_general(left, right, ((dims[0], dims[1]), ((), ())), preferred_element_type=F32)


def swap_quad(block, offset):
    size = lax.axis_size("section") * lax.axis_size("tensor")
    return lax.ppermute(block, ("section", "tensor"), [(i, i ^ offset) for i in range(size)])


def swap_dp(block, offset):
    return lax.ppermute(block, "dp", [(i, i ^ offset) for i in range(lax.axis_size("dp"))])


def quad_size():
    return lax.axis_size("section") * lax.axis_size("tensor")


def spread(block):
    return jnp.concatenate([block] + [swap_quad(block, k) for k in range(1, quad_size())], 0)


def collect(partial):
    rows = partial.shape[0] // quad_size()
    total = partial[:rows].astype(F32)
    for k in range(1, quad_size()):
        total = total + swap_quad(partial[k * rows : (k + 1) * rows], k).astype(F32)
    return total


def gather_dp(block):
    count = lax.axis_size("dp")
    far = [block] + [swap_dp(block, 2 * j) for j in range(1, count // 2)]
    near = swap_dp(jnp.stack(far), 1)
    return jnp.stack(far), near


def scatter_dp(near_even, near_odd):
    halves = near_even + swap_dp(near_odd.astype(BF16), 1).astype(F32)
    total = halves[0]
    for j in range(1, halves.shape[0]):
        total = total + swap_dp(halves[j].astype(BF16), 2 * j).astype(F32)
    return total


def scatter_all(blocks, wire):
    sections, count, tensors = blocks.shape[:3]
    me_s, me_d, me_t = lax.axis_index("section"), lax.axis_index("dp"), lax.axis_index("tensor")

    def pick(s, t):
        one = lax.dynamic_index_in_dim(blocks, me_s ^ s, 0, keepdims=False)
        return lax.dynamic_index_in_dim(one, me_t ^ t, 1, keepdims=False)

    total = pick(0, 0)
    for k in range(1, sections * tensors):
        total = total + swap_quad(pick(k // tensors, k % tensors).astype(wire), k).astype(F32)
    pairs = total.reshape((count // 2, 2) + total.shape[1:])
    core = me_d % 2
    kept = lax.dynamic_index_in_dim(pairs, core, 1, keepdims=False)
    given = lax.dynamic_index_in_dim(pairs, 1 - core, 1, keepdims=False)
    kept = kept + swap_dp(given.astype(wire), 1).astype(F32)
    place = me_d // 2
    result = lax.dynamic_index_in_dim(kept, place, 0, keepdims=False)
    for j in range(1, count // 2):
        piece = lax.dynamic_index_in_dim(kept, place ^ j, 0, keepdims=False)
        result = result + swap_dp(piece.astype(wire), 2 * j).astype(F32)
    return result


def gather_all(block):
    count, tensors = lax.axis_size("dp"), lax.axis_size("tensor")
    me_s, me_d, me_t = lax.axis_index("section"), lax.axis_index("dp"), lax.axis_index("tensor")
    even, odd = gather_dp(block)
    mine = jnp.stack([even, odd], 1).reshape((count,) + block.shape)
    passed = even
    beside = swap_quad(mine, 1)
    across = swap_quad(mine, tensors)
    corner = swap_quad(across, 1)

    def ordered(bit, own, other):
        return jnp.where(bit == 0, jnp.stack([own, other]), jnp.stack([other, own]))

    parts = ordered(me_s, ordered(me_t, mine, beside), ordered(me_t, across, corner))
    whole = jnp.zeros_like(parts)
    for j in range(count):
        whole = lax.dynamic_update_slice_in_dim(whole, parts[:, :, j : j + 1], me_d ^ j, 2)
    return jnp.swapaxes(whole, 1, 2), passed


def layer_norm(values, scale_row, shift_row):
    centered = values - jnp.mean(values, -1, keepdims=True)
    spread_of = jnp.mean(centered * centered, -1, keepdims=True)
    return centered * lax.rsqrt(spread_of + EPSILON) * scale_row + shift_row


def gelu_tanh(values):
    return jax.nn.gelu(values, approximate=True)


def dot_nn(left, right):
    return dot(left, right, ((1,), (0,)))


def dot_nt(left, right):
    return dot(left, right, ((1,), (1,)))


def dot_tn(left, right):
    return dot(left, right, ((0,), (0,)))


def attend_kernel(rows, heads, head, base_ref, limit_ref, query_ref, keyval_ref, out_ref, log_ref, score_ref, prob_ref):
    keys=keyval_ref.shape[1]; queries=query_ref.shape[0]
    blocks=keys//rows
    scale=head**-0.5*LOG2E
    limit=limit_ref[0]
    offset=lax.broadcasted_iota(jnp.int32,(rows,queries),0)
    values_t=keyval_ref[0,:,head:].T
    for h in range(heads):
        query=query_ref[:,h*head:(h+1)*head]
        def scores(b,peak):
            at=pl.ds(pl.multiple_of(b*rows,rows),rows)
            s=dot_nt(keyval_ref[0,at,:head],query)*scale
            s=jnp.where(offset<=limit-base_ref[b],s,NEGATIVE)
            score_ref[h%2,at,:]=s
            return jnp.maximum(peak,jnp.max(s.reshape(rows//8,8,queries),0))
        peak=lax.fori_loop(0,blocks,scores,jnp.full((8,queries),-jnp.inf,F32),unroll=4)
        peak=jnp.max(peak,0,keepdims=True)
        def probs(b,total):
            at=pl.ds(pl.multiple_of(b*rows,rows),rows)
            p=jnp.exp2(score_ref[h%2,at,:]-peak)
            prob_ref[h%2,at,:]=p.astype(BF16)
            return total+jnp.sum(p.reshape(rows//8,8,queries),0)
        total=lax.fori_loop(0,blocks,probs,jnp.zeros((8,queries),F32),unroll=4)
        total=jnp.sum(total,0,keepdims=True)
        out=dot_nn(values_t,prob_ref[h%2])*(1.0/total)
        out_ref[:,h*head:(h+1)*head]=out.T.astype(BF16)
        log_ref[0,h:h+1,:]=peak+jnp.log2(total)

def attend_forward(queries, keyval, limits, bases, rows):
    seqs,keys,two=keyval.shape
    head=two//2; heads=queries.shape[1]//head; count=queries.shape[0]//seqs
    return pl.pallas_call(
        functools.partial(attend_kernel,rows,heads,head),
        grid_spec=pltpu.PrefetchScalarGridSpec(
            num_scalar_prefetch=1, grid=(seqs,),
            in_specs=[pl.BlockSpec((1,1,count),lambda i,*_:(i,0,0)),
                      pl.BlockSpec((count,heads*head),lambda i,*_:(i,0)),
                      pl.BlockSpec((1,keys,two),lambda i,*_:(i,0,0))],
            out_specs=[pl.BlockSpec((count,heads*head),lambda i,*_:(i,0)),
                       pl.BlockSpec((1,heads,count),lambda i,*_:(i,0,0))],
            scratch_shapes=[pltpu.VMEM((2,keys,count),F32),pltpu.VMEM((2,keys,count),BF16)]),
        out_shape=[jax.ShapeDtypeStruct(queries.shape,BF16),jax.ShapeDtypeStruct((seqs,heads,count),F32)],
        compiler_params=pltpu.CompilerParams(vmem_limit_bytes=40*2**20),
        cost_estimate=pl.CostEstimate(flops=4*queries.shape[0]*heads*head*keys,bytes_accessed=4*queries.size+2*keyval.size,transcendentals=queries.shape[0]*heads*keys),
    )(bases,limits,queries,keyval)

def attend_grad_kernel(
    rows, heads, head, base_ref, limit_ref, query_ref, grad_ref, log_ref, keyval_ref,
    dq_ref, dkv_ref, prob_ref, score_ref, exact_ref, slope_ref,
):
    keys = keyval_ref.shape[1]
    queries = query_ref.shape[0]
    blocks = keys // rows
    scale = head**-0.5
    limit = limit_ref[0]
    offset = lax.broadcasted_iota(jnp.int32, (rows, queries), 0)
    keys_t = keyval_ref[0, :, :head].T
    for h in range(heads):
        cols = slice(h * head, (h + 1) * head)
        lanes = slice(h * queries, (h + 1) * queries)
        query = query_ref[:, cols]
        grad = grad_ref[:, cols]
        log = log_ref[0, h : h + 1, :]

        def first(b, weighted):
            at = pl.ds(pl.multiple_of(b * rows, rows), rows)
            s = dot_nt(keyval_ref[0, at, :head], query) * (scale * LOG2E) - log
            s = jnp.where(offset <= limit - base_ref[b], s, NEGATIVE)
            p = jnp.exp2(s)
            dp = dot_nt(keyval_ref[0, at, head:], grad)
            prob_ref[at, lanes] = p.astype(BF16)
            exact_ref[h % 2, at, :] = p
            slope_ref[h % 2, at, :] = dp
            return weighted + jnp.sum((p * dp).reshape(rows // 8, 8, queries), 0)

        weighted = jnp.zeros((8, queries), F32)
        weighted = lax.fori_loop(0, blocks, first, weighted, unroll=4)
        weighted = jnp.sum(weighted, 0, keepdims=True)

        def second(b, carry):
            at = pl.ds(pl.multiple_of(b * rows, rows), rows)
            term = exact_ref[h % 2, at, :] * ((slope_ref[h % 2, at, :] - weighted) * scale)
            score_ref[at, lanes] = term.astype(BF16)
            return carry

        lax.fori_loop(0, blocks, second, 0, unroll=4)
        dq_ref[:, cols] = dot_nn(keys_t, score_ref[:, lanes]).T.astype(BF16)
    stacked_q = jnp.concatenate(
        [query_ref[:, h * head : (h + 1) * head] for h in range(heads)], 0
    )
    stacked_g = jnp.concatenate([grad_ref[:, h * head : (h + 1) * head] for h in range(heads)], 0)
    dkv_ref[0, :, :head] = dot_nn(score_ref[...], stacked_q).astype(BF16)
    dkv_ref[0, :, head:] = dot_nn(prob_ref[...], stacked_g).astype(BF16)


def attend_backward(queries, grad, logs, keyval, limits, bases, rows):
    seqs,keys,two=keyval.shape
    head=two//2; heads=queries.shape[1]//head; count=queries.shape[0]//seqs
    q_spec=pl.BlockSpec((count,heads*head),lambda i,*_:(i,0))
    return pl.pallas_call(
        functools.partial(attend_grad_kernel,rows,heads,head),
        grid_spec=pltpu.PrefetchScalarGridSpec(
            num_scalar_prefetch=1, grid=(seqs,),
            in_specs=[pl.BlockSpec((1,1,count),lambda i,*_:(i,0,0)),q_spec,q_spec,
                      pl.BlockSpec((1,heads,count),lambda i,*_:(i,0,0)),
                      pl.BlockSpec((1,keys,two),lambda i,*_:(i,0,0))],
            out_specs=[q_spec,pl.BlockSpec((1,keys,two),lambda i,*_:(i,0,0))],
            scratch_shapes=[pltpu.VMEM((keys,heads*count),BF16),pltpu.VMEM((keys,heads*count),BF16),pltpu.VMEM((2,keys,count),F32),pltpu.VMEM((2,keys,count),F32)]),
        out_shape=[jax.ShapeDtypeStruct(queries.shape,BF16),jax.ShapeDtypeStruct(keyval.shape,BF16)],
        compiler_params=pltpu.CompilerParams(vmem_limit_bytes=40*2**20),
        cost_estimate=pl.CostEstimate(flops=10*queries.shape[0]*heads*head*keys,bytes_accessed=8*queries.size+4*keyval.size,transcendentals=queries.shape[0]*heads*keys),
    )(bases,limits,queries,grad,logs,keyval)


def gather_keyval(block):
    even, odd = gather_dp(block)
    mine = jnp.concatenate([even, odd], 0)
    parts = [mine] + [swap_quad(mine, k) for k in range(1, quad_size())]
    return jnp.stack(parts).reshape(lax.axis_size("section"), -1, block.shape[-1]), even


def scatter_keyval(partial, rows):
    count = lax.axis_size("dp")
    blocks = partial.reshape(quad_size(), count * rows, partial.shape[-1])
    total = blocks[0]
    for k in range(1, quad_size()):
        total = total + swap_quad(blocks[k].astype(BF16), k).astype(F32)
    halves = total.reshape(2, count // 2, rows, partial.shape[-1])
    return scatter_dp(halves[0], halves[1])


def send_chips(block, pairs):
    return lax.ppermute(block, "dp", [(2 * a + c, 2 * b + c) for a, b in pairs for c in (0, 1)])


def gather_chips(block):
    chips = lax.axis_size("dp") // 2
    if chips != 4:
        return [block] + [swap_dp(block, 2 * j) for j in range(1, chips)]
    two = send_chips(block, [(0, 2), (2, 0), (1, 3), (3, 1)])
    one = send_chips(block, [(0, 1), (1, 0), (2, 3), (3, 2)])
    three = send_chips(block, [(1, 2), (2, 1)])
    return [block, one, two, three + send_chips(two, [(2, 3), (1, 0)])]


def gather_cores(far):
    count = lax.axis_size("dp")
    place = lax.axis_index("dp")
    near = swap_dp(jnp.stack(far), 1)
    whole = jnp.zeros((count,) + far[0].shape, far[0].dtype)
    for j in range(count // 2):
        whole = lax.dynamic_update_slice_in_dim(whole, far[j][None], place ^ (2 * j), 0)
        whole = lax.dynamic_update_slice_in_dim(whole, near[j][None], place ^ (2 * j + 1), 0)
    return whole.reshape((-1,) + far[0].shape[1:])


def scatter_mat(partial):
    chips = lax.axis_size("dp") // 2
    place = lax.axis_index("dp")
    core, chip = place % 2, place // 2
    pairs = partial.reshape(chips, 2, -1, partial.shape[1])
    kept = lax.dynamic_index_in_dim(pairs, core, 1, keepdims=False).astype(F32)
    given = lax.dynamic_index_in_dim(pairs, 1 - core, 1, keepdims=False)
    kept = (kept + swap_dp(given, 1).astype(F32)).astype(BF16)

    def piece(j):
        return lax.dynamic_index_in_dim(kept, chip ^ j, 0, keepdims=False)

    total = piece(0).astype(F32)
    if chips != 4:
        for j in range(1, chips):
            total = total + swap_dp(piece(j), 2 * j).astype(F32)
        return total
    passed = send_chips(piece(3), [(0, 1), (3, 2)])
    one = send_chips(piece(1), [(0, 1), (1, 0), (2, 3), (3, 2)])
    three = send_chips(piece(3), [(1, 2), (2, 1)])
    two = (piece(2).astype(F32) + passed.astype(F32)).astype(BF16)
    two = send_chips(two, [(0, 2), (2, 0), (1, 3), (3, 1)])
    return total + one.astype(F32) + two.astype(F32) + three.astype(F32)


def after(value, *done):
    held = lax.optimization_barrier((value,) + done)
    return held[0], held[1:]


def attend_part(inputs, pair, keyval_mat, norms, limits, bases):
    rows = inputs.shape[0]
    normed = layer_norm(inputs, norms[0], norms[1]).astype(BF16)
    keyval, passed = gather_keyval(dot_nn(normed, keyval_mat).astype(BF16))
    normed_all = spread(normed)
    queries = dot_nn(normed_all, pair[0]).astype(BF16)
    attended, logs = attend_forward(queries, keyval, limits, bases, rows)
    middle = inputs + collect(dot_nt(attended, pair[1]).astype(BF16))
    return middle, (normed_all, keyval, queries, logs, attended), passed


def mix_part(middle, norms):
    return spread(layer_norm(middle, norms[2], norms[3]).astype(BF16))


def hidden_part(mixed_all, hidden_mat):
    hidden_pre = dot_nn(mixed_all, hidden_mat)
    return hidden_pre, gelu_tanh(hidden_pre).astype(BF16)


def scatter_rows(partial):
    return lax.psum_scatter(partial, "dp", scatter_dimension=0, tiled=True)


def scatter_columns(partial):
    return lax.psum_scatter(partial, "dp", scatter_dimension=1, tiled=True)


def layer_backward(inputs, grad_out, weights, limits, bases, saved, early, late):
    pair, keyval_mat, hidden_mat, project_mat, norms = weights
    normed_all, keyval, queries, logs, attended, middle, mixed_all, hidden_pre, hidden_act = saved
    rows = inputs.shape[0]
    grad_branch = spread(grad_out.astype(BF16))
    grad_act = dot_nt(grad_branch, project_mat)
    grad_pre = jax.vjp(gelu_tanh, hidden_pre)[1](grad_act)[0].astype(BF16)
    hidden_act, _ = after(hidden_act, *early)
    mixed_all, _ = after(mixed_all, *early)
    grad_project = dot_tn(hidden_act, grad_branch).astype(BF16)
    sum_project = scatter_columns(grad_project)
    grad_hidden = dot_tn(mixed_all, grad_pre).astype(BF16)
    sum_hidden = scatter_rows(grad_hidden)
    grad_mixed = collect(dot_nt(grad_pre, hidden_mat).astype(BF16))
    if not early:
        grad_mixed, _ = after(grad_mixed, grad_project, grad_hidden)
    pull = jax.vjp(layer_norm, middle, norms[2], norms[3])[1]
    grad_mid, grad_gain_two, grad_bias_two = pull(grad_mixed)
    grad_middle = grad_out + grad_mid
    grad_rows = spread(grad_middle.astype(BF16))
    grad_attended = dot_nt(grad_rows, pair[1].T).astype(BF16)
    grad_output = dot_tn(grad_rows, attended).astype(BF16)
    held = (grad_output, grad_project, grad_hidden) + late if early else (grad_output,)
    grad_attended, (grad_output, *_) = after(grad_attended, *held)
    grad_queries, grad_kv = attend_backward(
        queries, grad_attended, logs, keyval, limits, bases, rows
    )
    grad_normed = collect(dot_nt(grad_queries, pair[0]).astype(BF16))
    grad_query = dot_tn(normed_all, grad_queries).astype(BF16)
    grad_normed, (grad_query,) = after(grad_normed, grad_query)
    grad_pair = jnp.concatenate([grad_query, grad_output], 1)
    grad_keyval = scatter_keyval(grad_kv, rows).astype(BF16)
    grad_normed = grad_normed + dot_nt(grad_keyval, keyval_mat)
    pull = jax.vjp(layer_norm, inputs, norms[0], norms[1])[1]
    grad_in, grad_gain_one, grad_bias_one = pull(grad_normed)
    table = jnp.stack([grad_gain_one, grad_bias_one, grad_gain_two, grad_bias_two])

    grad_small = dot_tn(normed_all, spread(grad_keyval)).astype(BF16)
    count, tensors = lax.axis_size("dp"), lax.axis_size("tensor")
    grad_small = grad_small.reshape(count, tensors, 2, -1, grad_small.shape[1])
    grad_small = lax.dynamic_index_in_dim(grad_small, lax.axis_index("tensor"), 1, keepdims=False)
    grad_small = lax.dynamic_index_in_dim(grad_small, lax.axis_index("section"), 1, keepdims=False)
    sum_small = scatter_mat(grad_small.reshape(-1, grad_small.shape[-1]))
    return grad_middle + grad_in, (sum_small, sum_hidden, sum_project), grad_pair, table


def local(ends_in, pieces, w_query, w_keyval, w_output, w_hidden, w_project, norm_params):
    section = lax.axis_index("section")
    tensor = lax.axis_index("tensor")
    place = lax.axis_index("dp")
    first = section == 0
    count, tensors = lax.axis_size("dp"), lax.axis_size("tensor")
    rows, width = ends_in.shape[2:]

    given = lax.dynamic_index_in_dim(ends_in[0], 1 - section, 0, keepdims=False)
    kept = lax.dynamic_index_in_dim(ends_in[0], section, 0, keepdims=False)
    taken = lax.ppermute(given, "section", [(0, 1), (1, 0)])
    inputs = jnp.where(first, kept, taken).astype(F32)
    cotangent = jnp.where(first, taken, kept).astype(F32)

    depth = w_keyval.shape[1]
    columns = w_keyval.shape[2]
    table = jnp.pad(norm_params[0].reshape(-1), (0, 16 * columns - 4 * depth))
    small, _ = gather_all(jnp.concatenate([w_keyval[0], table.reshape(16, columns)], 0))
    keyval_mats = small[..., :depth, :].reshape(2, width, columns)
    norms = small[..., depth:, :].reshape(2, count * tensors, 16 * columns)
    norms = norms[..., : 4 * depth].reshape(2, count * tensors, 4, depth)
    norms = jnp.swapaxes(norms, 1, 2).reshape(2, 4, width).astype(F32)

    def quarter(array, cut, index):
        size = array.shape[cut] // 2
        return lax.dynamic_slice_in_dim(array, index * size, size, cut)

    row = jnp.arange(rows, dtype=jnp.int32)
    turn = tensor ^ jnp.arange(tensors, dtype=jnp.int32)
    query_pos = ((place * tensors + turn)[:, None] * rows + row).reshape(-1)
    order = jnp.concatenate([jnp.arange(0, count, 2), jnp.arange(1, count, 2)]).astype(jnp.int32)
    bases = (((place ^ order)[None, :] * tensors + turn[:, None]) * rows).reshape(-1)
    limits = []
    for k in range(2):
        starts = lax.dynamic_index_in_dim(pieces, section ^ k, 0, keepdims=False)[:, None]
        inside = (query_pos >= starts) & (query_pos < starts + SPAN)
        limits.append(jnp.max(jnp.where(inside, starts + SPAN - 1, query_pos), 0))
    limits = jnp.stack(limits)[:, None]

    def both(pick):
        kept = pick(section)
        moved = lax.ppermute(pick(1 - section), "section", [(0, 1), (1, 0)])
        return jnp.where(first, kept, moved), jnp.where(first, moved, kept)

    output_turned = w_output[0].T
    query_both = both(
        lambda k: jnp.concatenate([quarter(w_query[0], 1, k), quarter(output_turned, 1, k)], 1)
    )
    hidden_shard, project_shard = w_hidden[0], w_project[0]
    hidden_both = both(lambda k: quarter(hidden_shard, 1, k))
    project_both = both(lambda k: quarter(project_shard, 0, k))
    def rows_of(array):
        return lax.all_gather(array, "dp", axis=0, tiled=True)

    def columns_of(array):
        return lax.all_gather(array, "dp", axis=1, tiled=True)

    pair_one = jnp.split(rows_of(query_both[0]), 2, axis=1)
    pair_two = jnp.split(rows_of(query_both[1]), 2, axis=1)
    hidden_both, _ = after(hidden_both, norms)

    middle_one, saved_one, passed = attend_part(
        inputs, pair_one, keyval_mats[0], norms[0], limits, bases
    )
    project_both, _ = after(project_both, passed)
    project_one, project_two = (columns_of(p) for p in project_both)
    hidden_two = rows_of(hidden_both[1])
    hidden_one = rows_of(hidden_both[0])
    mixed_one = mix_part(middle_one, norms[0])
    pre_one, act_one = hidden_part(mixed_one, hidden_one)
    between = middle_one + collect(dot_nn(act_one, project_one).astype(BF16))
    between = between.astype(BF16).astype(F32)

    middle_two, saved_two, _ = attend_part(between, pair_two, keyval_mats[1], norms[1], limits, bases)
    mixed_two = mix_part(middle_two, norms[1])
    cotangent, _ = after(cotangent, mixed_two)
    pre_two, act_two = hidden_part(mixed_two, hidden_two)
    outputs = middle_two + collect(dot_nn(act_two, project_two).astype(BF16))

    grad_between, sums_two, grad_pair, table_two = layer_backward(
        between,
        cotangent,
        (pair_two, keyval_mats[1], hidden_two, project_two, norms[1]),
        limits,
        bases,
        saved_two + (middle_two, mixed_two, pre_two, act_two),
        (),
        (),
    )
    grad_between = grad_between.astype(BF16)
    grad_pair, _ = after(grad_pair, grad_between)
    sum_pair_two = scatter_rows(grad_pair)
    grad_between = grad_between.astype(F32)
    grad_inputs, sums_one, grad_pair, table_one = layer_backward(
        inputs,
        grad_between,
        (pair_one, keyval_mats[0], hidden_one, project_one, norms[0]),
        limits,
        bases,
        saved_one + (middle_one, mixed_one, pre_one, act_one),
        sums_two[1:],
        (),
    )
    sum_pair_one = scatter_rows(after(grad_pair, *sums_one[1:])[0])
    halves_two = jnp.split(sum_pair_two, 2, axis=1)
    halves_one = jnp.split(sum_pair_one, 2, axis=1)
    sums_two = (halves_two[0], sums_two[0], halves_two[1]) + sums_two[1:]
    sums_one = (halves_one[0], sums_one[0], halves_one[1]) + sums_one[1:]

    results = []
    for index, cut in enumerate((1, 0, 1, 1, 0)):
        halves = []
        for layer, sums in ((1, sums_two), (0, sums_one)):
            own = sums[index].astype(BF16)
            moved = lax.ppermute(own, "section", [(1 - layer, layer)])
            pair = (own, moved) if layer == 0 else (moved, own)
            halves.append(jnp.concatenate(pair, cut))
        results.append(jnp.where(first, halves[1], halves[0]).astype(F32)[None])

    tables = jnp.stack([table_one, table_two]).reshape(2, 4, count, tensors, depth)
    table_result = scatter_all(jnp.moveaxis(tables, 1, 3), F32)

    given = jnp.where(first, outputs, grad_inputs).astype(BF16)
    kept = jnp.where(first, grad_inputs, outputs)
    taken = lax.ppermute(given, "section", [(0, 1), (1, 0)]).astype(F32)
    ends_out = jnp.where(first, jnp.stack([kept, taken]), jnp.stack([taken, kept]))
    return (
        ends_out[None],
        results[0],
        results[1],
        jnp.swapaxes(results[2], 1, 2),
        results[3],
        results[4],
        table_result[None, :3],
        table_result[None, 3],
    )


def solution(mesh):
    placed = (
        P("section", None, ("dp", "tensor"), None),
        P(),
        P("section", "dp", "tensor"),
        P("section", ("dp", "tensor"), None),
        P("section", "tensor", "dp"),
        P("section", "dp", "tensor"),
        P("section", "tensor", "dp"),
        P("section", None, ("dp", "tensor")),
    )
    return jax.shard_map(
        local,
        mesh=mesh,
        in_specs=placed,
        out_specs=(
            P("section", None, ("dp", "tensor"), None),
            P("section", "dp", "tensor"),
            P("section", ("dp", "tensor"), None),
            P("section", "tensor", "dp"),
            P("section", "dp", "tensor"),
            P("section", "tensor", "dp"),
            P("section", None, ("dp", "tensor")),
            P("section", ("dp", "tensor")),
        ),
        check_vma=False,
    )
```

time: 1220 us -> 1050 us (0.86)
  matrix products: 316 us -> 151 us
  Pallas kernels: 0 us -> 71.1 us
  waiting for transfers between devices: 574 us -> 547 us
  local copies, waits for them, and re-layouts: 62.8 us -> 37.1 us
    dot_general x12 -> x0, matrix products: 160 us -> none  [the longest x2 51 us: attend_backward(): jnp.einsum('shqk,sqhd->skd', grad_scores, four, preferred_element_type=F32)]
    pallas_call x0 -> x4, Pallas kernels: none -> 71.1 us  [the longest x2 41.4 us: attend_backward(): pl.pallas_call(functools.partial(attend_grad_kernel, rows, heads, head),...]
    ppermute x28 -> x26, waiting for transfers between devices: 43.5 us -> 17.2 us  [swap_dp(): lax.ppermute(block, 'dp', [(i, i ^ offset) for i in range(lax.axis_size('...]
    ppermute x8 -> x11, waiting for transfers between devices: 51.7 us -> 28.4 us  [the longest x3 25.2 us: both(): moved = lax.ppermute(pick(1 - section), 'section', [(0, 1), (1, 0)])]
    select_n x9 -> x6, other arithmetic: 23.8 us -> 9.35 us  [the longest x3 7.35 us: both(): return (jnp.where(first, kept, moved), jnp.where(first, moved, kept))]
    dynamic_update_slice x32 -> x8, local copies, waits for them, and re-layouts: 12.9 us -> 0.21 us  [gather_all(): lax.dynamic_update_slice_in_dim(whole, parts[:, :, j:j + 1], me_d ^ j, 2)]
    ppermute x8 -> x11, starting transfers between devices: 25.6 us -> 17.6 us  [the longest x8 12.7 us: send_chips(): lax.ppermute(block, 'dp', [(2 * a + c, 2 * b + c) for a, b in pairs for c...]
    ppermute x28 -> x26, starting transfers between devices: 31.7 us -> 24.1 us  [swap_dp(): lax.ppermute(block, 'dp', [(i, i ^ offset) for i in range(lax.axis_size('...]
  transfers between devices with their start and end apart: 131 -> 133, of which waited for: 72 -> 59; matrix products, arithmetic and copies ran while one was open for 36% -> 22% of each run, Pallas kernels for 0% -> 7%
where the time goes in v2:
time: 1050 us; the launch traced here: 1040 us
  waiting for transfers between devices  547 us (52%)
  starting transfers between devices  156 us (15%)
  matrix products  151 us (14%)
  Pallas kernels  71.1 us (7%)
  other arithmetic  66.1 us (6%)
  local copies, waits for them, and re-layouts  37.1 us (4%)
  between operations  16.8 us (2%)
    ppermute x72, waiting for transfers between devices, swap_quad(): lax.ppermute(block, ('section', 'tensor'), [(i, i ^ offset) for i in rang...  391 us
    dot_general x30, matrix products, dot(): lax.dot_general(left, right, ((dims[0], dims[1]), ((), ())), preferred_el...  151 us
    ppermute x72, starting transfers between devices, swap_quad(): lax.ppermute(block, ('section', 'tensor'), [(i, i ^ offset) for i in rang...  88.4 us
    pallas_call x2, Pallas kernels, attend_backward(): pl.pallas_call(functools.partial(attend_grad_kernel, rows, heads, head),...  41.4 us
    reduce_scatter x4, waiting for transfers between devices, scatter_rows(): return lax.psum_scatter(partial, 'dp', scatter_dimension=0, tiled=True)  33.1 us
    reduce_scatter x2, waiting for transfers between devices, scatter_columns(): return lax.psum_scatter(partial, 'dp', scatter_dimension=1, tiled=True)  31 us
    pallas_call x2, Pallas kernels, attend_forward(): pl.pallas_call(functools.partial(attend_kernel, rows, heads, head), grid_...  29.8 us
    ppermute x10, waiting for transfers between devices, local(): moved = lax.ppermute(own, 'section', [(1 - layer, layer)])  29 us
  transfers between devices with their start and end apart: 133, of which 59 were waited for; matrix products, arithmetic and copies ran while one was open for 22% of the time, Pallas kernels for 7%

profile of v2, /device:TPU:0, one launch (start us, length us, event | category | flops | bytes accessed | tf_op | source)
XLA Modules:
  0.0 1045.0 jit_solution(8142154306623273617)
XLA Ops:
  13.5 12.0 %collective-permute-done.11 = bf16[256,1024]{1,0:T(8,128)(2,1)S(1)} collective-permute-done((bf16[256,1024]{1,0:T(8,128)(2,1)}, bf16[256,1024]{1,0:T(8,128)(2,1)S(1)}, u32[]{:S(2)}, u32[]{:S(2)}) %collective-permute-start.11) | collective-permute-done | bytes 524320 | tf_op jit(solution)/shard_map/ppermute | solution.py:430
  34.2 3.4 collective-permute-done.3
  42.4 34.7 %collective-permute-done.6 = bf16[8,144,256]{2,1,0:T(8,128)(2,1)S(1)} collective-permute-done((bf16[8,144,256]{2,1,0:T(8,128)(2,1)S(1)}, bf16[8,144,256]{2,1,0:T(8,128)(2,1)S(1)}, u32[]{:S(2)}, u32[]{:S(2)}) %collective-permute-start.6) | collective-permute-done | bytes 589856 | tf_op jit(solution)/shard_map/ppermute | solution.py:25
  83.1 8.9 collective-permute-done.7
  101.7 10.9 %collective-permute-done = bf16[128,2048]{1,0:T(8,128)(2,1)} collective-permute-done((bf16[128,2048]{1,0:T(8,128)(2,1)}, bf16[128,2048]{1,0:T(8,128)(2,1)}, u32[]{:S(2)}, u32[]{:S(2)}) %collective-permute-start) | collective-permute-done | bytes 524320 | tf_op jit(solution)/shard_map/ppermute | solution.py:399
  116.3 3.2 collective-permute-start.12
  119.6 13.2 %collective-permute-done.26 = bf16[2048,256]{1,0:T(8,128)(2,1)} collective-permute-done((bf16[2048,256]{1,0:T(8,128)(2,1)}, bf16[2048,256]{1,0:T(8,128)(2,1)}, u32[]{:S(2)}, u32[]{:S(2)}) %collective-permute-start.26) | collective-permute-done | bytes 1048608 | tf_op jit(solution)/shard_map/ppermute | solution.py:430
  145.5 9.1 collective-permute-done.18
  156.4 9.5 collective-permute-done.17
  168.5 8.7 collective-permute-done.10
  177.2 10.5 %collective-permute-done.9 = bf16[128,2048]{1,0:T(8,128)(2,1)} collective-permute-done((bf16[128,2048]{1,0:T(8,128)(2,1)S(1)}, bf16[128,2048]{1,0:T(8,128)(2,1)}, u32[]{:S(2)}, u32[]{:S(2)}) %collective-permute-start.9) | collective-permute-done | bytes 524320 | tf_op jit(solution)/shard_map/ppermute | solution.py:25
  187.7 3.3 fusion.36.query_ref
  191.1 14.7 %shard_map.143 = (bf16[512,512]{1,0:T(8,128)(2,1)S(1)}, f32[2,4,256]{2,1,0:T(4,128)S(1)}) custom-call(s32[16]{0:T(128)S(1)} %mul.381.base_ref, s32[2,1,256]{2,1,0:T(1,128)S(1)} %broadcast_in_dim.40.limit_ref, bf16[512,512]{1,0:T(8,128)(2,1)S(1)} %fusion.36.query_ref, bf16[2,2048,256]{2,1,0:T(8,128)(2,1)S(1)} %bitcast.328), custom_call_target="tpu_custom_call" | custom-call | flops 2147483648 | bytes 3145728 | tf_op jit(solution)/shard_map/pallas_call | solution.py:160
  212.7 21.3 %collective-permute-done.19 = bf16[128,2048]{1,0:T(8,128)(2,1)S(1)} collective-permute-done((bf16[128,2048]{1,0:T(8,128)(2,1)}, bf16[128,2048]{1,0:T(8,128)(2,1)S(1)}, u32[]{:S(2)}, u32[]{:S(2)}) %collective-permute-start.19) | collective-permute-done | bytes 524320 | tf_op jit(solution)/shard_map/ppermute | solution.py:25
  242.0 12.3 %collective-permute-done.24 = bf16[128,2048]{1,0:T(8,128)(2,1)S(1)} collective-permute-done((bf16[128,2048]{1,0:T(8,128)(2,1)S(1)}, bf16[128,2048]{1,0:T(8,128)(2,1)S(1)}, u32[]{:S(2)}, u32[]{:S(2)}) %collective-permute-start.24) | collective-permute-done | bytes 524320 | tf_op jit(solution)/shard_map/ppermute | solution.py:25
  254.3 9.5 collective-permute-done.23
  264.7 12.0 %multiply_convert_fusion.1 = (bf16[512,2048]{1,0:T(8,128)(2,1)}, f32[512,2048]{1,0:T(8,128)}) fusion(bf16[2048,2048]{1,0:T(8,128)(2,1)} %all-gather.9.cloned.1.call-done, bf16[128,2048]{1,0:T(8,128)(2,1)} %copy-done.47, bf16[128,2048]{1,0:T(8,128)(2,1)} %copy-done.49, bf16[128,2048]{1,0:T(8,128)(2,1)} %collective-permute-done.22, ...), kind=kOutput, calls=%fused_computation.25 | convolution fusion | flops 4312793088 | bytes 16777216 | tf_op jit(solution)/shard_map/dot_general | solution.py:20
  276.7 8.6 convolution_convert_fusion.14
  289.0 20.7 %collective-permute-done.27 = bf16[128,2048]{1,0:T(8,128)(2,1)S(1)} collective-permute-done((bf16[128,2048]{1,0:T(8,128)(2,1)S(1)}, bf16[128,2048]{1,0:T(8,128)(2,1)S(1)}, u32[]{:S(2)}, u32[]{:S(2)}) %collective-permute-start.27) | collective-permute-done | bytes 524320 | tf_op jit(solution)/shard_map/ppermute | solution.py:25
  326.9 6.4 collective-permute-done.32
  335.8 9.1 collective-permute-done.31
  344.9 3.4 fusion.42.query_ref
  348.3 7.7 collective-permute-done.39
  356.0 8.6 collective-permute-done.38
  366.4 15.1 %shard_map.144 = (bf16[512,512]{1,0:T(8,128)(2,1)S(1)}, f32[2,4,256]{2,1,0:T(4,128)S(1)}) custom-call(s32[16]{0:T(128)S(1)} %mul.381.base_ref, s32[2,1,256]{2,1,0:T(1,128)S(1)} %broadcast_in_dim.40.limit_ref, bf16[512,512]{1,0:T(8,128)(2,1)S(1)} %fusion.42.query_ref, bf16[2,2048,256]{2,1,0:T(8,128)(2,1)S(1)} %bitcast.330), custom_call_target="tpu_custom_call" | custom-call | flops 2147483648 | bytes 3145728 | tf_op jit(solution)/shard_map/pallas_call | solution.py:160
  386.5 21.3 %collective-permute-done.40 = bf16[128,2048]{1,0:T(8,128)(2,1)S(1)} collective-permute-done((bf16[128,2048]{1,0:T(8,128)(2,1)S(1)}, bf16[128,2048]{1,0:T(8,128)(2,1)S(1)}, u32[]{:S(2)}, u32[]{:S(2)}) %collective-permute-start.40) | collective-permute-done | bytes 524320 | tf_op jit(solution)/shard_map/ppermute | solution.py:25
  414.8 11.1 %collective-permute-done.45 = bf16[128,2048]{1,0:T(8,128)(2,1)S(1)} collective-permute-done((bf16[128,2048]{1,0:T(8,128)(2,1)S(1)}, bf16[128,2048]{1,0:T(8,128)(2,1)S(1)}, u32[]{:S(2)}, u32[]{:S(2)}) %collective-permute-start.45) | collective-permute-done | bytes 524320 | tf_op jit(solution)/shard_map/ppermute | solution.py:25
  425.9 9.4 collective-permute-done.44
  441.5 11.2 %multiply_convert_fusion = (bf16[512,2048]{1,0:T(8,128)(2,1)S(1)}, f32[512,2048]{1,0:T(8,128)}) fusion(bf16[2048,2048]{1,0:T(8,128)(2,1)} %all-gather.17.cloned.1.call-done, bf16[128,2048]{1,0:T(8,128)(2,1)} %copy-done.54, bf16[128,2048]{1,0:T(8,128)(2,1)} %copy-done.55, bf16[128,2048]{1,0:T(8,128)(2,1)} %copy-done.56, bf16[128,2048]{1,0:T(8,128)(2,1)} %copy-done.41), kind=kOutput, calls=%fused_computation.24 | convolution fusion | flops 4312793088 | bytes 16777216 | tf_op jit(solution)/shard_map/dot_general | solution.py:20
  454.1 10.2 collective-permute-done.47
  464.3 8.3 convolution_convert_fusion.3
  472.7 5.6 all-gather.15.cloned.1.call-done
  478.3 12.1 %fusion.13 = bf16[512,2048]{1,0:T(8,128)(2,1)S(1)} fusion(f32[512,2048]{1,0:T(8,128)} %get-tuple-element.224, bf16[2048,2048]{1,0:T(8,128)(2,1)} %all-gather.15.cloned.1.call-done, bf16[128,2048]{1,0:T(8,128)(2,1)} %collective-permute-done.48, bf16[128,2048]{1,0:T(8,128)(2,1)} %collective-permute-done.47, bf16[128,2048]{1,0:T(8,128)(2,1)} %collective-permute-done.46, ...), kind=kOutput, calls=%fused_computation.21 | convolution fusion | flops 4324327424 | bytes 16777216 | tf_op jit(solution)/shard_map/dot_general | solution.py:20
  491.8 6.8 convolution_convert_fusion.2
  498.6 8.6 convolution_convert_fusion.12
  511.0 21.9 %collective-permute-done.49 = bf16[128,2048]{1,0:T(8,128)(2,1)S(1)} collective-permute-done((bf16[128,2048]{1,0:T(8,128)(2,1)S(1)}, bf16[128,2048]{1,0:T(8,128)(2,1)S(1)}, u32[]{:S(2)}, u32[]{:S(2)}) %collective-permute-start.49) | collective-permute-done | bytes 524320 | tf_op jit(solution)/shard_map/ppermute | solution.py:25
  539.6 12.3 %collective-permute-done.54 = bf16[128,2048]{1,0:T(8,128)(2,1)S(1)} collective-permute-done((bf16[128,2048]{1,0:T(8,128)(2,1)S(1)}, bf16[128,2048]{1,0:T(8,128)(2,1)S(1)}, u32[]{:S(2)}, u32[]{:S(2)}) %collective-permute-start.54) | collective-permute-done | bytes 524320 | tf_op jit(solution)/shard_map/ppermute | solution.py:25
  551.9 9.5 collective-permute-done.53
  565.6 20.8 %shard_map.145 = (bf16[512,512]{1,0:T(8,128)(2,1)S(1)}, bf16[2,2048,256]{2,1,0:T(8,128)(2,1)S(1)}) custom-call(s32[16]{0:T(128)S(1)} %mul.381.base_ref, s32[2,1,256]{2,1,0:T(1,128)S(1)} %broadcast_in_dim.40.limit_ref, bf16[512,512]{1,0:T(8,128)(2,1)S(1)} %fusion.42.query_ref, bf16[512,512]{1,0:T(8,128)(2,1)S(1)} %fusion.45.grad_ref, ...), custom_call_target="tpu_custom_call" | custom-call | flops 5368709120 | bytes 6291456 | tf_op jit(solution)/shard_map/pallas_call | solution.py:228
  594.6 18.0 %collective-permute-done.58 = bf16[1024,256]{1,0:T(8,128)(2,1)S(1)} collective-permute-done((bf16[1024,256]{1,0:T(8,128)(2,1)S(1)}, bf16[1024,256]{1,0:T(8,128)(2,1)S(1)}, u32[]{:S(2)}, u32[]{:S(2)}) %collective-permute-start.58) | collective-permute-done | bytes 524320 | tf_op jit(solution)/shard_map/ppermute | solution.py:25
  614.5 4.0 convolution_convert_fusion.9
  620.8 13.4 %collective-permute-done.55 = bf16[128,2048]{1,0:T(8,128)(2,1)S(1)} collective-permute-done((bf16[128,2048]{1,0:T(8,128)(2,1)S(1)}, bf16[128,2048]{1,0:T(8,128)(2,1)S(1)}, u32[]{:S(2)}, u32[]{:S(2)}) %collective-permute-start.55) | collective-permute-done | bytes 524320 | tf_op jit(solution)/shard_map/ppermute | solution.py:25
  635.8 7.0 collective-permute-done.63
  651.5 9.7 collective-permute-done.67
  661.2 9.5 collective-permute-done.66
  671.8 11.4 %fusion.6 = bf16[512,2048]{1,0:T(8,128)(2,1)} fusion(f32[512,2048]{1,0:T(8,128)} %get-tuple-element.220, bf16[2048,2048]{1,0:T(8,128)(2,1)S(1)} %bitcast.431, bf16[128,2048]{1,0:T(8,128)(2,1)S(1)} %collective-permute-done.67, bf16[128,2048]{1,0:T(8,128)(2,1)S(1)} %collective-permute-done.66, bf16[128,2048]{1,0:T(8,128)(2,1)S(1)} %collective-permute-done.65, ...), kind=kOutput, calls=%fused_computation.14 | convolution fusion | flops 4324327424 | bytes 16777216 | tf_op jit(solution)/shard_map/dot_general | solution.py:20
  683.2 10.1 convolution_convert_fusion
  693.5 9.8 convolution_convert_fusion.1
  703.4 4.8 pad_maximum_fusion.1
  710.5 8.7 convolution_convert_fusion.8
  726.5 22.7 %collective-permute-done.100 = bf16[128,256]{1,0:T(8,128)(2,1)S(1)} collective-permute-done((bf16[128,256]{1,0:T(8,128)(2,1)S(1)}, bf16[128,256]{1,0:T(8,128)(2,1)S(1)}, u32[]{:S(2)}, u32[]{:S(2)}) %collective-permute-start.100) | collective-permute-done | bytes 65568 | tf_op jit(solution)/shard_map/ppermute | solution.py:25
  765.1 7.7 collective-permute-done.73
  772.8 7.5 collective-permute-done.72
  787.3 20.6 %shard_map.146 = (bf16[512,512]{1,0:T(8,128)(2,1)S(1)}, bf16[2,2048,256]{2,1,0:T(8,128)(2,1)S(1)}) custom-call(s32[16]{0:T(128)S(1)} %mul.381.base_ref, s32[2,1,256]{2,1,0:T(1,128)S(1)} %broadcast_in_dim.40.limit_ref, bf16[512,512]{1,0:T(8,128)(2,1)S(1)} %copy-done.6, bf16[512,512]{1,0:T(8,128)(2,1)S(1)} %fusion.39.grad_ref, ...), custom_call_target="tpu_custom_call" | custom-call | flops 5368709120 | bytes 6291456 | tf_op jit(solution)/shard_map/pallas_call | solution.py:228
  817.2 18.2 %collective-permute-done.74 = bf16[128,2048]{1,0:T(8,128)(2,1)S(1)} collective-permute-done((bf16[128,2048]{1,0:T(8,128)(2,1)S(1)}, bf16[128,2048]{1,0:T(8,128)(2,1)S(1)}, u32[]{:S(2)}, u32[]{:S(2)}) %collective-permute-start.74) | collective-permute-done | bytes 524320 | tf_op jit(solution)/shard_map/ppermute | solution.py:25
  840.7 31.0 %reduce-scatter.13.cloned.1.call-done = bf16[2048,256]{1,0:T(8,128)(2,1)} async-done(((bf16[2048,2048]{1,0:T(8,128)(2,1)}), bf16[2048,256]{1,0:T(8,128)(2,1)}) %reduce-scatter.13.cloned.1.call-update) | async-done | bytes 1048592 | tf_op jit(solution)/shard_map/reduce_scatter | solution.py:340
  871.7 8.5 convolution_convert_fusion.4
  895.4 33.1 %reduce-scatter.17.cloned.1.call-done = bf16[256,1024]{1,0:T(8,128)(2,1)} async-done(((bf16[2048,1024]{1,0:T(8,128)(2,1)}), bf16[256,1024]{1,0:T(8,128)(2,1)}) %reduce-scatter.17.cloned.1.call-update) | async-done | bytes 524304 | tf_op jit(solution)/shard_map/reduce_scatter | solution.py:336
  952.9 3.9 collective-permute-start.95
  978.1 4.6 collective-permute-start.109
  987.7 10.3 collective-permute-done.111
  997.9 4.4 collective-permute-start.89
  1009.5 16.5 %collective-permute-done.113 = bf16[2048,256]{1,0:T(8,128)(2,1)S(1)} collective-permute-done((bf16[2048,256]{1,0:T(8,128)(2,1)}, bf16[2048,256]{1,0:T(8,128)(2,1)S(1)}, u32[]{:S(2)}, u32[]{:S(2)}) %collective-permute-start.113) | collective-permute-done | bytes 1048608 | tf_op jit(solution)/shard_map/ppermute | solution.py:503
  1027.4 4.3 fusion.15
  (607 shorter events, 282.5 us)
Async XLA Ops:
  7.2 180.5 %all-gather.7.cloned.1.call-start = ((), (), s32[]{:S(2)}) async-start(), calls=%async_computation.6 | async-start | bytes 4718592 | tf_op jit(solution)/shard_map/all_gather | solution.py:441
  26.8 237.9 %all-gather.9.cloned.1.call-start = ((), (), s32[]{:S(2)}) async-start(), calls=%async_computation.7 | async-start | bytes 9437184 | tf_op jit(solution)/shard_map/all_gather | solution.py:441
  38.7 41.3 %collective-permute-start.25 = (bf16[256,2048]{1,0:T(8,128)(2,1)}, bf16[256,2048]{1,0:T(8,128)(2,1)}, u32[]{:S(2)}, u32[]{:S(2)}) collective-permute-start(bf16[256,2048]{1,0:T(8,128)(2,1)} %dynamic-slice_bitcast_fusion.1), channel_id=1, source_target_pairs={{0,16},{16,0},{1,17},{17,1},{2,18},{18,2},{3,19},{19,3},{4,20},{20... | collective-permute-start | bytes 3145736 | tf_op jit(solution)/shard_map/ppermute | solution.py:430
  40.3 36.8 %collective-permute-start.6 = (bf16[8,144,256]{2,1,0:T(8,128)(2,1)S(1)}, bf16[8,144,256]{2,1,0:T(8,128)(2,1)S(1)}, u32[]{:S(2)}, u32[]{:S(2)}) collective-permute-start(bf16[8,144,256]{2,1,0:T(8,128)(2,1)S(1)} %bitcast.342), channel_id=1, source_target_pairs={{0,16},{1,17},{16,0},{17,1},{2,18},{3,19},{18,2},{19,3},{4,20},{5,... | collective-permute-start | bytes 1769480 | tf_op jit(solution)/shard_map/ppermute | solution.py:25
  40.9 37.8 %collective-permute-start.5 = (bf16[8,144,256]{2,1,0:T(8,128)(2,1)S(1)}, bf16[8,144,256]{2,1,0:T(8,128)(2,1)}, u32[]{:S(2)}, u32[]{:S(2)}) collective-permute-start(bf16[8,144,256]{2,1,0:T(8,128)(2,1)S(1)} %bitcast.343), channel_id=1, source_target_pairs={{0,1},{1,0},{16,17},{17,16},{2,3},{3,2},{18,19},{19,18},{4,5},{5,4... | collective-permute-start | bytes 1769480 | tf_op jit(solution)/shard_map/ppermute | solution.py:25
  96.5 180.3 %all-gather.11.cloned.1.call-start = ((), (), s32[]{:S(2)}) async-start(), calls=%async_computation.8 | async-start | bytes 9437184 | tf_op jit(solution)/shard_map/all_gather | solution.py:444
  101.1 31.7 %collective-permute-start.26 = (bf16[2048,256]{1,0:T(8,128)(2,1)}, bf16[2048,256]{1,0:T(8,128)(2,1)}, u32[]{:S(2)}, u32[]{:S(2)}) collective-permute-start(bf16[2048,256]{1,0:T(8,128)(2,1)} %dynamic-slice_bitcast_fusion), channel_id=1, source_target_pairs={{0,16},{16,0},{1,17},{17,1},{2,18},{18,2},{3,19},{19,3},{4,20},{20... | collective-permute-start | bytes 3145736 | tf_op jit(solution)/shard_map/ppermute | solution.py:430
  135.9 199.9 %all-gather.13.cloned.1.call-start = ((), (), s32[]{:S(2)}) async-start(), calls=%async_computation.9 | async-start | bytes 4718592 | tf_op jit(solution)/shard_map/all_gather | solution.py:441
  136.5 305.1 %all-gather.17.cloned.1.call-start = ((), (), s32[]{:S(2)}) async-start(), calls=%async_computation.11 | async-start | bytes 9437184 | tf_op jit(solution)/shard_map/all_gather | solution.py:441
  137.1 341.3 %all-gather.15.cloned.1.call-start = ((), (), s32[]{:S(2)}) async-start(), calls=%async_computation.10 | async-start | bytes 9437184 | tf_op jit(solution)/shard_map/all_gather | solution.py:444
  141.5 24.4 %collective-permute-start.17 = (bf16[8,128,256]{2,1,0:T(8,128)(2,1)S(1)}, bf16[8,128,256]{2,1,0:T(8,128)(2,1)S(1)}, u32[]{:S(2)}, u32[]{:S(2)}) collective-permute-start(bf16[8,128,256]{2,1,0:T(8,128)(2,1)S(1)} %constant_dynamic-update-slice_fusion), channel_id=1, source_target_pairs={{0,16},{1,17},{16,0},{17,1},{2,18},{3,19},{18,2},{19,3},{4,20},{5,... | collective-permute-start | bytes 1572872 | tf_op jit(solution)/shard_map/ppermute | solution.py:25
  142.0 23.9 %collective-permute-start.16 = (bf16[8,128,256]{2,1,0:T(8,128)(2,1)S(1)}, bf16[8,128,256]{2,1,0:T(8,128)(2,1)S(1)}, u32[]{:S(2)}, u32[]{:S(2)}) collective-permute-start(bf16[8,128,256]{2,1,0:T(8,128)(2,1)S(1)} %constant_dynamic-update-slice_fusion), channel_id=1, source_target_pairs={{0,1},{1,0},{16,17},{17,16},{2,3},{3,2},{18,19},{19,18},{4,5},{5,4... | collective-permute-start | bytes 1572872 | tf_op jit(solution)/shard_map/ppermute | solution.py:25
  142.5 34.7 %collective-permute-start.10 = (bf16[128,2048]{1,0:T(8,128)(2,1)S(1)}, bf16[128,2048]{1,0:T(8,128)(2,1)}, u32[]{:S(2)}, u32[]{:S(2)}) collective-permute-start(bf16[128,2048]{1,0:T(8,128)(2,1)S(1)} %fusion.56), channel_id=1, source_target_pairs={{0,17},{1,16},{16,1},{17,0},{2,19},{3,18},{18,3},{19,2},{4,21},{5,... | collective-permute-start | bytes 1572872 | tf_op jit(solution)/shard_map/ppermute | solution.py:25
  144.9 42.7 %collective-permute-start.9 = (bf16[128,2048]{1,0:T(8,128)(2,1)S(1)}, bf16[128,2048]{1,0:T(8,128)(2,1)}, u32[]{:S(2)}, u32[]{:S(2)}) collective-permute-start(bf16[128,2048]{1,0:T(8,128)(2,1)S(1)} %fusion.56), channel_id=1, source_target_pairs={{0,16},{1,17},{16,0},{17,1},{2,18},{3,19},{18,2},{19,3},{4,20},{5,... | collective-permute-start | bytes 1572872 | tf_op jit(solution)/shard_map/ppermute | solution.py:25
  154.6 33.1 %collective-permute-start.8 = (bf16[128,2048]{1,0:T(8,128)(2,1)S(1)}, bf16[128,2048]{1,0:T(8,128)(2,1)}, u32[]{:S(2)}, u32[]{:S(2)}) collective-permute-start(bf16[128,2048]{1,0:T(8,128)(2,1)S(1)} %fusion.56), channel_id=1, source_target_pairs={{0,1},{1,0},{16,17},{17,16},{2,3},{3,2},{18,19},{19,18},{4,5},{5,4... | collective-permute-start | bytes 1572872 | tf_op jit(solution)/shard_map/ppermute | solution.py:25
  208.9 25.1 %collective-permute-start.19 = (bf16[128,2048]{1,0:T(8,128)(2,1)}, bf16[128,2048]{1,0:T(8,128)(2,1)S(1)}, u32[]{:S(2)}, u32[]{:S(2)}) collective-permute-start(bf16[128,2048]{1,0:T(8,128)(2,1)} %get-tuple-element.166), channel_id=1, source_target_pairs={{0,1},{1,0},{16,17},{17,16},{2,3},{3,2},{18,19},{19,18},{4,5},{5,4... | collective-permute-start | bytes 1572872 | tf_op jit(solution)/shard_map/ppermute | solution.py:25
  210.3 23.8 %collective-permute-start.21 = (bf16[128,2048]{1,0:T(8,128)(2,1)}, bf16[128,2048]{1,0:T(8,128)(2,1)S(1)}, u32[]{:S(2)}, u32[]{:S(2)}) collective-permute-start(bf16[128,2048]{1,0:T(8,128)(2,1)} %get-tuple-element.167), channel_id=1, source_target_pairs={{0,17},{1,16},{16,1},{17,0},{2,19},{3,18},{18,3},{19,2},{4,21},{5,... | collective-permute-start | bytes 1572872 | tf_op jit(solution)/shard_map/ppermute | solution.py:25
  211.8 23.8 %collective-permute-start.20 = (bf16[128,2048]{1,0:T(8,128)(2,1)}, bf16[128,2048]{1,0:T(8,128)(2,1)}, u32[]{:S(2)}, u32[]{:S(2)}) collective-permute-start(bf16[128,2048]{1,0:T(8,128)(2,1)} %get-tuple-element.168), channel_id=1, source_target_pairs={{0,16},{1,17},{16,0},{17,1},{2,18},{3,19},{18,2},{19,3},{4,20},{5,... | collective-permute-start | bytes 1572872 | tf_op jit(solution)/shard_map/ppermute | solution.py:25
  212.4 470.8 %reduce-scatter.9.cloned.1.call-start = ((), (), s32[]{:S(2)}) async-start(), calls=%async_computation.13 | async-start | bytes 9437184 | tf_op jit(solution)/shard_map/reduce_scatter | solution.py:340
  285.4 24.3 %collective-permute-start.27 = (bf16[128,2048]{1,0:T(8,128)(2,1)S(1)}, bf16[128,2048]{1,0:T(8,128)(2,1)S(1)}, u32[]{:S(2)}, u32[]{:S(2)}) collective-permute-start(bf16[128,2048]{1,0:T(8,128)(2,1)S(1)} %get-tuple-element.163), channel_id=1, source_target_pairs={{0,1},{1,0},{16,17},{17,16},{2,3},{3,2},{18,19},{19,18},{4,5},{5,4... | collective-permute-start | bytes 1572872 | tf_op jit(solution)/shard_map/ppermute | solution.py:25
  320.2 24.7 %collective-permute-start.31 = (bf16[128,2048]{1,0:T(8,128)(2,1)S(1)}, bf16[128,2048]{1,0:T(8,128)(2,1)}, u32[]{:S(2)}, u32[]{:S(2)}) collective-permute-start(bf16[128,2048]{1,0:T(8,128)(2,1)S(1)} %fusion.53), channel_id=1, source_target_pairs={{0,16},{1,17},{16,0},{17,1},{2,18},{3,19},{18,2},{19,3},{4,20},{5,... | collective-permute-start | bytes 1572872 | tf_op jit(solution)/shard_map/ppermute | solution.py:25
  320.7 24.2 %collective-permute-start.30 = (bf16[128,2048]{1,0:T(8,128)(2,1)S(1)}, bf16[128,2048]{1,0:T(8,128)(2,1)}, u32[]{:S(2)}, u32[]{:S(2)}) collective-permute-start(bf16[128,2048]{1,0:T(8,128)(2,1)S(1)} %fusion.53), channel_id=1, source_target_pairs={{0,1},{1,0},{16,17},{17,16},{2,3},{3,2},{18,19},{19,18},{4,5},{5,4... | collective-permute-start | bytes 1572872 | tf_op jit(solution)/shard_map/ppermute | solution.py:25
  323.9 32.0 %collective-permute-start.39 = (bf16[8,128,256]{2,1,0:T(8,128)(2,1)}, bf16[8,128,256]{2,1,0:T(8,128)(2,1)}, u32[]{:S(2)}, u32[]{:S(2)}) collective-permute-start(bf16[8,128,256]{2,1,0:T(8,128)(2,1)} %constant_dynamic-update-slice_fusion.5), channel_id=1, source_target_pairs={{0,17},{1,16},{16,1},{17,0},{2,19},{3,18},{18,3},{19,2},{4,21},{5,... | collective-permute-start | bytes 1572872 | tf_op jit(solution)/shard_map/ppermute | solution.py:25
  326.4 38.1 %collective-permute-start.38 = (bf16[8,128,256]{2,1,0:T(8,128)(2,1)}, bf16[8,128,256]{2,1,0:T(8,128)(2,1)}, u32[]{:S(2)}, u32[]{:S(2)}) collective-permute-start(bf16[8,128,256]{2,1,0:T(8,128)(2,1)} %constant_dynamic-update-slice_fusion.5), channel_id=1, source_target_pairs={{0,16},{1,17},{16,0},{17,1},{2,18},{3,19},{18,2},{19,3},{4,20},{5,... | collective-permute-start | bytes 1572872 | tf_op jit(solution)/shard_map/ppermute | solution.py:25
  334.2 30.4 %collective-permute-start.37 = (bf16[8,128,256]{2,1,0:T(8,128)(2,1)}, bf16[8,128,256]{2,1,0:T(8,128)(2,1)}, u32[]{:S(2)}, u32[]{:S(2)}) collective-permute-start(bf16[8,128,256]{2,1,0:T(8,128)(2,1)} %constant_dynamic-update-slice_fusion.5), channel_id=1, source_target_pairs={{0,1},{1,0},{16,17},{17,16},{2,3},{3,2},{18,19},{19,18},{4,5},{5,4... | collective-permute-start | bytes 1572872 | tf_op jit(solution)/shard_map/ppermute | solution.py:25
  382.9 24.8 %collective-permute-start.40 = (bf16[128,2048]{1,0:T(8,128)(2,1)S(1)}, bf16[128,2048]{1,0:T(8,128)(2,1)S(1)}, u32[]{:S(2)}, u32[]{:S(2)}) collective-permute-start(bf16[128,2048]{1,0:T(8,128)(2,1)S(1)} %get-tuple-element.160), channel_id=1, source_target_pairs={{0,1},{1,0},{16,17},{17,16},{2,3},{3,2},{18,19},{19,18},{4,5},{5,4... | collective-permute-start | bytes 1572872 | tf_op jit(solution)/shard_map/ppermute | solution.py:25
  440.3 24.0 %collective-permute-start.47 = (bf16[128,2048]{1,0:T(8,128)(2,1)}, bf16[128,2048]{1,0:T(8,128)(2,1)}, u32[]{:S(2)}, u32[]{:S(2)}) collective-permute-start(bf16[128,2048]{1,0:T(8,128)(2,1)} %convert_element_type.494), channel_id=1, source_target_pairs={{0,16},{1,17},{16,0},{17,1},{2,18},{3,19},{18,2},{19,3},{4,20},{5,... | collective-permute-start | bytes 1572872 | tf_op jit(solution)/shard_map/ppermute | solution.py:25
  472.7 210.5 %reduce-scatter.7.cloned.1.call-start = ((), (), s32[]{:S(2)}) async-start(), calls=%async_computation.12 | async-start | bytes 9437184 | tf_op jit(solution)/shard_map/reduce_scatter | solution.py:336
  498.6 342.1 %reduce-scatter.11.cloned.1.call-start = ((), (), s32[]{:S(2)}) async-start(), calls=%async_computation.14 | async-start | bytes 9437184 | tf_op jit(solution)/shard_map/reduce_scatter | solution.py:336
  507.5 25.4 %collective-permute-start.49 = (bf16[128,2048]{1,0:T(8,128)(2,1)S(1)}, bf16[128,2048]{1,0:T(8,128)(2,1)S(1)}, u32[]{:S(2)}, u32[]{:S(2)}) collective-permute-start(bf16[128,2048]{1,0:T(8,128)(2,1)S(1)} %get-tuple-element.154), channel_id=1, source_target_pairs={{0,1},{1,0},{16,17},{17,16},{2,3},{3,2},{18,19},{19,18},{4,5},{5,4... | collective-permute-start | bytes 1572872 | tf_op jit(solution)/shard_map/ppermute | solution.py:25
  509.0 23.9 %collective-permute-start.51 = (bf16[128,2048]{1,0:T(8,128)(2,1)S(1)}, bf16[128,2048]{1,0:T(8,128)(2,1)S(1)}, u32[]{:S(2)}, u32[]{:S(2)}) collective-permute-start(bf16[128,2048]{1,0:T(8,128)(2,1)S(1)} %get-tuple-element.155), channel_id=1, source_target_pairs={{0,17},{1,16},{16,1},{17,0},{2,19},{3,18},{18,3},{19,2},{4,21},{5,... | collective-permute-start | bytes 1572872 | tf_op jit(solution)/shard_map/ppermute | solution.py:25
  510.5 23.6 %collective-permute-start.50 = (bf16[128,2048]{1,0:T(8,128)(2,1)S(1)}, bf16[128,2048]{1,0:T(8,128)(2,1)S(1)}, u32[]{:S(2)}, u32[]{:S(2)}) collective-permute-start(bf16[128,2048]{1,0:T(8,128)(2,1)S(1)} %get-tuple-element.156), channel_id=1, source_target_pairs={{0,16},{1,17},{16,0},{17,1},{2,18},{3,19},{18,2},{19,3},{4,20},{5,... | collective-permute-start | bytes 1572872 | tf_op jit(solution)/shard_map/ppermute | solution.py:25
  586.5 26.1 %collective-permute-start.58 = (bf16[1024,256]{1,0:T(8,128)(2,1)S(1)}, bf16[1024,256]{1,0:T(8,128)(2,1)S(1)}, u32[]{:S(2)}, u32[]{:S(2)}) collective-permute-start(bf16[1024,256]{1,0:T(8,128)(2,1)S(1)} %get-tuple-element.148), channel_id=1, source_target_pairs={{0,1},{1,0},{16,17},{17,16},{2,3},{3,2},{18,19},{19,18},{4,5},{5,4... | collective-permute-start | bytes 1572872 | tf_op jit(solution)/shard_map/ppermute | solution.py:25
  588.0 26.1 %collective-permute-start.60 = (bf16[1024,256]{1,0:T(8,128)(2,1)S(1)}, bf16[1024,256]{1,0:T(8,128)(2,1)S(1)}, u32[]{:S(2)}, u32[]{:S(2)}) collective-permute-start(bf16[1024,256]{1,0:T(8,128)(2,1)S(1)} %get-tuple-element.149), channel_id=1, source_target_pairs={{0,17},{1,16},{16,1},{17,0},{2,19},{3,18},{18,3},{19,2},{4,21},{5,... | collective-permute-start | bytes 1572872 | tf_op jit(solution)/shard_map/ppermute | solution.py:25
  589.5 24.6 %collective-permute-start.59 = (bf16[1024,256]{1,0:T(8,128)(2,1)S(1)}, bf16[1024,256]{1,0:T(8,128)(2,1)S(1)}, u32[]{:S(2)}, u32[]{:S(2)}) collective-permute-start(bf16[1024,256]{1,0:T(8,128)(2,1)S(1)} %get-tuple-element.150), channel_id=1, source_target_pairs={{0,16},{1,17},{16,0},{17,1},{2,18},{3,19},{18,2},{19,3},{4,20},{5,... | collective-permute-start | bytes 1572872 | tf_op jit(solution)/shard_map/ppermute | solution.py:25
  591.6 42.6 %collective-permute-start.55 = (bf16[128,2048]{1,0:T(8,128)(2,1)S(1)}, bf16[128,2048]{1,0:T(8,128)(2,1)S(1)}, u32[]{:S(2)}, u32[]{:S(2)}) collective-permute-start(bf16[128,2048]{1,0:T(8,128)(2,1)S(1)} %get-tuple-element.151), channel_id=1, source_target_pairs={{0,1},{1,0},{16,17},{17,16},{2,3},{3,2},{18,19},{19,18},{4,5},{5,4... | collective-permute-start | bytes 1572872 | tf_op jit(solution)/shard_map/ppermute | solution.py:25
  593.1 41.7 %collective-permute-start.57 = (bf16[128,2048]{1,0:T(8,128)(2,1)S(1)}, bf16[128,2048]{1,0:T(8,128)(2,1)S(1)}, u32[]{:S(2)}, u32[]{:S(2)}) collective-permute-start(bf16[128,2048]{1,0:T(8,128)(2,1)S(1)} %get-tuple-element.152), channel_id=1, source_target_pairs={{0,17},{1,16},{16,1},{17,0},{2,19},{3,18},{18,3},{19,2},{4,21},{5,... | collective-permute-start | bytes 1572872 | tf_op jit(solution)/shard_map/ppermute | solution.py:25
  693.3 178.3 %reduce-scatter.13.cloned.1.call-start = ((), (), s32[]{:S(2)}) async-start(), calls=%async_computation.15 | async-start | bytes 9437184 | tf_op jit(solution)/shard_map/reduce_scatter | solution.py:340
  703.4 225.1 %reduce-scatter.17.cloned.1.call-start = ((), (), s32[]{:S(2)}) async-start(), calls=%async_computation.17 | async-start | bytes 4718592 | tf_op jit(solution)/shard_map/reduce_scatter | solution.py:336
  708.3 298.1 %reduce-scatter.15.cloned.1.call-start = ((), (), s32[]{:S(2)}) async-start(), calls=%async_computation.16 | async-start | bytes 4718592 | tf_op jit(solution)/shard_map/reduce_scatter | solution.py:336
  721.6 29.8 %collective-permute-start.68 = (bf16[128,2048]{1,0:T(8,128)(2,1)}, bf16[128,2048]{1,0:T(8,128)(2,1)}, u32[]{:S(2)}, u32[]{:S(2)}) collective-permute-start(bf16[128,2048]{1,0:T(8,128)(2,1)} %get-tuple-element.145), channel_id=1, source_target_pairs={{0,1},{1,0},{16,17},{17,16},{2,3},{3,2},{18,19},{19,18},{4,5},{5,4... | collective-permute-start | bytes 1572872 | tf_op jit(solution)/shard_map/ppermute | solution.py:25
  722.5 29.0 %collective-permute-start.70 = (bf16[128,2048]{1,0:T(8,128)(2,1)}, bf16[128,2048]{1,0:T(8,128)(2,1)}, u32[]{:S(2)}, u32[]{:S(2)}) collective-permute-start(bf16[128,2048]{1,0:T(8,128)(2,1)} %get-tuple-element.146), channel_id=1, source_target_pairs={{0,17},{1,16},{16,1},{17,0},{2,19},{3,18},{18,3},{19,2},{4,21},{5,... | collective-permute-start | bytes 1572872 | tf_op jit(solution)/shard_map/ppermute | solution.py:25
  723.7 27.8 %collective-permute-start.69 = (bf16[128,2048]{1,0:T(8,128)(2,1)}, bf16[128,2048]{1,0:T(8,128)(2,1)}, u32[]{:S(2)}, u32[]{:S(2)}) collective-permute-start(bf16[128,2048]{1,0:T(8,128)(2,1)} %get-tuple-element.147), channel_id=1, source_target_pairs={{0,16},{1,17},{16,0},{17,1},{2,18},{3,19},{18,2},{19,3},{4,20},{5,... | collective-permute-start | bytes 1572872 | tf_op jit(solution)/shard_map/ppermute | solution.py:25
  725.1 24.1 %collective-permute-start.100 = (bf16[128,256]{1,0:T(8,128)(2,1)S(1)}, bf16[128,256]{1,0:T(8,128)(2,1)S(1)}, u32[]{:S(2)}, u32[]{:S(2)}) collective-permute-start(bf16[128,256]{1,0:T(8,128)(2,1)S(1)} %fusion.103), channel_id=1, source_target_pairs={{0,16},{1,17},{16,0},{17,1},{2,18},{3,19},{18,2},{19,3},{4,20},{5,... | collective-permute-start | bytes 196616 | tf_op jit(solution)/shard_map/ppermute | solution.py:25
  763.3 117.8 %collective-permute-start.104 = (bf16[64,256]{1,0:T(8,128)(2,1)}, bf16[64,256]{1,0:T(8,128)(2,1)S(1)}, u32[]{:S(2)}, u32[]{:S(2)}) collective-permute-start(bf16[64,256]{1,0:T(8,128)(2,1)} %get-tuple-element.192), channel_id=1, source_target_pairs={{0,4},{2,6},{12,8},{14,10},{1,5},{3,7},{13,9},{15,11},{16,20},{18,... | collective-permute-start | bytes 98312 | tf_op jit(solution)/shard_map/ppermute | solution.py:261
  809.4 26.1 %collective-permute-start.74 = (bf16[128,2048]{1,0:T(8,128)(2,1)S(1)}, bf16[128,2048]{1,0:T(8,128)(2,1)S(1)}, u32[]{:S(2)}, u32[]{:S(2)}) collective-permute-start(bf16[128,2048]{1,0:T(8,128)(2,1)S(1)} %get-tuple-element.142), channel_id=1, source_target_pairs={{0,1},{1,0},{16,17},{17,16},{2,3},{3,2},{18,19},{19,18},{4,5},{5,4... | collective-permute-start | bytes 1572872 | tf_op jit(solution)/shard_map/ppermute | solution.py:25
  810.1 25.9 %collective-permute-start.76 = (bf16[128,2048]{1,0:T(8,128)(2,1)S(1)}, bf16[128,2048]{1,0:T(8,128)(2,1)S(1)}, u32[]{:S(2)}, u32[]{:S(2)}) collective-permute-start(bf16[128,2048]{1,0:T(8,128)(2,1)S(1)} %get-tuple-element.143), channel_id=1, source_target_pairs={{0,17},{1,16},{16,1},{17,0},{2,19},{3,18},{18,3},{19,2},{4,21},{5,... | collective-permute-start | bytes 1572872 | tf_op jit(solution)/shard_map/ppermute | solution.py:25
  811.5 26.2 %collective-permute-start.75 = (bf16[128,2048]{1,0:T(8,128)(2,1)S(1)}, bf16[128,2048]{1,0:T(8,128)(2,1)S(1)}, u32[]{:S(2)}, u32[]{:S(2)}) collective-permute-start(bf16[128,2048]{1,0:T(8,128)(2,1)S(1)} %get-tuple-element.144), channel_id=1, source_target_pairs={{0,16},{1,17},{16,0},{17,1},{2,18},{3,19},{18,2},{19,3},{4,20},{5,... | collective-permute-start | bytes 1572872 | tf_op jit(solution)/shard_map/ppermute | solution.py:25
  813.8 69.0 %collective-permute-start.77 = (bf16[1024,256]{1,0:T(8,128)(2,1)}, bf16[1024,256]{1,0:T(8,128)(2,1)S(1)}, u32[]{:S(2)}, u32[]{:S(2)}) collective-permute-start(bf16[1024,256]{1,0:T(8,128)(2,1)} %get-tuple-element.139), channel_id=1, source_target_pairs={{0,1},{1,0},{16,17},{17,16},{2,3},{3,2},{18,19},{19,18},{4,5},{5,4... | collective-permute-start | bytes 1572872 | tf_op jit(solution)/shard_map/ppermute | solution.py:25
  835.4 47.5 %collective-permute-start.79 = (bf16[1024,256]{1,0:T(8,128)(2,1)S(1)}, bf16[1024,256]{1,0:T(8,128)(2,1)}, u32[]{:S(2)}, u32[]{:S(2)}) collective-permute-start(bf16[1024,256]{1,0:T(8,128)(2,1)S(1)} %get-tuple-element.140), channel_id=1, source_target_pairs={{0,17},{1,16},{16,1},{17,0},{2,19},{3,18},{18,3},{19,2},{4,21},{5,... | collective-permute-start | bytes 1572872 | tf_op jit(solution)/shard_map/ppermute | solution.py:25
  836.0 46.9 %collective-permute-start.78 = (bf16[1024,256]{1,0:T(8,128)(2,1)S(1)}, bf16[1024,256]{1,0:T(8,128)(2,1)}, u32[]{:S(2)}, u32[]{:S(2)}) collective-permute-start(bf16[1024,256]{1,0:T(8,128)(2,1)S(1)} %get-tuple-element.141), channel_id=1, source_target_pairs={{0,16},{1,17},{16,0},{17,1},{2,18},{3,19},{18,2},{19,3},{4,20},{5,... | collective-permute-start | bytes 1572872 | tf_op jit(solution)/shard_map/ppermute | solution.py:25
  886.2 51.4 %collective-permute-start.84 = (bf16[128,2048]{1,0:T(8,128)(2,1)}, bf16[128,2048]{1,0:T(8,128)(2,1)}, u32[]{:S(2)}, u32[]{:S(2)}) collective-permute-start(bf16[128,2048]{1,0:T(8,128)(2,1)} %get-tuple-element.157), channel_id=1, source_target_pairs={{0,1},{1,0},{16,17},{17,16},{2,3},{3,2},{18,19},{19,18},{4,5},{5,4... | collective-permute-start | bytes 1572872 | tf_op jit(solution)/shard_map/ppermute | solution.py:25
  887.7 52.6 %collective-permute-start.86 = (bf16[128,2048]{1,0:T(8,128)(2,1)}, bf16[128,2048]{1,0:T(8,128)(2,1)}, u32[]{:S(2)}, u32[]{:S(2)}) collective-permute-start(bf16[128,2048]{1,0:T(8,128)(2,1)} %get-tuple-element.158), channel_id=1, source_target_pairs={{0,17},{1,16},{16,1},{17,0},{2,19},{3,18},{18,3},{19,2},{4,21},{5,... | collective-permute-start | bytes 1572872 | tf_op jit(solution)/shard_map/ppermute | solution.py:25
  891.8 38.6 %collective-permute-start.81 = (bf16[128,256]{1,0:T(8,128)(2,1)}, bf16[128,256]{1,0:T(8,128)(2,1)S(1)}, u32[]{:S(2)}, u32[]{:S(2)}) collective-permute-start(bf16[128,256]{1,0:T(8,128)(2,1)} %get-tuple-element.185), channel_id=1, source_target_pairs={{0,4},{2,6},{4,0},{6,2},{8,12},{10,14},{12,8},{14,10},{1,5},{3,7},... | collective-permute-start | bytes 196616 | tf_op jit(solution)/shard_map/ppermute | solution.py:29
  893.1 38.9 %collective-permute-start.83 = (bf16[128,256]{1,0:T(8,128)(2,1)}, bf16[128,256]{1,0:T(8,128)(2,1)}, u32[]{:S(2)}, u32[]{:S(2)}) collective-permute-start(bf16[128,256]{1,0:T(8,128)(2,1)} %get-tuple-element.186), channel_id=1, source_target_pairs={{0,12},{2,14},{4,8},{6,10},{8,4},{10,6},{12,0},{14,2},{1,13},{3,15... | collective-permute-start | bytes 196616 | tf_op jit(solution)/shard_map/ppermute | solution.py:29
  895.4 39.0 %collective-permute-start.82 = (bf16[128,256]{1,0:T(8,128)(2,1)}, bf16[128,256]{1,0:T(8,128)(2,1)}, u32[]{:S(2)}, u32[]{:S(2)}) collective-permute-start(bf16[128,256]{1,0:T(8,128)(2,1)} %get-tuple-element.187), channel_id=1, source_target_pairs={{0,8},{2,10},{4,12},{6,14},{8,0},{10,2},{12,4},{14,6},{1,9},{3,11}... | collective-permute-start | bytes 196616 | tf_op jit(solution)/shard_map/ppermute | solution.py:29
  932.0 46.1 %collective-permute-start.107 = (bf16[64,256]{1,0:T(8,128)(2,1)S(1)}, bf16[64,256]{1,0:T(8,128)(2,1)S(1)}, u32[]{:S(2)}, u32[]{:S(2)}) collective-permute-start(bf16[64,256]{1,0:T(8,128)(2,1)S(1)} %copy-done.62), channel_id=1, source_target_pairs={{0,16},{1,17},{2,18},{3,19},{4,20},{5,21},{6,22},{7,23},{8,24},{9,... | collective-permute-start | bytes 98312 | tf_op jit(solution)/shard_map/ppermute | solution.py:503
  958.5 26.3 %collective-permute-start.87 = (bf16[128,2048]{1,0:T(8,128)(2,1)S(1)}, bf16[128,2048]{1,0:T(8,128)(2,1)S(1)}, u32[]{:S(2)}, u32[]{:S(2)}) collective-permute-start(bf16[128,2048]{1,0:T(8,128)(2,1)S(1)} %select_convert_fusion), channel_id=1, source_target_pairs={{0,16},{16,0},{1,17},{17,1},{2,18},{18,2},{3,19},{19,3},{4,20},{20... | collective-permute-start | bytes 1572872 | tf_op jit(solution)/shard_map/ppermute | solution.py:513
  972.0 25.9 %collective-permute-start.111 = (bf16[256,2048]{1,0:T(8,128)(2,1)S(1)}, bf16[256,2048]{1,0:T(8,128)(2,1)S(1)}, u32[]{:S(2)}, u32[]{:S(2)}) collective-permute-start(bf16[256,2048]{1,0:T(8,128)(2,1)S(1)} %copy-done.42), channel_id=1, source_target_pairs={{0,16},{1,17},{2,18},{3,19},{4,20},{5,21},{6,22},{7,23},{8,24},{9,... | collective-permute-start | bytes 3145736 | tf_op jit(solution)/shard_map/ppermute | solution.py:503
  975.7 28.0 %collective-permute-start.110 = (bf16[256,2048]{1,0:T(8,128)(2,1)S(1)}, bf16[256,2048]{1,0:T(8,128)(2,1)S(1)}, u32[]{:S(2)}, u32[]{:S(2)}) collective-permute-start(bf16[256,2048]{1,0:T(8,128)(2,1)S(1)} %copy-done.43), channel_id=1, source_target_pairs={{16,0},{17,1},{18,2},{19,3},{20,4},{21,5},{22,6},{23,7},{24,8},{25... | collective-permute-start | bytes 3145736 | tf_op jit(solution)/shard_map/ppermute | solution.py:503
  978.1 53.7 %collective-permute-start.109 = (bf16[256,512]{1,0:T(8,128)(2,1)}, bf16[256,512]{1,0:T(8,128)(2,1)S(1)}, u32[]{:S(2)}, u32[]{:S(2)}) collective-permute-start(bf16[256,512]{1,0:T(8,128)(2,1)} %get-tuple-element.171), channel_id=1, source_target_pairs={{0,16},{1,17},{2,18},{3,19},{4,20},{5,21},{6,22},{7,23},{8,24},{9,... | collective-permute-start | bytes 786440 | tf_op jit(solution)/shard_map/ppermute | solution.py:503
  982.7 43.4 %collective-permute-start.113 = (bf16[2048,256]{1,0:T(8,128)(2,1)}, bf16[2048,256]{1,0:T(8,128)(2,1)S(1)}, u32[]{:S(2)}, u32[]{:S(2)}) collective-permute-start(bf16[2048,256]{1,0:T(8,128)(2,1)} %reduce-scatter.9.cloned.1.call-done), channel_id=1, source_target_pairs={{0,16},{1,17},{2,18},{3,19},{4,20},{5,21},{6,22},{7,23},{8,24},{9,... | collective-permute-start | bytes 3145736 | tf_op jit(solution)/shard_map/ppermute | solution.py:503
  984.9 42.5 %collective-permute-start.112 = (bf16[2048,256]{1,0:T(8,128)(2,1)}, bf16[2048,256]{1,0:T(8,128)(2,1)}, u32[]{:S(2)}, u32[]{:S(2)}) collective-permute-start(bf16[2048,256]{1,0:T(8,128)(2,1)} %reduce-scatter.13.cloned.1.call-done), channel_id=1, source_target_pairs={{16,0},{17,1},{18,2},{19,3},{20,4},{21,5},{22,6},{23,7},{24,8},{25... | collective-permute-start | bytes 3145736 | tf_op jit(solution)/shard_map/ppermute | solution.py:503
  997.9 37.0 %collective-permute-start.89 = (bf16[256,512]{1,0:T(8,128)(2,1)}, bf16[256,512]{1,0:T(8,128)(2,1)S(1)}, u32[]{:S(2)}, u32[]{:S(2)}) collective-permute-start(bf16[256,512]{1,0:T(8,128)(2,1)} %get-tuple-element.174), channel_id=1, source_target_pairs={{0,16},{1,17},{2,18},{3,19},{4,20},{5,21},{6,22},{7,23},{8,24},{9,... | collective-permute-start | bytes 786440 | tf_op jit(solution)/shard_map/ppermute | solution.py:503
  (168 other events, 2625.4 us)
Sparse Core Ops, SparseCore 0:
  26.9 48.6 all-gather.6
  96.6 86.3 all-gather.8
  185.2 80.9 all-gather.10
  267.6 45.3 all-gather.12
  315.0 80.7 all-gather.16
  397.2 81.0 all-gather.14
  480.6 87.7 reduce-scatter.8
  570.7 92.1 reduce-scatter.6
  693.4 88.2 reduce-scatter.10
  783.8 87.7 reduce-scatter.12
  874.5 53.9 reduce-scatter.16
  931.2 51.7 reduce-scatter.14

commit v3 on v2

--- a/solution.py
+++ b/solution.py
@@ -33,16 +33,23 @@
     return lax.axis_size("section") * lax.axis_size("tensor")
 
 
+def spread_blocks(block):
+    return [block] + [swap_quad(block, k) for k in range(1, quad_size())]
+
+
 def spread(block):
-    return jnp.concatenate([block] + [swap_quad(block, k) for k in range(1, quad_size())], 0)
+    return jnp.concatenate(spread_blocks(block), 0)
+
+
+def collect_blocks(blocks):
+    total = blocks[0].astype(F32)
+    for k in range(1, quad_size()):
+        total = total + swap_quad(blocks[k].astype(BF16), k).astype(F32)
+    return total
 
 
 def collect(partial):
-    rows = partial.shape[0] // quad_size()
-    total = partial[:rows].astype(F32)
-    for k in range(1, quad_size()):
-        total = total + swap_quad(partial[k * rows : (k + 1) * rows], k).astype(F32)
-    return total
+    return collect_blocks(jnp.split(partial, quad_size(), 0))
 
 
 def gather_dp(block):
@@ -323,13 +330,16 @@
     return middle, (normed_all, keyval, queries, logs, attended), passed
 
 
-def mix_part(middle, norms):
-    return spread(layer_norm(middle, norms[2], norms[3]).astype(BF16))
-
-
-def hidden_part(mixed_all, hidden_mat):
-    hidden_pre = dot_nn(mixed_all, hidden_mat)
-    return hidden_pre, gelu_tanh(hidden_pre).astype(BF16)
+def feed_forward(middle, hidden_mat, project_mat, norms, whole):
+    mixed = spread_blocks(layer_norm(middle, norms[2], norms[3]).astype(BF16))
+    if whole:
+        mixed = [jnp.concatenate(mixed, 0)]
+    pre = [dot_nn(block, hidden_mat) for block in mixed]
+    act = [gelu_tanh(block).astype(BF16) for block in pre]
+    products = [dot_nn(block, project_mat).astype(BF16) for block in act]
+    if whole:
+        products = jnp.split(products[0], quad_size(), 0)
+    return middle + collect_blocks(products), (middle, mixed, pre, act)
 
 
 def scatter_rows(partial):
@@ -344,25 +354,32 @@
     pair, keyval_mat, hidden_mat, project_mat, norms = weights
     normed_all, keyval, queries, logs, attended, middle, mixed_all, hidden_pre, hidden_act = saved
     rows = inputs.shape[0]
-    grad_branch = spread(grad_out.astype(BF16))
-    grad_act = dot_nt(grad_branch, project_mat)
-    grad_pre = jax.vjp(gelu_tanh, hidden_pre)[1](grad_act)[0].astype(BF16)
-    hidden_act, _ = after(hidden_act, *early)
-    mixed_all, _ = after(mixed_all, *early)
+    branch = spread_blocks(grad_out.astype(BF16))
+    if len(hidden_pre) == 1:
+        branch = [jnp.concatenate(branch, 0)]
+    pre = [
+        jax.vjp(gelu_tanh, values)[1](dot_nt(block, project_mat))[0].astype(BF16)
+        for values, block in zip(hidden_pre, branch)
+    ]
+    grad_branch, grad_pre = jnp.concatenate(branch, 0), jnp.concatenate(pre, 0)
+    if len(pre) == 1:
+        pre = jnp.split(grad_pre, quad_size(), 0)
+    grad_mixed = collect_blocks([dot_nt(block, hidden_mat) for block in pre])
+    hidden_act, _ = after(jnp.concatenate(hidden_act, 0), *early)
+    mixed_all, _ = after(jnp.concatenate(mixed_all, 0), *early)
     grad_project = dot_tn(hidden_act, grad_branch).astype(BF16)
     sum_project = scatter_columns(grad_project)
     grad_hidden = dot_tn(mixed_all, grad_pre).astype(BF16)
     sum_hidden = scatter_rows(grad_hidden)
-    grad_mixed = collect(dot_nt(grad_pre, hidden_mat).astype(BF16))
     if not early:
-        grad_mixed, _ = after(grad_mixed, grad_project, grad_hidden)
+        grad_mixed, _ = after(grad_mixed, grad_project)
     pull = jax.vjp(layer_norm, middle, norms[2], norms[3])[1]
     grad_mid, grad_gain_two, grad_bias_two = pull(grad_mixed)
     grad_middle = grad_out + grad_mid
     grad_rows = spread(grad_middle.astype(BF16))
     grad_attended = dot_nt(grad_rows, pair[1].T).astype(BF16)
     grad_output = dot_tn(grad_rows, attended).astype(BF16)
-    held = (grad_output, grad_project, grad_hidden) + late if early else (grad_output,)
+    held = (grad_output, grad_project, grad_hidden) + late
     grad_attended, (grad_output, *_) = after(grad_attended, *held)
     grad_queries, grad_kv = attend_backward(
         queries, grad_attended, logs, keyval, limits, bases, rows
@@ -372,6 +389,7 @@
     grad_normed, (grad_query,) = after(grad_normed, grad_query)
     grad_pair = jnp.concatenate([grad_query, grad_output], 1)
     grad_keyval = scatter_keyval(grad_kv, rows).astype(BF16)
+    grad_pair, _ = after(grad_pair, grad_keyval)
     grad_normed = grad_normed + dot_nt(grad_keyval, keyval_mat)
     pull = jax.vjp(layer_norm, inputs, norms[0], norms[1])[1]
     grad_in, grad_gain_one, grad_bias_one = pull(grad_normed)
@@ -403,7 +421,7 @@
     depth = w_keyval.shape[1]
     columns = w_keyval.shape[2]
     table = jnp.pad(norm_params[0].reshape(-1), (0, 16 * columns - 4 * depth))
-    small, _ = gather_all(jnp.concatenate([w_keyval[0], table.reshape(16, columns)], 0))
+    small, small_passed = gather_all(jnp.concatenate([w_keyval[0], table.reshape(16, columns)], 0))
     keyval_mats = small[..., :depth, :].reshape(2, width, columns)
     norms = small[..., depth:, :].reshape(2, count * tensors, 16 * columns)
     norms = norms[..., : 4 * depth].reshape(2, count * tensors, 4, depth)
@@ -445,25 +463,23 @@
 
     pair_one = jnp.split(rows_of(query_both[0]), 2, axis=1)
     pair_two = jnp.split(rows_of(query_both[1]), 2, axis=1)
-    hidden_both, _ = after(hidden_both, norms)
+    hidden_both, _ = after(hidden_both, small_passed)
 
     middle_one, saved_one, passed = attend_part(
         inputs, pair_one, keyval_mats[0], norms[0], limits, bases
     )
     project_both, _ = after(project_both, passed)
-    project_one, project_two = (columns_of(p) for p in project_both)
+    project_one = columns_of(project_both[0])
     hidden_two = rows_of(hidden_both[1])
     hidden_one = rows_of(hidden_both[0])
-    mixed_one = mix_part(middle_one, norms[0])
-    pre_one, act_one = hidden_part(mixed_one, hidden_one)
-    between = middle_one + collect(dot_nn(act_one, project_one).astype(BF16))
-    between = between.astype(BF16).astype(F32)
+    between, fed_one = feed_forward(middle_one, hidden_one, project_one, norms[0], False)
+    between = between.astype(BF16)
+    project_two = columns_of(project_both[1])
+    between = between.astype(F32)
 
     middle_two, saved_two, _ = attend_part(between, pair_two, keyval_mats[1], norms[1], limits, bases)
-    mixed_two = mix_part(middle_two, norms[1])
-    cotangent, _ = after(cotangent, mixed_two)
-    pre_two, act_two = hidden_part(mixed_two, hidden_two)
-    outputs = middle_two + collect(dot_nn(act_two, project_two).astype(BF16))
+    cotangent, _ = after(cotangent, middle_two)
+    outputs, fed_two = feed_forward(middle_two, hidden_two, project_two, norms[1], True)
 
     grad_between, sums_two, grad_pair, table_two = layer_backward(
         between,
@@ -471,12 +487,11 @@
         (pair_two, keyval_mats[1], hidden_two, project_two, norms[1]),
         limits,
         bases,
-        saved_two + (middle_two, mixed_two, pre_two, act_two),
+        saved_two + fed_two,
         (),
         (),
     )
     grad_between = grad_between.astype(BF16)
-    grad_pair, _ = after(grad_pair, grad_between)
     sum_pair_two = scatter_rows(grad_pair)
     grad_between = grad_between.astype(F32)
     grad_inputs, sums_one, grad_pair, table_one = layer_backward(
@@ -485,25 +500,43 @@
         (pair_one, keyval_mats[0], hidden_one, project_one, norms[0]),
         limits,
         bases,
-        saved_one + (middle_one, mixed_one, pre_one, act_one),
+        saved_one + fed_one,
         sums_two[1:],
         (),
     )
-    sum_pair_one = scatter_rows(after(grad_pair, *sums_one[1:])[0])
-    halves_two = jnp.split(sum_pair_two, 2, axis=1)
-    halves_one = jnp.split(sum_pair_one, 2, axis=1)
-    sums_two = (halves_two[0], sums_two[0], halves_two[1]) + sums_two[1:]
-    sums_one = (halves_one[0], sums_one[0], halves_one[1]) + sums_one[1:]
-
-    results = []
-    for index, cut in enumerate((1, 0, 1, 1, 0)):
-        halves = []
-        for layer, sums in ((1, sums_two), (0, sums_one)):
-            own = sums[index].astype(BF16)
-            moved = lax.ppermute(own, "section", [(1 - layer, layer)])
-            pair = (own, moved) if layer == 0 else (moved, own)
-            halves.append(jnp.concatenate(pair, cut))
-        results.append(jnp.where(first, halves[1], halves[0]).astype(F32)[None])
+    def move(value, layer):
+        value = value.astype(BF16)
+        return value, lax.ppermute(value, "section", [(1 - layer, layer)])
+
+    small_two, hidden_moved_two, project_moved_two = (move(v, 1) for v in sums_two)
+    pair_moved_two = move(sum_pair_two, 1)
+    small_one, hidden_moved_one, project_moved_one = (move(v, 0) for v in sums_one)
+    grad_pair, _ = after(
+        grad_pair,
+        grad_inputs,
+        *hidden_moved_two,
+        *project_moved_two,
+        *hidden_moved_one,
+        *project_moved_one
+    )
+    pair_moved_one = move(scatter_rows(grad_pair), 0)
+
+    def merged(one, two, cut):
+        pair = jnp.where(
+            first, jnp.concatenate(one, cut), jnp.concatenate((two[1], two[0]), cut)
+        )
+        return pair.astype(F32)[None]
+
+    def columns_half(moved, index):
+        return tuple(jnp.split(value, 2, axis=1)[index] for value in moved)
+
+    results = [
+        merged(columns_half(pair_moved_one, 0), columns_half(pair_moved_two, 0), 1),
+        merged(small_one, small_two, 0),
+        merged(columns_half(pair_moved_one, 1), columns_half(pair_moved_two, 1), 1),
+        merged(hidden_moved_one, hidden_moved_two, 1),
+        merged(project_moved_one, project_moved_two, 0),
+    ]
 
     tables = jnp.stack([table_one, table_two]).reshape(2, 4, count, tensors, depth)
     table_result = scatter_all(jnp.moveaxis(tables, 1, 3), F32)

time: 1050 us -> 1020 us (0.971)
  waiting for transfers between devices: 547 us -> 477 us
  matrix products: 151 us -> 195 us
    dot_general x30 -> x45, matrix products: 151 us -> 195 us  [dot(): lax.dot_general(left, right, ((dims[0], dims[1]), ((), ())), preferred_el...]
    ppermute x72, waiting for transfers between devices: 391 us -> 349 us  [swap_quad(): lax.ppermute(block, ('section', 'tensor'), [(i, i ^ offset) for i in rang...]
    reduce_scatter x4, waiting for transfers between devices: 33.1 us -> 0.02 us  [scatter_rows(): return lax.psum_scatter(partial, 'dp', scatter_dimension=0, tiled=True)]
    reduce_scatter x2, waiting for transfers between devices: 31 us -> 1.02 us  [scatter_columns(): return lax.psum_scatter(partial, 'dp', scatter_dimension=1, tiled=True)]
    ppermute x10 -> x8, waiting for transfers between devices: 29 us -> 50.2 us  [move(): return (value, lax.ppermute(value, 'section', [(1 - layer, layer)]))]
    ppermute x26, waiting for transfers between devices: 17.2 us -> 36.8 us  [swap_dp(): lax.ppermute(block, 'dp', [(i, i ^ offset) for i in range(lax.axis_size('...]
    ppermute x10 -> x8, starting transfers between devices: 21.6 us -> 17.4 us  [move(): return (value, lax.ppermute(value, 'section', [(1 - layer, layer)]))]
  transfers between devices with their start and end apart: 133 -> 131, of which waited for: 59 -> 75; matrix products, arithmetic and copies ran while one was open for 22% -> 26% of each run, Pallas kernels for 7% -> 7%
where the time goes in v3:
time: 1020 us; the launch traced here: 1010 us
  waiting for transfers between devices  477 us (47%)
  matrix products  195 us (19%)
  starting transfers between devices  150 us (15%)
  Pallas kernels  70.8 us (7%)
  other arithmetic  64.3 us (6%)
  local copies, waits for them, and re-layouts  34.1 us (3%)
  between operations  16.8 us (2%)
    ppermute x72, waiting for transfers between devices, swap_quad(): lax.ppermute(block, ('section', 'tensor'), [(i, i ^ offset) for i in rang...  349 us
    dot_general x45, matrix products, dot(): lax.dot_general(left, right, ((dims[0], dims[1]), ((), ())), preferred_el...  195 us
    ppermute x72, starting transfers between devices, swap_quad(): lax.ppermute(block, ('section', 'tensor'), [(i, i ^ offset) for i in rang...  90.2 us
    ppermute x8, waiting for transfers between devices, move(): return (value, lax.ppermute(value, 'section', [(1 - layer, layer)]))  50.2 us
    pallas_call x2, Pallas kernels, attend_backward(): pl.pallas_call(functools.partial(attend_grad_kernel, rows, heads, head),...  41.5 us
    ppermute x26, waiting for transfers between devices, swap_dp(): lax.ppermute(block, 'dp', [(i, i ^ offset) for i in range(lax.axis_size('...  36.8 us
    pallas_call x2, Pallas kernels, attend_forward(): pl.pallas_call(functools.partial(attend_kernel, rows, heads, head), grid_...  29.3 us
    ppermute x3, waiting for transfers between devices, both(): moved = lax.ppermute(pick(1 - section), 'section', [(0, 1), (1, 0)])  22.6 us
  transfers between devices with their start and end apart: 131, of which 75 were waited for; matrix products, arithmetic and copies ran while one was open for 26% of the time, Pallas kernels for 7%

profile of v3, /device:TPU:0, one launch (start us, length us, event | category | flops | bytes accessed | tf_op | source)
XLA Modules:
  0.0 1007.6 jit_solution(10014631644116376416)
XLA Ops:
  12.8 11.8 %collective-permute-done.11 = bf16[256,1024]{1,0:T(8,128)(2,1)S(1)} collective-permute-done((bf16[256,1024]{1,0:T(8,128)(2,1)S(1)}, bf16[256,1024]{1,0:T(8,128)(2,1)S(1)}, u32[]{:S(2)}, u32[]{:S(2)}) %collective-permute-start.11) | collective-permute-done | bytes 524320 | tf_op jit(solution)/shard_map/ppermute | solution.py:448
  37.5 4.5 collective-permute-done.3
  42.0 10.8 %collective-permute-done.22 = bf16[256,2048]{1,0:T(8,128)(2,1)S(1)} collective-permute-done((bf16[256,2048]{1,0:T(8,128)(2,1)}, bf16[256,2048]{1,0:T(8,128)(2,1)S(1)}, u32[]{:S(2)}, u32[]{:S(2)}) %collective-permute-start.22) | collective-permute-done | bytes 1048608 | tf_op jit(solution)/shard_map/ppermute | solution.py:448
  64.3 7.6 collective-permute-done
  72.1 12.4 %collective-permute-done.6 = bf16[8,144,256]{2,1,0:T(8,128)(2,1)S(1)} collective-permute-done((bf16[8,144,256]{2,1,0:T(8,128)(2,1)S(1)}, bf16[8,144,256]{2,1,0:T(8,128)(2,1)S(1)}, u32[]{:S(2)}, u32[]{:S(2)}) %collective-permute-start.6) | collective-permute-done | bytes 589856 | tf_op jit(solution)/shard_map/ppermute | solution.py:25
  86.5 12.5 %collective-permute-done.7 = bf16[8,144,256]{2,1,0:T(8,128)(2,1)S(1)} collective-permute-done((bf16[8,144,256]{2,1,0:T(8,128)(2,1)S(1)}, bf16[8,144,256]{2,1,0:T(8,128)(2,1)S(1)}, u32[]{:S(2)}, u32[]{:S(2)}) %collective-permute-start.7) | collective-permute-done | bytes 589856 | tf_op jit(solution)/shard_map/ppermute | solution.py:25
  111.1 9.1 collective-permute-done.13
  129.8 9.1 collective-permute-done.18
  140.6 9.6 collective-permute-done.17
  152.8 8.7 collective-permute-done.10
  161.6 10.5 %collective-permute-done.9 = bf16[128,2048]{1,0:T(8,128)(2,1)} collective-permute-done((bf16[128,2048]{1,0:T(8,128)(2,1)S(1)}, bf16[128,2048]{1,0:T(8,128)(2,1)}, u32[]{:S(2)}, u32[]{:S(2)}) %collective-permute-start.9) | collective-permute-done | bytes 524320 | tf_op jit(solution)/shard_map/ppermute | solution.py:25
  175.8 14.7 %shard_map.143 = (bf16[512,512]{1,0:T(8,128)(2,1)S(1)}, f32[2,4,256]{2,1,0:T(4,128)S(1)}) custom-call(s32[16]{0:T(128)S(1)} %mul.512.base_ref, s32[2,1,256]{2,1,0:T(1,128)S(1)} %broadcast_in_dim.40.limit_ref, bf16[512,512]{1,0:T(8,128)(2,1)S(1)} %fusion.44.query_ref, bf16[2,2048,256]{2,1,0:T(8,128)(2,1)S(1)} %bitcast.359), custom_call_target="tpu_custom_call" | custom-call | flops 2147483648 | bytes 3145728 | tf_op jit(solution)/shard_map/pallas_call | solution.py:167
  197.4 21.3 %collective-permute-done.19 = bf16[128,2048]{1,0:T(8,128)(2,1)S(1)} collective-permute-done((bf16[128,2048]{1,0:T(8,128)(2,1)}, bf16[128,2048]{1,0:T(8,128)(2,1)S(1)}, u32[]{:S(2)}, u32[]{:S(2)}) %collective-permute-start.19) | collective-permute-done | bytes 524320 | tf_op jit(solution)/shard_map/ppermute | solution.py:25
  227.4 21.0 %collective-permute-done.24 = bf16[128,2048]{1,0:T(8,128)(2,1)} collective-permute-done((bf16[128,2048]{1,0:T(8,128)(2,1)}, bf16[128,2048]{1,0:T(8,128)(2,1)}, u32[]{:S(2)}, u32[]{:S(2)}) %collective-permute-start.24) | collective-permute-done | bytes 524320 | tf_op jit(solution)/shard_map/ppermute | solution.py:25
  248.5 6.4 multiply_convert_fusion.3
  262.7 5.0 convolution_convert_fusion.23
  280.4 5.2 collective-permute-done.27
  285.6 9.6 collective-permute-done.29
  295.3 12.1 %convert_reduce_fusion = (f32[128]{0:T(128)S(1)}, bf16[128,2048]{1,0:T(8,128)(2,1)S(1)}) fusion(f32[128,2048]{1,0:T(8,128)S(1)} %get-tuple-element.128, bf16[128,2048]{1,0:T(8,128)(2,1)S(1)} %collective-permute-done.29, bf16[128,2048]{1,0:T(8,128)(2,1)S(1)} %collective-permute-done.27, bf16[128,2048]{1,0:T(8,128)(2,1)S(1)} %collective-permute-done.25, ...), kind=kOutput, calls=%fused_computation.86 | convolution fusion | flops 1076887424 | bytes 12059136 | tf_op jit(solution)/shard_map/dot_general | solution.py:20
  331.3 9.0 collective-permute-done.31
  344.5 7.9 collective-permute-done.39
  352.4 6.5 collective-permute-done.38
  361.6 14.6 %shard_map.144 = (bf16[512,512]{1,0:T(8,128)(2,1)S(1)}, f32[2,4,256]{2,1,0:T(4,128)S(1)}) custom-call(s32[16]{0:T(128)S(1)} %mul.512.base_ref, s32[2,1,256]{2,1,0:T(1,128)S(1)} %broadcast_in_dim.40.limit_ref, bf16[512,512]{1,0:T(8,128)(2,1)S(1)} %fusion.50.query_ref, bf16[2,2048,256]{2,1,0:T(8,128)(2,1)S(1)} %bitcast.361), custom_call_target="tpu_custom_call" | custom-call | flops 2147483648 | bytes 3145728 | tf_op jit(solution)/shard_map/pallas_call | solution.py:167
  381.2 21.6 %collective-permute-done.40 = bf16[128,2048]{1,0:T(8,128)(2,1)S(1)} collective-permute-done((bf16[128,2048]{1,0:T(8,128)(2,1)S(1)}, bf16[128,2048]{1,0:T(8,128)(2,1)S(1)}, u32[]{:S(2)}, u32[]{:S(2)}) %collective-permute-start.40) | collective-permute-done | bytes 524320 | tf_op jit(solution)/shard_map/ppermute | solution.py:25
  414.0 8.7 collective-permute-done.48
  423.2 9.8 collective-permute-done.47
  434.0 11.3 %multiply_convert_fusion = (bf16[512,2048]{1,0:T(8,128)(2,1)S(1)}, f32[512,2048]{1,0:T(8,128)}) fusion(bf16[2048,2048]{1,0:T(8,128)(2,1)} %all-gather.17.cloned.1.call-done, bf16[128,2048]{1,0:T(8,128)(2,1)} %collective-permute-done.48, bf16[128,2048]{1,0:T(8,128)(2,1)} %collective-permute-done.47, bf16[128,2048]{1,0:T(8,128)(2,1)} %collective-permute-done.46, ...), kind=kOutput, calls=%fused_computation.15 | convolution fusion | flops 4312793088 | bytes 16777216 | tf_op jit(solution)/shard_map/dot_general | solution.py:20
  445.4 7.9 collective-permute-done.44
  454.4 8.3 convolution_convert_fusion.3
  465.9 12.5 %fusion.6 = bf16[512,2048]{1,0:T(8,128)(2,1)S(1)} fusion(f32[512,2048]{1,0:T(8,128)} %get-tuple-element.223, bf16[2048,2048]{1,0:T(8,128)(2,1)} %all-gather.15.cloned.1.call-done, bf16[128,2048]{1,0:T(8,128)(2,1)} %collective-permute-done.45, bf16[128,2048]{1,0:T(8,128)(2,1)} %collective-permute-done.44, bf16[128,2048]{1,0:T(8,128)(2,1)} %collective-permute-done.43, ...), kind=kOutput, calls=%fused_computation.12 | convolution fusion | flops 4324327424 | bytes 16777216 | tf_op jit(solution)/shard_map/dot_general | solution.py:20
  479.7 6.8 convolution_convert_fusion.2
  486.6 6.7 convolution_convert_fusion.20
  494.0 6.7 convolution_convert_fusion.19
  507.2 8.4 collective-permute-done.50
  515.5 10.7 %collective-permute-done.51 = bf16[128,2048]{1,0:T(8,128)(2,1)S(1)} collective-permute-done((bf16[128,2048]{1,0:T(8,128)(2,1)S(1)}, bf16[128,2048]{1,0:T(8,128)(2,1)S(1)}, u32[]{:S(2)}, u32[]{:S(2)}) %collective-permute-start.51) | collective-permute-done | bytes 524320 | tf_op jit(solution)/shard_map/ppermute | solution.py:25
  537.5 9.1 collective-permute-done.54
  546.6 8.7 collective-permute-done.53
  560.2 20.7 %shard_map.145 = (bf16[512,512]{1,0:T(8,128)(2,1)S(1)}, bf16[2,2048,256]{2,1,0:T(8,128)(2,1)S(1)}) custom-call(s32[16]{0:T(128)S(1)} %mul.512.base_ref, s32[2,1,256]{2,1,0:T(1,128)S(1)} %broadcast_in_dim.40.limit_ref, bf16[512,512]{1,0:T(8,128)(2,1)S(1)} %fusion.50.query_ref, bf16[512,512]{1,0:T(8,128)(2,1)S(1)} %fusion.53.grad_ref, ...), custom_call_target="tpu_custom_call" | custom-call | flops 5368709120 | bytes 6291456 | tf_op jit(solution)/shard_map/pallas_call | solution.py:235
  589.3 18.6 %collective-permute-done.58 = bf16[1024,256]{1,0:T(8,128)(2,1)S(1)} collective-permute-done((bf16[1024,256]{1,0:T(8,128)(2,1)S(1)}, bf16[1024,256]{1,0:T(8,128)(2,1)S(1)}, u32[]{:S(2)}, u32[]{:S(2)}) %collective-permute-start.58) | collective-permute-done | bytes 524320 | tf_op jit(solution)/shard_map/ppermute | solution.py:25
  614.6 14.1 %collective-permute-done.55 = bf16[128,2048]{1,0:T(8,128)(2,1)S(1)} collective-permute-done((bf16[128,2048]{1,0:T(8,128)(2,1)S(1)}, bf16[128,2048]{1,0:T(8,128)(2,1)S(1)}, u32[]{:S(2)}, u32[]{:S(2)}) %collective-permute-start.55) | collective-permute-done | bytes 524320 | tf_op jit(solution)/shard_map/ppermute | solution.py:25
  630.3 7.1 collective-permute-done.63
  646.9 9.0 collective-permute-done.69
  659.3 5.3 collective-permute-done.67
  664.5 4.5 fusion.86
  669.8 4.1 fusion.79
  673.9 9.7 convolution_convert_fusion
  686.6 6.9 convolution_convert_fusion.1
  694.6 7.3 convolution_convert_fusion.15
  704.4 7.1 convolution_convert_fusion.16
  719.2 7.3 collective-permute-done.68
  728.4 7.9 multiply_reduce_fusion.1
  741.4 8.2 convolution_convert_fusion.4
  753.7 7.9 collective-permute-done.72
  764.4 20.8 %shard_map.146 = (bf16[512,512]{1,0:T(8,128)(2,1)S(1)}, bf16[2,2048,256]{2,1,0:T(8,128)(2,1)S(1)}) custom-call(s32[16]{0:T(128)S(1)} %mul.512.base_ref, s32[2,1,256]{2,1,0:T(1,128)S(1)} %broadcast_in_dim.40.limit_ref, bf16[512,512]{1,0:T(8,128)(2,1)S(1)} %copy-done.5, bf16[512,512]{1,0:T(8,128)(2,1)S(1)} %fusion.47.grad_ref, ...), custom_call_target="tpu_custom_call" | custom-call | flops 5368709120 | bytes 6291456 | tf_op jit(solution)/shard_map/pallas_call | solution.py:235
  793.6 17.7 %collective-permute-done.77 = bf16[1024,256]{1,0:T(8,128)(2,1)S(1)} collective-permute-done((bf16[1024,256]{1,0:T(8,128)(2,1)S(1)}, bf16[1024,256]{1,0:T(8,128)(2,1)S(1)}, u32[]{:S(2)}, u32[]{:S(2)}) %collective-permute-start.77) | collective-permute-done | bytes 524320 | tf_op jit(solution)/shard_map/ppermute | solution.py:25
  818.8 15.0 %collective-permute-done.74 = bf16[128,2048]{1,0:T(8,128)(2,1)S(1)} collective-permute-done((bf16[128,2048]{1,0:T(8,128)(2,1)S(1)}, bf16[128,2048]{1,0:T(8,128)(2,1)S(1)}, u32[]{:S(2)}, u32[]{:S(2)}) %collective-permute-start.74) | collective-permute-done | bytes 524320 | tf_op jit(solution)/shard_map/ppermute | solution.py:25
  853.1 4.7 collective-permute-start.88
  873.0 9.9 collective-permute-done.89
  882.9 18.2 %collective-permute-done.88 = bf16[256,2048]{1,0:T(8,128)(2,1)} collective-permute-done((bf16[256,2048]{1,0:T(8,128)(2,1)}, bf16[256,2048]{1,0:T(8,128)(2,1)}, u32[]{:S(2)}, u32[]{:S(2)}) %collective-permute-start.88) | collective-permute-done | bytes 1048608 | tf_op jit(solution)/shard_map/ppermute | solution.py:509
  901.1 10.0 collective-permute-done.91
  931.8 5.0 collective-permute-done.109
  980.6 4.4 fusion.22
  986.3 4.1 fusion.23
  990.4 7.3 collective-permute-done.92
  (660 shorter events, 350.5 us)
Async XLA Ops:
  7.2 164.8 %all-gather.7.cloned.1.call-start = ((), (), s32[]{:S(2)}) async-start(), calls=%async_computation.6 | async-start | bytes 4718592 | tf_op jit(solution)/shard_map/all_gather | solution.py:459
  25.8 222.6 %all-gather.9.cloned.1.call-start = ((), (), s32[]{:S(2)}) async-start(), calls=%async_computation.7 | async-start | bytes 9437184 | tf_op jit(solution)/shard_map/all_gather | solution.py:459
  28.3 24.6 %collective-permute-start.22 = (bf16[256,2048]{1,0:T(8,128)(2,1)}, bf16[256,2048]{1,0:T(8,128)(2,1)S(1)}, u32[]{:S(2)}, u32[]{:S(2)}) collective-permute-start(bf16[256,2048]{1,0:T(8,128)(2,1)} %dynamic-slice_bitcast_fusion.1), channel_id=1, source_target_pairs={{0,16},{16,0},{1,17},{17,1},{2,18},{18,2},{3,19},{19,3},{4,20},{20... | collective-permute-start | bytes 3145736 | tf_op jit(solution)/shard_map/ppermute | solution.py:448
  56.0 206.8 %all-gather.11.cloned.1.call-start = ((), (), s32[]{:S(2)}) async-start(), calls=%async_computation.8 | async-start | bytes 9437184 | tf_op jit(solution)/shard_map/all_gather | solution.py:462
  58.4 26.1 %collective-permute-start.6 = (bf16[8,144,256]{2,1,0:T(8,128)(2,1)S(1)}, bf16[8,144,256]{2,1,0:T(8,128)(2,1)S(1)}, u32[]{:S(2)}, u32[]{:S(2)}) collective-permute-start(bf16[8,144,256]{2,1,0:T(8,128)(2,1)S(1)} %bitcast.381), channel_id=1, source_target_pairs={{0,16},{1,17},{16,0},{17,1},{2,18},{3,19},{18,2},{19,3},{4,20},{5,... | collective-permute-start | bytes 1769480 | tf_op jit(solution)/shard_map/ppermute | solution.py:25
  61.4 45.9 %collective-permute-start.23 = (bf16[2048,256]{1,0:T(8,128)(2,1)}, bf16[2048,256]{1,0:T(8,128)(2,1)}, u32[]{:S(2)}, u32[]{:S(2)}) collective-permute-start(bf16[2048,256]{1,0:T(8,128)(2,1)} %dynamic-slice_bitcast_fusion), channel_id=1, source_target_pairs={{0,16},{16,0},{1,17},{17,1},{2,18},{18,2},{3,19},{19,3},{4,20},{20... | collective-permute-start | bytes 3145736 | tf_op jit(solution)/shard_map/ppermute | solution.py:448
  62.8 23.5 %collective-permute-start.5 = (bf16[8,144,256]{2,1,0:T(8,128)(2,1)S(1)}, bf16[8,144,256]{2,1,0:T(8,128)(2,1)S(1)}, u32[]{:S(2)}, u32[]{:S(2)}) collective-permute-start(bf16[8,144,256]{2,1,0:T(8,128)(2,1)S(1)} %bitcast.382), channel_id=1, source_target_pairs={{0,1},{1,0},{16,17},{17,16},{2,3},{3,2},{18,19},{19,18},{4,5},{5,4... | collective-permute-start | bytes 1769480 | tf_op jit(solution)/shard_map/ppermute | solution.py:25
  120.2 211.1 %all-gather.13.cloned.1.call-start = ((), (), s32[]{:S(2)}) async-start(), calls=%async_computation.9 | async-start | bytes 4718592 | tf_op jit(solution)/shard_map/all_gather | solution.py:459
  120.8 302.4 %all-gather.17.cloned.1.call-start = ((), (), s32[]{:S(2)}) async-start(), calls=%async_computation.11 | async-start | bytes 9437184 | tf_op jit(solution)/shard_map/all_gather | solution.py:459
  121.4 344.5 %all-gather.15.cloned.1.call-start = ((), (), s32[]{:S(2)}) async-start(), calls=%async_computation.10 | async-start | bytes 9437184 | tf_op jit(solution)/shard_map/all_gather | solution.py:462
  125.7 24.4 %collective-permute-start.17 = (bf16[8,128,256]{2,1,0:T(8,128)(2,1)S(1)}, bf16[8,128,256]{2,1,0:T(8,128)(2,1)S(1)}, u32[]{:S(2)}, u32[]{:S(2)}) collective-permute-start(bf16[8,128,256]{2,1,0:T(8,128)(2,1)S(1)} %constant_dynamic-update-slice_fusion), channel_id=1, source_target_pairs={{0,16},{1,17},{16,0},{17,1},{2,18},{3,19},{18,2},{19,3},{4,20},{5,... | collective-permute-start | bytes 1572872 | tf_op jit(solution)/shard_map/ppermute | solution.py:25
  126.3 23.9 %collective-permute-start.16 = (bf16[8,128,256]{2,1,0:T(8,128)(2,1)S(1)}, bf16[8,128,256]{2,1,0:T(8,128)(2,1)S(1)}, u32[]{:S(2)}, u32[]{:S(2)}) collective-permute-start(bf16[8,128,256]{2,1,0:T(8,128)(2,1)S(1)} %constant_dynamic-update-slice_fusion), channel_id=1, source_target_pairs={{0,1},{1,0},{16,17},{17,16},{2,3},{3,2},{18,19},{19,18},{4,5},{5,4... | collective-permute-start | bytes 1572872 | tf_op jit(solution)/shard_map/ppermute | solution.py:25
  126.9 34.7 %collective-permute-start.10 = (bf16[128,2048]{1,0:T(8,128)(2,1)S(1)}, bf16[128,2048]{1,0:T(8,128)(2,1)}, u32[]{:S(2)}, u32[]{:S(2)}) collective-permute-start(bf16[128,2048]{1,0:T(8,128)(2,1)S(1)} %fusion.64), channel_id=1, source_target_pairs={{0,17},{1,16},{16,1},{17,0},{2,19},{3,18},{18,3},{19,2},{4,21},{5,... | collective-permute-start | bytes 1572872 | tf_op jit(solution)/shard_map/ppermute | solution.py:25
  129.2 42.8 %collective-permute-start.9 = (bf16[128,2048]{1,0:T(8,128)(2,1)S(1)}, bf16[128,2048]{1,0:T(8,128)(2,1)}, u32[]{:S(2)}, u32[]{:S(2)}) collective-permute-start(bf16[128,2048]{1,0:T(8,128)(2,1)S(1)} %fusion.64), channel_id=1, source_target_pairs={{0,16},{1,17},{16,0},{17,1},{2,18},{3,19},{18,2},{19,3},{4,20},{5,... | collective-permute-start | bytes 1572872 | tf_op jit(solution)/shard_map/ppermute | solution.py:25
  138.9 33.1 %collective-permute-start.8 = (bf16[128,2048]{1,0:T(8,128)(2,1)S(1)}, bf16[128,2048]{1,0:T(8,128)(2,1)}, u32[]{:S(2)}, u32[]{:S(2)}) collective-permute-start(bf16[128,2048]{1,0:T(8,128)(2,1)S(1)} %fusion.64), channel_id=1, source_target_pairs={{0,1},{1,0},{16,17},{17,16},{2,3},{3,2},{18,19},{19,18},{4,5},{5,4... | collective-permute-start | bytes 1572872 | tf_op jit(solution)/shard_map/ppermute | solution.py:25
  193.6 25.2 %collective-permute-start.19 = (bf16[128,2048]{1,0:T(8,128)(2,1)}, bf16[128,2048]{1,0:T(8,128)(2,1)S(1)}, u32[]{:S(2)}, u32[]{:S(2)}) collective-permute-start(bf16[128,2048]{1,0:T(8,128)(2,1)} %get-tuple-element.159), channel_id=1, source_target_pairs={{0,1},{1,0},{16,17},{17,16},{2,3},{3,2},{18,19},{19,18},{4,5},{5,4... | collective-permute-start | bytes 1572872 | tf_op jit(solution)/shard_map/ppermute | solution.py:25
  195.0 23.8 %collective-permute-start.21 = (bf16[128,2048]{1,0:T(8,128)(2,1)}, bf16[128,2048]{1,0:T(8,128)(2,1)S(1)}, u32[]{:S(2)}, u32[]{:S(2)}) collective-permute-start(bf16[128,2048]{1,0:T(8,128)(2,1)} %get-tuple-element.160), channel_id=1, source_target_pairs={{0,17},{1,16},{16,1},{17,0},{2,19},{3,18},{18,3},{19,2},{4,21},{5,... | collective-permute-start | bytes 1572872 | tf_op jit(solution)/shard_map/ppermute | solution.py:25
  196.5 23.9 %collective-permute-start.20 = (bf16[128,2048]{1,0:T(8,128)(2,1)}, bf16[128,2048]{1,0:T(8,128)(2,1)}, u32[]{:S(2)}, u32[]{:S(2)}) collective-permute-start(bf16[128,2048]{1,0:T(8,128)(2,1)} %get-tuple-element.161), channel_id=1, source_target_pairs={{0,16},{1,17},{16,0},{17,1},{2,18},{3,19},{18,2},{19,3},{4,20},{5,... | collective-permute-start | bytes 1572872 | tf_op jit(solution)/shard_map/ppermute | solution.py:25
  197.1 476.8 %reduce-scatter.9.cloned.1.call-start = ((), (), s32[]{:S(2)}) async-start(), calls=%async_computation.13 | async-start | bytes 9437184 | tf_op jit(solution)/shard_map/reduce_scatter | solution.py:350
  224.0 24.5 %collective-permute-start.24 = (bf16[128,2048]{1,0:T(8,128)(2,1)}, bf16[128,2048]{1,0:T(8,128)(2,1)}, u32[]{:S(2)}, u32[]{:S(2)}) collective-permute-start(bf16[128,2048]{1,0:T(8,128)(2,1)} %add_convert_fusion.3), channel_id=1, source_target_pairs={{0,1},{1,0},{16,17},{17,16},{2,3},{3,2},{18,19},{19,18},{4,5},{5,4... | collective-permute-start | bytes 1572872 | tf_op jit(solution)/shard_map/ppermute | solution.py:25
  225.5 33.4 %collective-permute-start.28 = (bf16[128,2048]{1,0:T(8,128)(2,1)}, bf16[128,2048]{1,0:T(8,128)(2,1)}, u32[]{:S(2)}, u32[]{:S(2)}) collective-permute-start(bf16[128,2048]{1,0:T(8,128)(2,1)} %add_convert_fusion.3), channel_id=1, source_target_pairs={{0,17},{1,16},{16,1},{17,0},{2,19},{3,18},{18,3},{19,2},{4,21},{5,... | collective-permute-start | bytes 1572872 | tf_op jit(solution)/shard_map/ppermute | solution.py:25
  226.9 28.0 %collective-permute-start.26 = (bf16[128,2048]{1,0:T(8,128)(2,1)}, bf16[128,2048]{1,0:T(8,128)(2,1)}, u32[]{:S(2)}, u32[]{:S(2)}) collective-permute-start(bf16[128,2048]{1,0:T(8,128)(2,1)} %add_convert_fusion.3), channel_id=1, source_target_pairs={{0,16},{1,17},{16,0},{17,1},{2,18},{3,19},{18,2},{19,3},{4,20},{5,... | collective-permute-start | bytes 1572872 | tf_op jit(solution)/shard_map/ppermute | solution.py:25
  315.6 24.8 %collective-permute-start.31 = (bf16[128,2048]{1,0:T(8,128)(2,1)S(1)}, bf16[128,2048]{1,0:T(8,128)(2,1)}, u32[]{:S(2)}, u32[]{:S(2)}) collective-permute-start(bf16[128,2048]{1,0:T(8,128)(2,1)S(1)} %fusion.61), channel_id=1, source_target_pairs={{0,16},{1,17},{16,0},{17,1},{2,18},{3,19},{18,2},{19,3},{4,20},{5,... | collective-permute-start | bytes 1572872 | tf_op jit(solution)/shard_map/ppermute | solution.py:25
  317.7 23.4 %collective-permute-start.30 = (bf16[128,2048]{1,0:T(8,128)(2,1)S(1)}, bf16[128,2048]{1,0:T(8,128)(2,1)}, u32[]{:S(2)}, u32[]{:S(2)}) collective-permute-start(bf16[128,2048]{1,0:T(8,128)(2,1)S(1)} %fusion.61), channel_id=1, source_target_pairs={{0,1},{1,0},{16,17},{17,16},{2,3},{3,2},{18,19},{19,18},{4,5},{5,4... | collective-permute-start | bytes 1572872 | tf_op jit(solution)/shard_map/ppermute | solution.py:25
  324.5 27.9 %collective-permute-start.39 = (bf16[8,128,256]{2,1,0:T(8,128)(2,1)}, bf16[8,128,256]{2,1,0:T(8,128)(2,1)}, u32[]{:S(2)}, u32[]{:S(2)}) collective-permute-start(bf16[8,128,256]{2,1,0:T(8,128)(2,1)} %constant_dynamic-update-slice_fusion.5), channel_id=1, source_target_pairs={{0,17},{1,16},{16,1},{17,0},{2,19},{3,18},{18,3},{19,2},{4,21},{5,... | collective-permute-start | bytes 1572872 | tf_op jit(solution)/shard_map/ppermute | solution.py:25
  326.3 32.6 %collective-permute-start.38 = (bf16[8,128,256]{2,1,0:T(8,128)(2,1)}, bf16[8,128,256]{2,1,0:T(8,128)(2,1)}, u32[]{:S(2)}, u32[]{:S(2)}) collective-permute-start(bf16[8,128,256]{2,1,0:T(8,128)(2,1)} %constant_dynamic-update-slice_fusion.5), channel_id=1, source_target_pairs={{0,16},{1,17},{16,0},{17,1},{2,18},{3,19},{18,2},{19,3},{4,20},{5,... | collective-permute-start | bytes 1572872 | tf_op jit(solution)/shard_map/ppermute | solution.py:25
  330.6 29.2 %collective-permute-start.37 = (bf16[8,128,256]{2,1,0:T(8,128)(2,1)}, bf16[8,128,256]{2,1,0:T(8,128)(2,1)}, u32[]{:S(2)}, u32[]{:S(2)}) collective-permute-start(bf16[8,128,256]{2,1,0:T(8,128)(2,1)} %constant_dynamic-update-slice_fusion.5), channel_id=1, source_target_pairs={{0,1},{1,0},{16,17},{17,16},{2,3},{3,2},{18,19},{19,18},{4,5},{5,4... | collective-permute-start | bytes 1572872 | tf_op jit(solution)/shard_map/ppermute | solution.py:25
  377.7 25.1 %collective-permute-start.40 = (bf16[128,2048]{1,0:T(8,128)(2,1)S(1)}, bf16[128,2048]{1,0:T(8,128)(2,1)S(1)}, u32[]{:S(2)}, u32[]{:S(2)}) collective-permute-start(bf16[128,2048]{1,0:T(8,128)(2,1)S(1)} %get-tuple-element.156), channel_id=1, source_target_pairs={{0,1},{1,0},{16,17},{17,16},{2,3},{3,2},{18,19},{19,18},{4,5},{5,4... | collective-permute-start | bytes 1572872 | tf_op jit(solution)/shard_map/ppermute | solution.py:25
  378.4 24.4 %collective-permute-start.42 = (bf16[128,2048]{1,0:T(8,128)(2,1)S(1)}, bf16[128,2048]{1,0:T(8,128)(2,1)S(1)}, u32[]{:S(2)}, u32[]{:S(2)}) collective-permute-start(bf16[128,2048]{1,0:T(8,128)(2,1)S(1)} %get-tuple-element.157), channel_id=1, source_target_pairs={{0,17},{1,16},{16,1},{17,0},{2,19},{3,18},{18,3},{19,2},{4,21},{5,... | collective-permute-start | bytes 1572872 | tf_op jit(solution)/shard_map/ppermute | solution.py:25
  380.6 23.5 %collective-permute-start.41 = (bf16[128,2048]{1,0:T(8,128)(2,1)S(1)}, bf16[128,2048]{1,0:T(8,128)(2,1)S(1)}, u32[]{:S(2)}, u32[]{:S(2)}) collective-permute-start(bf16[128,2048]{1,0:T(8,128)(2,1)S(1)} %get-tuple-element.158), channel_id=1, source_target_pairs={{0,16},{1,17},{16,0},{17,1},{2,18},{3,19},{18,2},{19,3},{4,20},{5,... | collective-permute-start | bytes 1572872 | tf_op jit(solution)/shard_map/ppermute | solution.py:25
  407.9 25.1 %collective-permute-start.47 = (bf16[128,2048]{1,0:T(8,128)(2,1)}, bf16[128,2048]{1,0:T(8,128)(2,1)}, u32[]{:S(2)}, u32[]{:S(2)}) collective-permute-start(bf16[128,2048]{1,0:T(8,128)(2,1)} %add_convert_fusion.1), channel_id=1, source_target_pairs={{0,16},{1,17},{16,0},{17,1},{2,18},{3,19},{18,2},{19,3},{4,20},{5,... | collective-permute-start | bytes 1572872 | tf_op jit(solution)/shard_map/ppermute | solution.py:25
  408.6 25.4 %collective-permute-start.46 = (bf16[128,2048]{1,0:T(8,128)(2,1)}, bf16[128,2048]{1,0:T(8,128)(2,1)}, u32[]{:S(2)}, u32[]{:S(2)}) collective-permute-start(bf16[128,2048]{1,0:T(8,128)(2,1)} %add_convert_fusion.1), channel_id=1, source_target_pairs={{0,1},{1,0},{16,17},{17,16},{2,3},{3,2},{18,19},{19,18},{4,5},{5,4... | collective-permute-start | bytes 1572872 | tf_op jit(solution)/shard_map/ppermute | solution.py:25
  412.0 33.3 %collective-permute-start.45 = (bf16[128,2048]{1,0:T(8,128)(2,1)}, bf16[128,2048]{1,0:T(8,128)(2,1)}, u32[]{:S(2)}, u32[]{:S(2)}) collective-permute-start(bf16[128,2048]{1,0:T(8,128)(2,1)} %convert_element_type.532), channel_id=1, source_target_pairs={{0,17},{1,16},{16,1},{17,0},{2,19},{3,18},{18,3},{19,2},{4,21},{5,... | collective-permute-start | bytes 1572872 | tf_op jit(solution)/shard_map/ppermute | solution.py:25
  413.4 39.9 %collective-permute-start.44 = (bf16[128,2048]{1,0:T(8,128)(2,1)}, bf16[128,2048]{1,0:T(8,128)(2,1)}, u32[]{:S(2)}, u32[]{:S(2)}) collective-permute-start(bf16[128,2048]{1,0:T(8,128)(2,1)} %convert_element_type.532), channel_id=1, source_target_pairs={{0,16},{1,17},{16,0},{17,1},{2,18},{3,19},{18,2},{19,3},{4,20},{5,... | collective-permute-start | bytes 1572872 | tf_op jit(solution)/shard_map/ppermute | solution.py:25
  422.7 31.6 %collective-permute-start.43 = (bf16[128,2048]{1,0:T(8,128)(2,1)}, bf16[128,2048]{1,0:T(8,128)(2,1)}, u32[]{:S(2)}, u32[]{:S(2)}) collective-permute-start(bf16[128,2048]{1,0:T(8,128)(2,1)} %convert_element_type.532), channel_id=1, source_target_pairs={{0,1},{1,0},{16,17},{17,16},{2,3},{3,2},{18,19},{19,18},{4,5},{5,4... | collective-permute-start | bytes 1572872 | tf_op jit(solution)/shard_map/ppermute | solution.py:25
  462.7 211.2 %reduce-scatter.7.cloned.1.call-start = ((), (), s32[]{:S(2)}) async-start(), calls=%async_computation.12 | async-start | bytes 9437184 | tf_op jit(solution)/shard_map/reduce_scatter | solution.py:346
  486.5 377.2 %reduce-scatter.11.cloned.1.call-start = ((), (), s32[]{:S(2)}) async-start(), calls=%async_computation.14 | async-start | bytes 9437184 | tf_op jit(solution)/shard_map/reduce_scatter | solution.py:346
  532.7 22.7 %collective-permute-start.53 = (bf16[128,2048]{1,0:T(8,128)(2,1)S(1)}, bf16[128,2048]{1,0:T(8,128)(2,1)S(1)}, u32[]{:S(2)}, u32[]{:S(2)}) collective-permute-start(bf16[128,2048]{1,0:T(8,128)(2,1)S(1)} %fusion.137), channel_id=1, source_target_pairs={{0,16},{1,17},{16,0},{17,1},{2,18},{3,19},{18,2},{19,3},{4,20},{5,... | collective-permute-start | bytes 1572872 | tf_op jit(solution)/shard_map/ppermute | solution.py:25
  533.2 22.8 %collective-permute-start.52 = (bf16[128,2048]{1,0:T(8,128)(2,1)S(1)}, bf16[128,2048]{1,0:T(8,128)(2,1)S(1)}, u32[]{:S(2)}, u32[]{:S(2)}) collective-permute-start(bf16[128,2048]{1,0:T(8,128)(2,1)S(1)} %fusion.137), channel_id=1, source_target_pairs={{0,1},{1,0},{16,17},{17,16},{2,3},{3,2},{18,19},{19,18},{4,5},{5,4... | collective-permute-start | bytes 1572872 | tf_op jit(solution)/shard_map/ppermute | solution.py:25
  581.1 26.8 %collective-permute-start.58 = (bf16[1024,256]{1,0:T(8,128)(2,1)S(1)}, bf16[1024,256]{1,0:T(8,128)(2,1)S(1)}, u32[]{:S(2)}, u32[]{:S(2)}) collective-permute-start(bf16[1024,256]{1,0:T(8,128)(2,1)S(1)} %get-tuple-element.147), channel_id=1, source_target_pairs={{0,1},{1,0},{16,17},{17,16},{2,3},{3,2},{18,19},{19,18},{4,5},{5,4... | collective-permute-start | bytes 1572872 | tf_op jit(solution)/shard_map/ppermute | solution.py:25
  581.9 27.6 %collective-permute-start.60 = (bf16[1024,256]{1,0:T(8,128)(2,1)S(1)}, bf16[1024,256]{1,0:T(8,128)(2,1)S(1)}, u32[]{:S(2)}, u32[]{:S(2)}) collective-permute-start(bf16[1024,256]{1,0:T(8,128)(2,1)S(1)} %get-tuple-element.148), channel_id=1, source_target_pairs={{0,17},{1,16},{16,1},{17,0},{2,19},{3,18},{18,3},{19,2},{4,21},{5,... | collective-permute-start | bytes 1572872 | tf_op jit(solution)/shard_map/ppermute | solution.py:25
  584.2 25.3 %collective-permute-start.59 = (bf16[1024,256]{1,0:T(8,128)(2,1)S(1)}, bf16[1024,256]{1,0:T(8,128)(2,1)S(1)}, u32[]{:S(2)}, u32[]{:S(2)}) collective-permute-start(bf16[1024,256]{1,0:T(8,128)(2,1)S(1)} %get-tuple-element.149), channel_id=1, source_target_pairs={{0,16},{1,17},{16,0},{17,1},{2,18},{3,19},{18,2},{19,3},{4,20},{5,... | collective-permute-start | bytes 1572872 | tf_op jit(solution)/shard_map/ppermute | solution.py:25
  586.1 42.6 %collective-permute-start.55 = (bf16[128,2048]{1,0:T(8,128)(2,1)S(1)}, bf16[128,2048]{1,0:T(8,128)(2,1)S(1)}, u32[]{:S(2)}, u32[]{:S(2)}) collective-permute-start(bf16[128,2048]{1,0:T(8,128)(2,1)S(1)} %get-tuple-element.150), channel_id=1, source_target_pairs={{0,1},{1,0},{16,17},{17,16},{2,3},{3,2},{18,19},{19,18},{4,5},{5,4... | collective-permute-start | bytes 1572872 | tf_op jit(solution)/shard_map/ppermute | solution.py:25
  587.0 41.7 %collective-permute-start.57 = (bf16[128,2048]{1,0:T(8,128)(2,1)S(1)}, bf16[128,2048]{1,0:T(8,128)(2,1)S(1)}, u32[]{:S(2)}, u32[]{:S(2)}) collective-permute-start(bf16[128,2048]{1,0:T(8,128)(2,1)S(1)} %get-tuple-element.151), channel_id=1, source_target_pairs={{0,17},{1,16},{16,1},{17,0},{2,19},{3,18},{18,3},{19,2},{4,21},{5,... | collective-permute-start | bytes 1572872 | tf_op jit(solution)/shard_map/ppermute | solution.py:25
  607.9 22.1 %collective-permute-start.56 = (bf16[128,2048]{1,0:T(8,128)(2,1)S(1)}, bf16[128,2048]{1,0:T(8,128)(2,1)S(1)}, u32[]{:S(2)}, u32[]{:S(2)}) collective-permute-start(bf16[128,2048]{1,0:T(8,128)(2,1)S(1)} %get-tuple-element.152), channel_id=1, source_target_pairs={{0,16},{1,17},{16,0},{17,1},{2,18},{3,19},{18,2},{19,3},{4,20},{5,... | collective-permute-start | bytes 1572872 | tf_op jit(solution)/shard_map/ppermute | solution.py:25
  641.7 22.8 %collective-permute-start.67 = (bf16[128,2048]{1,0:T(8,128)(2,1)S(1)}, bf16[128,2048]{1,0:T(8,128)(2,1)S(1)}, u32[]{:S(2)}, u32[]{:S(2)}) collective-permute-start(bf16[128,2048]{1,0:T(8,128)(2,1)S(1)} %add_convert_fusion), channel_id=1, source_target_pairs={{0,16},{1,17},{16,0},{17,1},{2,18},{3,19},{18,2},{19,3},{4,20},{5,... | collective-permute-start | bytes 1572872 | tf_op jit(solution)/shard_map/ppermute | solution.py:25
  642.2 26.9 %collective-permute-start.65 = (bf16[128,2048]{1,0:T(8,128)(2,1)S(1)}, bf16[128,2048]{1,0:T(8,128)(2,1)S(1)}, u32[]{:S(2)}, u32[]{:S(2)}) collective-permute-start(bf16[128,2048]{1,0:T(8,128)(2,1)S(1)} %add_convert_fusion), channel_id=1, source_target_pairs={{0,1},{1,0},{16,17},{17,16},{2,3},{3,2},{18,19},{19,18},{4,5},{5,4... | collective-permute-start | bytes 1572872 | tf_op jit(solution)/shard_map/ppermute | solution.py:25
  683.6 182.4 %reduce-scatter.13.cloned.1.call-start = ((), (), s32[]{:S(2)}) async-start(), calls=%async_computation.15 | async-start | bytes 9437184 | tf_op jit(solution)/shard_map/reduce_scatter | solution.py:350
  693.6 234.0 %reduce-scatter.17.cloned.1.call-start = ((), (), s32[]{:S(2)}) async-start(), calls=%async_computation.17 | async-start | bytes 4718592 | tf_op jit(solution)/shard_map/reduce_scatter | solution.py:346
  719.0 266.0 %reduce-scatter.15.cloned.1.call-start = ((), (), s32[]{:S(2)}) async-start(), calls=%async_computation.16 | async-start | bytes 4718592 | tf_op jit(solution)/shard_map/reduce_scatter | solution.py:346
  785.3 26.1 %collective-permute-start.77 = (bf16[1024,256]{1,0:T(8,128)(2,1)S(1)}, bf16[1024,256]{1,0:T(8,128)(2,1)S(1)}, u32[]{:S(2)}, u32[]{:S(2)}) collective-permute-start(bf16[1024,256]{1,0:T(8,128)(2,1)S(1)} %get-tuple-element.141), channel_id=1, source_target_pairs={{0,1},{1,0},{16,17},{17,16},{2,3},{3,2},{18,19},{19,18},{4,5},{5,4... | collective-permute-start | bytes 1572872 | tf_op jit(solution)/shard_map/ppermute | solution.py:25
  786.6 29.3 %collective-permute-start.79 = (bf16[1024,256]{1,0:T(8,128)(2,1)S(1)}, bf16[1024,256]{1,0:T(8,128)(2,1)S(1)}, u32[]{:S(2)}, u32[]{:S(2)}) collective-permute-start(bf16[1024,256]{1,0:T(8,128)(2,1)S(1)} %get-tuple-element.142), channel_id=1, source_target_pairs={{0,17},{1,16},{16,1},{17,0},{2,19},{3,18},{18,3},{19,2},{4,21},{5,... | collective-permute-start | bytes 1572872 | tf_op jit(solution)/shard_map/ppermute | solution.py:25
  788.6 29.9 %collective-permute-start.78 = (bf16[1024,256]{1,0:T(8,128)(2,1)S(1)}, bf16[1024,256]{1,0:T(8,128)(2,1)S(1)}, u32[]{:S(2)}, u32[]{:S(2)}) collective-permute-start(bf16[1024,256]{1,0:T(8,128)(2,1)S(1)} %get-tuple-element.143), channel_id=1, source_target_pairs={{0,16},{1,17},{16,0},{17,1},{2,18},{3,19},{18,2},{19,3},{4,20},{5,... | collective-permute-start | bytes 1572872 | tf_op jit(solution)/shard_map/ppermute | solution.py:25
  790.3 43.5 %collective-permute-start.74 = (bf16[128,2048]{1,0:T(8,128)(2,1)S(1)}, bf16[128,2048]{1,0:T(8,128)(2,1)S(1)}, u32[]{:S(2)}, u32[]{:S(2)}) collective-permute-start(bf16[128,2048]{1,0:T(8,128)(2,1)S(1)} %get-tuple-element.144), channel_id=1, source_target_pairs={{0,1},{1,0},{16,17},{17,16},{2,3},{3,2},{18,19},{19,18},{4,5},{5,4... | collective-permute-start | bytes 1572872 | tf_op jit(solution)/shard_map/ppermute | solution.py:25
  791.6 42.2 %collective-permute-start.76 = (bf16[128,2048]{1,0:T(8,128)(2,1)S(1)}, bf16[128,2048]{1,0:T(8,128)(2,1)S(1)}, u32[]{:S(2)}, u32[]{:S(2)}) collective-permute-start(bf16[128,2048]{1,0:T(8,128)(2,1)S(1)} %get-tuple-element.145), channel_id=1, source_target_pairs={{0,17},{1,16},{16,1},{17,0},{2,19},{3,18},{18,3},{19,2},{4,21},{5,... | collective-permute-start | bytes 1572872 | tf_op jit(solution)/shard_map/ppermute | solution.py:25
  811.4 24.0 %collective-permute-start.75 = (bf16[128,2048]{1,0:T(8,128)(2,1)S(1)}, bf16[128,2048]{1,0:T(8,128)(2,1)S(1)}, u32[]{:S(2)}, u32[]{:S(2)}) collective-permute-start(bf16[128,2048]{1,0:T(8,128)(2,1)S(1)} %get-tuple-element.146), channel_id=1, source_target_pairs={{0,16},{1,17},{16,0},{17,1},{2,18},{3,19},{18,2},{19,3},{4,20},{5,... | collective-permute-start | bytes 1572872 | tf_op jit(solution)/shard_map/ppermute | solution.py:25
  815.9 47.8 %collective-permute-start.84 = (bf16[128,2048]{1,0:T(8,128)(2,1)}, bf16[128,2048]{1,0:T(8,128)(2,1)}, u32[]{:S(2)}, u32[]{:S(2)}) collective-permute-start(bf16[128,2048]{1,0:T(8,128)(2,1)} %get-tuple-element.153), channel_id=1, source_target_pairs={{0,1},{1,0},{16,17},{17,16},{2,3},{3,2},{18,19},{19,18},{4,5},{5,4... | collective-permute-start | bytes 1572872 | tf_op jit(solution)/shard_map/ppermute | solution.py:25
  818.5 46.6 %collective-permute-start.86 = (bf16[128,2048]{1,0:T(8,128)(2,1)}, bf16[128,2048]{1,0:T(8,128)(2,1)}, u32[]{:S(2)}, u32[]{:S(2)}) collective-permute-start(bf16[128,2048]{1,0:T(8,128)(2,1)} %get-tuple-element.154), channel_id=1, source_target_pairs={{0,17},{1,16},{16,1},{17,0},{2,19},{3,18},{18,3},{19,2},{4,21},{5,... | collective-permute-start | bytes 1572872 | tf_op jit(solution)/shard_map/ppermute | solution.py:25
  845.9 23.3 %collective-permute-start.85 = (bf16[128,2048]{1,0:T(8,128)(2,1)}, bf16[128,2048]{1,0:T(8,128)(2,1)}, u32[]{:S(2)}, u32[]{:S(2)}) collective-permute-start(bf16[128,2048]{1,0:T(8,128)(2,1)} %get-tuple-element.155), channel_id=1, source_target_pairs={{0,16},{1,17},{16,0},{17,1},{2,18},{3,19},{18,2},{19,3},{4,20},{5,... | collective-permute-start | bytes 1572872 | tf_op jit(solution)/shard_map/ppermute | solution.py:25
  847.7 35.2 %collective-permute-start.89 = (bf16[2048,256]{1,0:T(8,128)(2,1)}, bf16[2048,256]{1,0:T(8,128)(2,1)}, u32[]{:S(2)}, u32[]{:S(2)}) collective-permute-start(bf16[2048,256]{1,0:T(8,128)(2,1)} %reduce-scatter.9.cloned.1.call-done), channel_id=1, source_target_pairs={{0,16},{1,17},{2,18},{3,19},{4,20},{5,21},{6,22},{7,23},{8,24},{9,... | collective-permute-start | bytes 3145736 | tf_op jit(solution)/shard_map/ppermute | solution.py:509
  853.1 48.0 %collective-permute-start.88 = (bf16[256,2048]{1,0:T(8,128)(2,1)}, bf16[256,2048]{1,0:T(8,128)(2,1)}, u32[]{:S(2)}, u32[]{:S(2)}) collective-permute-start(bf16[256,2048]{1,0:T(8,128)(2,1)} %reduce-scatter.7.cloned.1.call-done), channel_id=1, source_target_pairs={{0,16},{1,17},{2,18},{3,19},{4,20},{5,21},{6,22},{7,23},{8,24},{9,... | collective-permute-start | bytes 3145736 | tf_op jit(solution)/shard_map/ppermute | solution.py:509
  863.7 37.4 %collective-permute-start.90 = (bf16[256,2048]{1,0:T(8,128)(2,1)}, bf16[256,2048]{1,0:T(8,128)(2,1)}, u32[]{:S(2)}, u32[]{:S(2)}) collective-permute-start(bf16[256,2048]{1,0:T(8,128)(2,1)} %reduce-scatter.11.cloned.1.call-done), channel_id=1, source_target_pairs={{16,0},{17,1},{18,2},{19,3},{20,4},{21,5},{22,6},{23,7},{24,8},{25... | collective-permute-start | bytes 3145736 | tf_op jit(solution)/shard_map/ppermute | solution.py:509
  866.1 45.1 %collective-permute-start.91 = (bf16[2048,256]{1,0:T(8,128)(2,1)}, bf16[2048,256]{1,0:T(8,128)(2,1)}, u32[]{:S(2)}, u32[]{:S(2)}) collective-permute-start(bf16[2048,256]{1,0:T(8,128)(2,1)} %reduce-scatter.13.cloned.1.call-done), channel_id=1, source_target_pairs={{16,0},{17,1},{18,2},{19,3},{20,4},{21,5},{22,6},{23,7},{24,8},{25... | collective-permute-start | bytes 3145736 | tf_op jit(solution)/shard_map/ppermute | solution.py:509
  936.9 38.5 %collective-permute-start.111 = (bf16[64,256]{1,0:T(8,128)(2,1)S(1)}, bf16[64,256]{1,0:T(8,128)(2,1)S(1)}, u32[]{:S(2)}, u32[]{:S(2)}) collective-permute-start(bf16[64,256]{1,0:T(8,128)(2,1)S(1)} %fusion.150), channel_id=1, source_target_pairs={{0,16},{1,17},{2,18},{3,19},{4,20},{5,21},{6,22},{7,23},{8,24},{9,... | collective-permute-start | bytes 98312 | tf_op jit(solution)/shard_map/ppermute | solution.py:509
  (186 other events, 2531.0 us)
Sparse Core Ops, SparseCore 0:
  26.0 49.6 all-gather.6
  77.8 86.5 all-gather.8
  166.5 80.9 all-gather.10
  248.9 45.3 all-gather.12
  296.3 86.1 all-gather.16
  383.9 81.0 all-gather.14
  467.3 87.7 reduce-scatter.8
  557.4 92.1 reduce-scatter.6
  683.7 87.9 reduce-scatter.10
  773.9 92.1 reduce-scatter.12
  868.9 49.0 reduce-scatter.16
  920.7 52.1 reduce-scatter.14

commit v4 on v3

--- a/solution.py
+++ b/solution.py
@@ -340,6 +340,31 @@
     if whole:
         products = jnp.split(products[0], quad_size(), 0)
     return middle + collect_blocks(products), (middle, mixed, pre, act)
+
+
+def core_sum(partial):
+    count = lax.axis_size("dp")
+    core = lax.axis_index("dp") % 2
+    rows = partial.shape[0] // count
+
+    def shards(index):
+        return jnp.concatenate(
+            [
+                lax.dynamic_slice_in_dim(partial, (2 * j + index) * rows, rows, 0)
+                for j in range(count // 2)
+            ],
+            0,
+        )
+
+    return (shards(core).astype(F32) + swap_dp(shards(1 - core), 1).astype(F32)).astype(BF16)
+
+
+def scatter_line(partial):
+    count = lax.axis_size("dp")
+    lines = [[2 * i + core for i in range(count // 2)] for core in range(2)]
+    return lax.psum_scatter(
+        partial, "dp", scatter_dimension=0, axis_index_groups=lines, tiled=True
+    )
 
 
 def scatter_rows(partial):
@@ -387,7 +412,7 @@
     grad_normed = collect(dot_nt(grad_queries, pair[0]).astype(BF16))
     grad_query = dot_tn(normed_all, grad_queries).astype(BF16)
     grad_normed, (grad_query,) = after(grad_normed, grad_query)
-    grad_pair = jnp.concatenate([grad_query, grad_output], 1)
+    grad_pair = core_sum(jnp.concatenate([grad_query, grad_output], 1))
     grad_keyval = scatter_keyval(grad_kv, rows).astype(BF16)
     grad_pair, _ = after(grad_pair, grad_keyval)
     grad_normed = grad_normed + dot_nt(grad_keyval, keyval_mat)
@@ -492,7 +517,7 @@
         (),
     )
     grad_between = grad_between.astype(BF16)
-    sum_pair_two = scatter_rows(grad_pair)
+    sum_pair_two = scatter_line(grad_pair)
     grad_between = grad_between.astype(F32)
     grad_inputs, sums_one, grad_pair, table_one = layer_backward(
         inputs,
@@ -516,10 +541,9 @@
         grad_inputs,
         *hidden_moved_two,
         *project_moved_two,
-        *hidden_moved_one,
         *project_moved_one
     )
-    pair_moved_one = move(scatter_rows(grad_pair), 0)
+    pair_moved_one = move(scatter_line(grad_pair), 0)
 
     def merged(one, two, cut):
         pair = jnp.where(

time: 1020 us -> 1050 us (1.029)
  waiting for transfers between devices: 477 us -> 501 us
    ppermute x72, waiting for transfers between devices: 349 us -> 373 us  [swap_quad(): lax.ppermute(block, ('section', 'tensor'), [(i, i ^ offset) for i in rang...]
    ppermute x26 -> x28, waiting for transfers between devices: 36.8 us -> 30.2 us  [swap_dp(): lax.ppermute(block, 'dp', [(i, i ^ offset) for i in range(lax.axis_size('...]
    ppermute x26 -> x28, starting transfers between devices: 22.2 us -> 24 us  [swap_dp(): lax.ppermute(block, 'dp', [(i, i ^ offset) for i in range(lax.axis_size('...]
  transfers between devices with their start and end apart: 131 -> 133, of which waited for: 75 -> 72; matrix products, arithmetic and copies ran while one was open for 26% -> 26% of each run, Pallas kernels for 7% -> 7%
where the time goes in v4:
time: 1050 us; the launch traced here: 1040 us
  waiting for transfers between devices  501 us (48%)
  matrix products  186 us (18%)
  starting transfers between devices  160 us (15%)
  Pallas kernels  70.6 us (7%)
  other arithmetic  64.4 us (6%)
  local copies, waits for them, and re-layouts  37.9 us (4%)
  between operations  17.1 us (2%)
    ppermute x72, waiting for transfers between devices, swap_quad(): lax.ppermute(block, ('section', 'tensor'), [(i, i ^ offset) for i in rang...  373 us
    dot_general x45, matrix products, dot(): lax.dot_general(left, right, ((dims[0], dims[1]), ((), ())), preferred_el...  186 us
    ppermute x72, starting transfers between devices, swap_quad(): lax.ppermute(block, ('section', 'tensor'), [(i, i ^ offset) for i in rang...  88.1 us
    ppermute x8, waiting for transfers between devices, move(): return (value, lax.ppermute(value, 'section', [(1 - layer, layer)]))  57.1 us
    pallas_call x2, Pallas kernels, attend_backward(): pl.pallas_call(functools.partial(attend_grad_kernel, rows, heads, head),...  41.3 us
    ppermute x28, waiting for transfers between devices, swap_dp(): lax.ppermute(block, 'dp', [(i, i ^ offset) for i in range(lax.axis_size('...  30.2 us
    pallas_call x2, Pallas kernels, attend_forward(): pl.pallas_call(functools.partial(attend_kernel, rows, heads, head), grid_...  29.3 us
    ppermute x8, starting transfers between devices, move(): return (value, lax.ppermute(value, 'section', [(1 - layer, layer)]))  25.5 us
  transfers between devices with their start and end apart: 133, of which 72 were waited for; matrix products, arithmetic and copies ran while one was open for 26% of the time, Pallas kernels for 7%

profile of v4, /device:TPU:0, one launch (start us, length us, event | category | flops | bytes accessed | tf_op | source)
XLA Modules:
  0.0 1036.0 jit_solution(4072266786828360501)
XLA Ops:
  12.8 11.8 %collective-permute-done.11 = bf16[256,1024]{1,0:T(8,128)(2,1)S(1)} collective-permute-done((bf16[256,1024]{1,0:T(8,128)(2,1)S(1)}, bf16[256,1024]{1,0:T(8,128)(2,1)S(1)}, u32[]{:S(2)}, u32[]{:S(2)}) %collective-permute-start.11) | collective-permute-done | bytes 524320 | tf_op jit(solution)/shard_map/ppermute | solution.py:473
  37.4 4.5 collective-permute-done.3
  42.0 10.8 %collective-permute-done.22 = bf16[256,2048]{1,0:T(8,128)(2,1)S(1)} collective-permute-done((bf16[256,2048]{1,0:T(8,128)(2,1)}, bf16[256,2048]{1,0:T(8,128)(2,1)S(1)}, u32[]{:S(2)}, u32[]{:S(2)}) %collective-permute-start.22) | collective-permute-done | bytes 1048608 | tf_op jit(solution)/shard_map/ppermute | solution.py:473
  64.2 7.6 collective-permute-done
  72.1 12.4 %collective-permute-done.6 = bf16[8,144,256]{2,1,0:T(8,128)(2,1)S(1)} collective-permute-done((bf16[8,144,256]{2,1,0:T(8,128)(2,1)S(1)}, bf16[8,144,256]{2,1,0:T(8,128)(2,1)S(1)}, u32[]{:S(2)}, u32[]{:S(2)}) %collective-permute-start.6) | collective-permute-done | bytes 589856 | tf_op jit(solution)/shard_map/ppermute | solution.py:25
  86.4 12.5 %collective-permute-done.7 = bf16[8,144,256]{2,1,0:T(8,128)(2,1)S(1)} collective-permute-done((bf16[8,144,256]{2,1,0:T(8,128)(2,1)S(1)}, bf16[8,144,256]{2,1,0:T(8,128)(2,1)S(1)}, u32[]{:S(2)}, u32[]{:S(2)}) %collective-permute-start.7) | collective-permute-done | bytes 589856 | tf_op jit(solution)/shard_map/ppermute | solution.py:25
  111.0 9.1 collective-permute-done.13
  129.8 9.1 collective-permute-done.18
  140.6 9.6 collective-permute-done.17
  152.8 8.7 collective-permute-done.10
  161.5 10.5 %collective-permute-done.9 = bf16[128,2048]{1,0:T(8,128)(2,1)} collective-permute-done((bf16[128,2048]{1,0:T(8,128)(2,1)S(1)}, bf16[128,2048]{1,0:T(8,128)(2,1)}, u32[]{:S(2)}, u32[]{:S(2)}) %collective-permute-start.9) | collective-permute-done | bytes 524320 | tf_op jit(solution)/shard_map/ppermute | solution.py:25
  175.7 14.7 %shard_map.143 = (bf16[512,512]{1,0:T(8,128)(2,1)S(1)}, f32[2,4,256]{2,1,0:T(4,128)S(1)}) custom-call(s32[16]{0:T(128)S(1)} %mul.544.base_ref, s32[2,1,256]{2,1,0:T(1,128)S(1)} %broadcast_in_dim.40.limit_ref, bf16[512,512]{1,0:T(8,128)(2,1)S(1)} %fusion.44.query_ref, bf16[2,2048,256]{2,1,0:T(8,128)(2,1)S(1)} %bitcast.359), custom_call_target="tpu_custom_call" | custom-call | flops 2147483648 | bytes 3145728 | tf_op jit(solution)/shard_map/pallas_call | solution.py:167
  197.6 21.1 %collective-permute-done.19 = bf16[128,2048]{1,0:T(8,128)(2,1)S(1)} collective-permute-done((bf16[128,2048]{1,0:T(8,128)(2,1)}, bf16[128,2048]{1,0:T(8,128)(2,1)S(1)}, u32[]{:S(2)}, u32[]{:S(2)}) %collective-permute-start.19) | collective-permute-done | bytes 524320 | tf_op jit(solution)/shard_map/ppermute | solution.py:25
  227.4 21.0 %collective-permute-done.24 = bf16[128,2048]{1,0:T(8,128)(2,1)} collective-permute-done((bf16[128,2048]{1,0:T(8,128)(2,1)}, bf16[128,2048]{1,0:T(8,128)(2,1)}, u32[]{:S(2)}, u32[]{:S(2)}) %collective-permute-start.24) | collective-permute-done | bytes 524320 | tf_op jit(solution)/shard_map/ppermute | solution.py:25
  248.4 6.4 multiply_convert_fusion.3
  262.7 5.0 convolution_convert_fusion.23
  280.4 5.2 collective-permute-done.27
  285.6 9.6 collective-permute-done.29
  312.3 7.4 collective-permute-done.32
  321.1 9.1 collective-permute-done.31
  334.5 7.8 collective-permute-done.39
  342.3 6.5 collective-permute-done.38
  351.5 14.6 %shard_map.144 = (bf16[512,512]{1,0:T(8,128)(2,1)S(1)}, f32[2,4,256]{2,1,0:T(4,128)S(1)}) custom-call(s32[16]{0:T(128)S(1)} %mul.544.base_ref, s32[2,1,256]{2,1,0:T(1,128)S(1)} %broadcast_in_dim.40.limit_ref, bf16[512,512]{1,0:T(8,128)(2,1)S(1)} %fusion.50.query_ref, bf16[2,2048,256]{2,1,0:T(8,128)(2,1)S(1)} %bitcast.361), custom_call_target="tpu_custom_call" | custom-call | flops 2147483648 | bytes 3145728 | tf_op jit(solution)/shard_map/pallas_call | solution.py:167
  371.2 21.6 %collective-permute-done.40 = bf16[128,2048]{1,0:T(8,128)(2,1)S(1)} collective-permute-done((bf16[128,2048]{1,0:T(8,128)(2,1)S(1)}, bf16[128,2048]{1,0:T(8,128)(2,1)S(1)}, u32[]{:S(2)}, u32[]{:S(2)}) %collective-permute-start.40) | collective-permute-done | bytes 524320 | tf_op jit(solution)/shard_map/ppermute | solution.py:25
  403.9 8.7 collective-permute-done.48
  413.2 9.8 collective-permute-done.47
  424.0 11.5 %multiply_convert_fusion = (bf16[512,2048]{1,0:T(8,128)(2,1)S(1)}, f32[512,2048]{1,0:T(8,128)}) fusion(bf16[2048,2048]{1,0:T(8,128)(2,1)} %all-gather.17.cloned.1.call-done, bf16[128,2048]{1,0:T(8,128)(2,1)} %collective-permute-done.48, bf16[128,2048]{1,0:T(8,128)(2,1)} %collective-permute-done.47, bf16[128,2048]{1,0:T(8,128)(2,1)} %collective-permute-done.46, ...), kind=kOutput, calls=%fused_computation.15 | convolution fusion | flops 4312793088 | bytes 16777216 | tf_op jit(solution)/shard_map/dot_general | solution.py:20
  435.4 7.8 collective-permute-done.44
  444.3 8.3 convolution_convert_fusion.3
  459.7 12.4 %fusion.6 = bf16[512,2048]{1,0:T(8,128)(2,1)S(1)} fusion(f32[512,2048]{1,0:T(8,128)} %get-tuple-element.239, bf16[2048,2048]{1,0:T(8,128)(2,1)} %all-gather.15.cloned.1.call-done, bf16[128,2048]{1,0:T(8,128)(2,1)} %collective-permute-done.45, bf16[128,2048]{1,0:T(8,128)(2,1)} %collective-permute-done.44, bf16[128,2048]{1,0:T(8,128)(2,1)} %collective-permute-done.43, ...), kind=kOutput, calls=%fused_computation.12 | convolution fusion | flops 4324327424 | bytes 16777216 | tf_op jit(solution)/shard_map/dot_general | solution.py:20
  473.5 6.9 convolution_convert_fusion.2
  480.4 6.7 convolution_convert_fusion.20
  488.7 6.3 convolution_convert_fusion.19
  501.3 8.6 collective-permute-done.50
  509.9 10.4 %collective-permute-done.51 = bf16[128,2048]{1,0:T(8,128)(2,1)S(1)} collective-permute-done((bf16[128,2048]{1,0:T(8,128)(2,1)S(1)}, bf16[128,2048]{1,0:T(8,128)(2,1)S(1)}, u32[]{:S(2)}, u32[]{:S(2)}) %collective-permute-start.51) | collective-permute-done | bytes 524320 | tf_op jit(solution)/shard_map/ppermute | solution.py:25
  528.4 12.3 %collective-permute-done.54 = bf16[128,2048]{1,0:T(8,128)(2,1)S(1)} collective-permute-done((bf16[128,2048]{1,0:T(8,128)(2,1)S(1)}, bf16[128,2048]{1,0:T(8,128)(2,1)S(1)}, u32[]{:S(2)}, u32[]{:S(2)}) %collective-permute-start.54) | collective-permute-done | bytes 524320 | tf_op jit(solution)/shard_map/ppermute | solution.py:25
  540.7 9.2 collective-permute-done.53
  554.1 20.7 %shard_map.145 = (bf16[512,512]{1,0:T(8,128)(2,1)S(1)}, bf16[2,2048,256]{2,1,0:T(8,128)(2,1)S(1)}) custom-call(s32[16]{0:T(128)S(1)} %mul.544.base_ref, s32[2,1,256]{2,1,0:T(1,128)S(1)} %broadcast_in_dim.40.limit_ref, bf16[512,512]{1,0:T(8,128)(2,1)S(1)} %fusion.50.query_ref, bf16[512,512]{1,0:T(8,128)(2,1)S(1)} %fusion.53.grad_ref, ...), custom_call_target="tpu_custom_call" | custom-call | flops 5368709120 | bytes 6291456 | tf_op jit(solution)/shard_map/pallas_call | solution.py:235
  584.2 19.2 %collective-permute-done.55 = bf16[128,2048]{1,0:T(8,128)(2,1)} collective-permute-done((bf16[128,2048]{1,0:T(8,128)(2,1)}, bf16[128,2048]{1,0:T(8,128)(2,1)}, u32[]{:S(2)}, u32[]{:S(2)}) %collective-permute-start.55) | collective-permute-done | bytes 524320 | tf_op jit(solution)/shard_map/ppermute | solution.py:25
  613.8 20.7 %collective-permute-done.58 = bf16[1024,256]{1,0:T(8,128)(2,1)S(1)} collective-permute-done((bf16[1024,256]{1,0:T(8,128)(2,1)S(1)}, bf16[1024,256]{1,0:T(8,128)(2,1)S(1)}, u32[]{:S(2)}, u32[]{:S(2)}) %collective-permute-start.58) | collective-permute-done | bytes 524320 | tf_op jit(solution)/shard_map/ppermute | solution.py:25
  660.0 10.8 %collective-permute-done.69 = bf16[128,2048]{1,0:T(8,128)(2,1)} collective-permute-done((bf16[128,2048]{1,0:T(8,128)(2,1)S(1)}, bf16[128,2048]{1,0:T(8,128)(2,1)}, u32[]{:S(2)}, u32[]{:S(2)}) %collective-permute-start.69) | collective-permute-done | bytes 524320 | tf_op jit(solution)/shard_map/ppermute | solution.py:25
  670.8 9.6 collective-permute-done.67
  680.5 9.9 convolution_convert_fusion.1
  692.7 6.8 fusion.72
  699.6 7.4 fusion.93
  707.1 4.5 fusion.86
  715.8 7.0 convolution_convert_fusion
  735.4 6.6 convolution_convert_fusion.15
  743.9 7.1 convolution_convert_fusion.16
  755.8 6.5 convolution_convert_fusion.4
  777.6 11.1 %collective-permute-done.73 = bf16[128,2048]{1,0:T(8,128)(2,1)S(1)} collective-permute-done((bf16[128,2048]{1,0:T(8,128)(2,1)S(1)}, bf16[128,2048]{1,0:T(8,128)(2,1)S(1)}, u32[]{:S(2)}, u32[]{:S(2)}) %collective-permute-start.73) | collective-permute-done | bytes 524320 | tf_op jit(solution)/shard_map/ppermute | solution.py:25
  788.7 8.8 collective-permute-done.72
  808.8 7.7 collective-permute-done.94
  817.3 20.6 %shard_map.146 = (bf16[512,512]{1,0:T(8,128)(2,1)S(1)}, bf16[2,2048,256]{2,1,0:T(8,128)(2,1)S(1)}) custom-call(s32[16]{0:T(128)S(1)} %mul.544.base_ref, s32[2,1,256]{2,1,0:T(1,128)S(1)} %broadcast_in_dim.40.limit_ref, bf16[512,512]{1,0:T(8,128)(2,1)S(1)} %copy-done.7, bf16[512,512]{1,0:T(8,128)(2,1)S(1)} %copy-done.8, ...), custom_call_target="tpu_custom_call" | custom-call | flops 5368709120 | bytes 6291456 | tf_op jit(solution)/shard_map/pallas_call | solution.py:235
  846.9 26.1 %collective-permute-done.77 = bf16[1024,256]{1,0:T(8,128)(2,1)S(1)} collective-permute-done((bf16[1024,256]{1,0:T(8,128)(2,1)S(1)}, bf16[1024,256]{1,0:T(8,128)(2,1)S(1)}, u32[]{:S(2)}, u32[]{:S(2)}) %collective-permute-start.77) | collective-permute-done | bytes 524320 | tf_op jit(solution)/shard_map/ppermute | solution.py:25
  880.1 8.8 collective-permute-done.74
  899.1 4.8 collective-permute-start.90
  907.0 5.3 collective-permute-start.89
  914.4 6.1 collective-permute-start.112
  928.4 5.9 collective-permute-done.90
  936.8 20.0 %collective-permute-done.89 = bf16[256,2048]{1,0:T(8,128)(2,1)} collective-permute-done((bf16[256,2048]{1,0:T(8,128)(2,1)}, bf16[256,2048]{1,0:T(8,128)(2,1)}, u32[]{:S(2)}, u32[]{:S(2)}) %collective-permute-start.89) | collective-permute-done | bytes 1048608 | tf_op jit(solution)/shard_map/ppermute | solution.py:534
  994.4 16.0 %collective-permute-done.113 = bf16[256,2048]{1,0:T(8,128)(2,1)S(1)} collective-permute-done((bf16[256,2048]{1,0:T(8,128)(2,1)}, bf16[256,2048]{1,0:T(8,128)(2,1)S(1)}, u32[]{:S(2)}, u32[]{:S(2)}) %collective-permute-start.113) | collective-permute-done | bytes 1048608 | tf_op jit(solution)/shard_map/ppermute | solution.py:534
  1016.1 4.4 fusion.23
  1020.6 5.8 collective-permute-done.92
  (712 shorter events, 355.2 us)
Async XLA Ops:
  7.2 164.8 %all-gather.7.cloned.1.call-start = ((), (), s32[]{:S(2)}) async-start(), calls=%async_computation.6 | async-start | bytes 4718592 | tf_op jit(solution)/shard_map/all_gather | solution.py:484
  25.8 222.6 %all-gather.9.cloned.1.call-start = ((), (), s32[]{:S(2)}) async-start(), calls=%async_computation.7 | async-start | bytes 9437184 | tf_op jit(solution)/shard_map/all_gather | solution.py:484
  28.3 24.6 %collective-permute-start.22 = (bf16[256,2048]{1,0:T(8,128)(2,1)}, bf16[256,2048]{1,0:T(8,128)(2,1)S(1)}, u32[]{:S(2)}, u32[]{:S(2)}) collective-permute-start(bf16[256,2048]{1,0:T(8,128)(2,1)} %dynamic-slice_bitcast_fusion.1), channel_id=1, source_target_pairs={{0,16},{16,0},{1,17},{17,1},{2,18},{18,2},{3,19},{19,3},{4,20},{20... | collective-permute-start | bytes 3145736 | tf_op jit(solution)/shard_map/ppermute | solution.py:473
  55.9 206.8 %all-gather.11.cloned.1.call-start = ((), (), s32[]{:S(2)}) async-start(), calls=%async_computation.8 | async-start | bytes 9437184 | tf_op jit(solution)/shard_map/all_gather | solution.py:487
  58.4 26.1 %collective-permute-start.6 = (bf16[8,144,256]{2,1,0:T(8,128)(2,1)S(1)}, bf16[8,144,256]{2,1,0:T(8,128)(2,1)S(1)}, u32[]{:S(2)}, u32[]{:S(2)}) collective-permute-start(bf16[8,144,256]{2,1,0:T(8,128)(2,1)S(1)} %bitcast.382), channel_id=1, source_target_pairs={{0,16},{1,17},{16,0},{17,1},{2,18},{3,19},{18,2},{19,3},{4,20},{5,... | collective-permute-start | bytes 1769480 | tf_op jit(solution)/shard_map/ppermute | solution.py:25
  61.4 45.9 %collective-permute-start.23 = (bf16[2048,256]{1,0:T(8,128)(2,1)}, bf16[2048,256]{1,0:T(8,128)(2,1)}, u32[]{:S(2)}, u32[]{:S(2)}) collective-permute-start(bf16[2048,256]{1,0:T(8,128)(2,1)} %dynamic-slice_bitcast_fusion), channel_id=1, source_target_pairs={{0,16},{16,0},{1,17},{17,1},{2,18},{18,2},{3,19},{19,3},{4,20},{20... | collective-permute-start | bytes 3145736 | tf_op jit(solution)/shard_map/ppermute | solution.py:473
  62.7 23.5 %collective-permute-start.5 = (bf16[8,144,256]{2,1,0:T(8,128)(2,1)S(1)}, bf16[8,144,256]{2,1,0:T(8,128)(2,1)S(1)}, u32[]{:S(2)}, u32[]{:S(2)}) collective-permute-start(bf16[8,144,256]{2,1,0:T(8,128)(2,1)S(1)} %bitcast.383), channel_id=1, source_target_pairs={{0,1},{1,0},{16,17},{17,16},{2,3},{3,2},{18,19},{19,18},{4,5},{5,4... | collective-permute-start | bytes 1769480 | tf_op jit(solution)/shard_map/ppermute | solution.py:25
  120.2 201.0 %all-gather.13.cloned.1.call-start = ((), (), s32[]{:S(2)}) async-start(), calls=%async_computation.9 | async-start | bytes 4718592 | tf_op jit(solution)/shard_map/all_gather | solution.py:484
  120.7 292.4 %all-gather.17.cloned.1.call-start = ((), (), s32[]{:S(2)}) async-start(), calls=%async_computation.11 | async-start | bytes 9437184 | tf_op jit(solution)/shard_map/all_gather | solution.py:484
  121.3 338.4 %all-gather.15.cloned.1.call-start = ((), (), s32[]{:S(2)}) async-start(), calls=%async_computation.10 | async-start | bytes 9437184 | tf_op jit(solution)/shard_map/all_gather | solution.py:487
  125.7 24.4 %collective-permute-start.17 = (bf16[8,128,256]{2,1,0:T(8,128)(2,1)S(1)}, bf16[8,128,256]{2,1,0:T(8,128)(2,1)S(1)}, u32[]{:S(2)}, u32[]{:S(2)}) collective-permute-start(bf16[8,128,256]{2,1,0:T(8,128)(2,1)S(1)} %constant_dynamic-update-slice_fusion), channel_id=1, source_target_pairs={{0,16},{1,17},{16,0},{17,1},{2,18},{3,19},{18,2},{19,3},{4,20},{5,... | collective-permute-start | bytes 1572872 | tf_op jit(solution)/shard_map/ppermute | solution.py:25
  126.3 23.9 %collective-permute-start.16 = (bf16[8,128,256]{2,1,0:T(8,128)(2,1)S(1)}, bf16[8,128,256]{2,1,0:T(8,128)(2,1)S(1)}, u32[]{:S(2)}, u32[]{:S(2)}) collective-permute-start(bf16[8,128,256]{2,1,0:T(8,128)(2,1)S(1)} %constant_dynamic-update-slice_fusion), channel_id=1, source_target_pairs={{0,1},{1,0},{16,17},{17,16},{2,3},{3,2},{18,19},{19,18},{4,5},{5,4... | collective-permute-start | bytes 1572872 | tf_op jit(solution)/shard_map/ppermute | solution.py:25
  126.8 34.7 %collective-permute-start.10 = (bf16[128,2048]{1,0:T(8,128)(2,1)S(1)}, bf16[128,2048]{1,0:T(8,128)(2,1)}, u32[]{:S(2)}, u32[]{:S(2)}) collective-permute-start(bf16[128,2048]{1,0:T(8,128)(2,1)S(1)} %fusion.64), channel_id=1, source_target_pairs={{0,17},{1,16},{16,1},{17,0},{2,19},{3,18},{18,3},{19,2},{4,21},{5,... | collective-permute-start | bytes 1572872 | tf_op jit(solution)/shard_map/ppermute | solution.py:25
  129.2 42.8 %collective-permute-start.9 = (bf16[128,2048]{1,0:T(8,128)(2,1)S(1)}, bf16[128,2048]{1,0:T(8,128)(2,1)}, u32[]{:S(2)}, u32[]{:S(2)}) collective-permute-start(bf16[128,2048]{1,0:T(8,128)(2,1)S(1)} %fusion.64), channel_id=1, source_target_pairs={{0,16},{1,17},{16,0},{17,1},{2,18},{3,19},{18,2},{19,3},{4,20},{5,... | collective-permute-start | bytes 1572872 | tf_op jit(solution)/shard_map/ppermute | solution.py:25
  138.9 33.1 %collective-permute-start.8 = (bf16[128,2048]{1,0:T(8,128)(2,1)S(1)}, bf16[128,2048]{1,0:T(8,128)(2,1)}, u32[]{:S(2)}, u32[]{:S(2)}) collective-permute-start(bf16[128,2048]{1,0:T(8,128)(2,1)S(1)} %fusion.64), channel_id=1, source_target_pairs={{0,1},{1,0},{16,17},{17,16},{2,3},{3,2},{18,19},{19,18},{4,5},{5,4... | collective-permute-start | bytes 1572872 | tf_op jit(solution)/shard_map/ppermute | solution.py:25
  193.6 25.2 %collective-permute-start.19 = (bf16[128,2048]{1,0:T(8,128)(2,1)}, bf16[128,2048]{1,0:T(8,128)(2,1)S(1)}, u32[]{:S(2)}, u32[]{:S(2)}) collective-permute-start(bf16[128,2048]{1,0:T(8,128)(2,1)} %get-tuple-element.175), channel_id=1, source_target_pairs={{0,1},{1,0},{16,17},{17,16},{2,3},{3,2},{18,19},{19,18},{4,5},{5,4... | collective-permute-start | bytes 1572872 | tf_op jit(solution)/shard_map/ppermute | solution.py:25
  194.9 23.8 %collective-permute-start.21 = (bf16[128,2048]{1,0:T(8,128)(2,1)}, bf16[128,2048]{1,0:T(8,128)(2,1)S(1)}, u32[]{:S(2)}, u32[]{:S(2)}) collective-permute-start(bf16[128,2048]{1,0:T(8,128)(2,1)} %get-tuple-element.176), channel_id=1, source_target_pairs={{0,17},{1,16},{16,1},{17,0},{2,19},{3,18},{18,3},{19,2},{4,21},{5,... | collective-permute-start | bytes 1572872 | tf_op jit(solution)/shard_map/ppermute | solution.py:25
  196.5 23.9 %collective-permute-start.20 = (bf16[128,2048]{1,0:T(8,128)(2,1)}, bf16[128,2048]{1,0:T(8,128)(2,1)}, u32[]{:S(2)}, u32[]{:S(2)}) collective-permute-start(bf16[128,2048]{1,0:T(8,128)(2,1)} %get-tuple-element.177), channel_id=1, source_target_pairs={{0,16},{1,17},{16,0},{17,1},{2,18},{3,19},{18,2},{19,3},{4,20},{5,... | collective-permute-start | bytes 1572872 | tf_op jit(solution)/shard_map/ppermute | solution.py:25
  197.1 462.9 %reduce-scatter.9.cloned.1.call-start = ((), (), s32[]{:S(2)}) async-start(), calls=%async_computation.13 | async-start | bytes 9437184 | tf_op jit(solution)/shard_map/reduce_scatter | solution.py:375
  223.9 24.5 %collective-permute-start.24 = (bf16[128,2048]{1,0:T(8,128)(2,1)}, bf16[128,2048]{1,0:T(8,128)(2,1)}, u32[]{:S(2)}, u32[]{:S(2)}) collective-permute-start(bf16[128,2048]{1,0:T(8,128)(2,1)} %add_convert_fusion.5), channel_id=1, source_target_pairs={{0,1},{1,0},{16,17},{17,16},{2,3},{3,2},{18,19},{19,18},{4,5},{5,4... | collective-permute-start | bytes 1572872 | tf_op jit(solution)/shard_map/ppermute | solution.py:25
  225.4 33.4 %collective-permute-start.28 = (bf16[128,2048]{1,0:T(8,128)(2,1)}, bf16[128,2048]{1,0:T(8,128)(2,1)}, u32[]{:S(2)}, u32[]{:S(2)}) collective-permute-start(bf16[128,2048]{1,0:T(8,128)(2,1)} %add_convert_fusion.5), channel_id=1, source_target_pairs={{0,17},{1,16},{16,1},{17,0},{2,19},{3,18},{18,3},{19,2},{4,21},{5,... | collective-permute-start | bytes 1572872 | tf_op jit(solution)/shard_map/ppermute | solution.py:25
  226.9 28.0 %collective-permute-start.26 = (bf16[128,2048]{1,0:T(8,128)(2,1)}, bf16[128,2048]{1,0:T(8,128)(2,1)}, u32[]{:S(2)}, u32[]{:S(2)}) collective-permute-start(bf16[128,2048]{1,0:T(8,128)(2,1)} %add_convert_fusion.5), channel_id=1, source_target_pairs={{0,16},{1,17},{16,0},{17,1},{2,18},{3,19},{18,2},{19,3},{4,20},{5,... | collective-permute-start | bytes 1572872 | tf_op jit(solution)/shard_map/ppermute | solution.py:25
  305.4 24.8 %collective-permute-start.31 = (bf16[128,2048]{1,0:T(8,128)(2,1)S(1)}, bf16[128,2048]{1,0:T(8,128)(2,1)}, u32[]{:S(2)}, u32[]{:S(2)}) collective-permute-start(bf16[128,2048]{1,0:T(8,128)(2,1)S(1)} %fusion.61), channel_id=1, source_target_pairs={{0,16},{1,17},{16,0},{17,1},{2,18},{3,19},{18,2},{19,3},{4,20},{5,... | collective-permute-start | bytes 1572872 | tf_op jit(solution)/shard_map/ppermute | solution.py:25
  306.0 25.0 %collective-permute-start.30 = (bf16[128,2048]{1,0:T(8,128)(2,1)S(1)}, bf16[128,2048]{1,0:T(8,128)(2,1)}, u32[]{:S(2)}, u32[]{:S(2)}) collective-permute-start(bf16[128,2048]{1,0:T(8,128)(2,1)S(1)} %fusion.61), channel_id=1, source_target_pairs={{0,1},{1,0},{16,17},{17,16},{2,3},{3,2},{18,19},{19,18},{4,5},{5,4... | collective-permute-start | bytes 1572872 | tf_op jit(solution)/shard_map/ppermute | solution.py:25
  310.9 31.4 %collective-permute-start.39 = (bf16[8,128,256]{2,1,0:T(8,128)(2,1)}, bf16[8,128,256]{2,1,0:T(8,128)(2,1)}, u32[]{:S(2)}, u32[]{:S(2)}) collective-permute-start(bf16[8,128,256]{2,1,0:T(8,128)(2,1)} %constant_dynamic-update-slice_fusion.5), channel_id=1, source_target_pairs={{0,17},{1,16},{16,1},{17,0},{2,19},{3,18},{18,3},{19,2},{4,21},{5,... | collective-permute-start | bytes 1572872 | tf_op jit(solution)/shard_map/ppermute | solution.py:25
  311.7 37.1 %collective-permute-start.38 = (bf16[8,128,256]{2,1,0:T(8,128)(2,1)}, bf16[8,128,256]{2,1,0:T(8,128)(2,1)}, u32[]{:S(2)}, u32[]{:S(2)}) collective-permute-start(bf16[8,128,256]{2,1,0:T(8,128)(2,1)} %constant_dynamic-update-slice_fusion.5), channel_id=1, source_target_pairs={{0,16},{1,17},{16,0},{17,1},{2,18},{3,19},{18,2},{19,3},{4,20},{5,... | collective-permute-start | bytes 1572872 | tf_op jit(solution)/shard_map/ppermute | solution.py:25
  320.5 29.2 %collective-permute-start.37 = (bf16[8,128,256]{2,1,0:T(8,128)(2,1)}, bf16[8,128,256]{2,1,0:T(8,128)(2,1)}, u32[]{:S(2)}, u32[]{:S(2)}) collective-permute-start(bf16[8,128,256]{2,1,0:T(8,128)(2,1)} %constant_dynamic-update-slice_fusion.5), channel_id=1, source_target_pairs={{0,1},{1,0},{16,17},{17,16},{2,3},{3,2},{18,19},{19,18},{4,5},{5,4... | collective-permute-start | bytes 1572872 | tf_op jit(solution)/shard_map/ppermute | solution.py:25
  367.6 25.2 %collective-permute-start.40 = (bf16[128,2048]{1,0:T(8,128)(2,1)S(1)}, bf16[128,2048]{1,0:T(8,128)(2,1)S(1)}, u32[]{:S(2)}, u32[]{:S(2)}) collective-permute-start(bf16[128,2048]{1,0:T(8,128)(2,1)S(1)} %get-tuple-element.172), channel_id=1, source_target_pairs={{0,1},{1,0},{16,17},{17,16},{2,3},{3,2},{18,19},{19,18},{4,5},{5,4... | collective-permute-start | bytes 1572872 | tf_op jit(solution)/shard_map/ppermute | solution.py:25
  368.4 24.4 %collective-permute-start.42 = (bf16[128,2048]{1,0:T(8,128)(2,1)S(1)}, bf16[128,2048]{1,0:T(8,128)(2,1)S(1)}, u32[]{:S(2)}, u32[]{:S(2)}) collective-permute-start(bf16[128,2048]{1,0:T(8,128)(2,1)S(1)} %get-tuple-element.173), channel_id=1, source_target_pairs={{0,17},{1,16},{16,1},{17,0},{2,19},{3,18},{18,3},{19,2},{4,21},{5,... | collective-permute-start | bytes 1572872 | tf_op jit(solution)/shard_map/ppermute | solution.py:25
  370.5 23.5 %collective-permute-start.41 = (bf16[128,2048]{1,0:T(8,128)(2,1)S(1)}, bf16[128,2048]{1,0:T(8,128)(2,1)S(1)}, u32[]{:S(2)}, u32[]{:S(2)}) collective-permute-start(bf16[128,2048]{1,0:T(8,128)(2,1)S(1)} %get-tuple-element.174), channel_id=1, source_target_pairs={{0,16},{1,17},{16,0},{17,1},{2,18},{3,19},{18,2},{19,3},{4,20},{5,... | collective-permute-start | bytes 1572872 | tf_op jit(solution)/shard_map/ppermute | solution.py:25
  397.9 25.0 %collective-permute-start.47 = (bf16[128,2048]{1,0:T(8,128)(2,1)}, bf16[128,2048]{1,0:T(8,128)(2,1)}, u32[]{:S(2)}, u32[]{:S(2)}) collective-permute-start(bf16[128,2048]{1,0:T(8,128)(2,1)} %add_convert_fusion.3), channel_id=1, source_target_pairs={{0,16},{1,17},{16,0},{17,1},{2,18},{3,19},{18,2},{19,3},{4,20},{5,... | collective-permute-start | bytes 1572872 | tf_op jit(solution)/shard_map/ppermute | solution.py:25
  398.5 25.5 %collective-permute-start.46 = (bf16[128,2048]{1,0:T(8,128)(2,1)}, bf16[128,2048]{1,0:T(8,128)(2,1)}, u32[]{:S(2)}, u32[]{:S(2)}) collective-permute-start(bf16[128,2048]{1,0:T(8,128)(2,1)} %add_convert_fusion.3), channel_id=1, source_target_pairs={{0,1},{1,0},{16,17},{17,16},{2,3},{3,2},{18,19},{19,18},{4,5},{5,4... | collective-permute-start | bytes 1572872 | tf_op jit(solution)/shard_map/ppermute | solution.py:25
  402.0 33.4 %collective-permute-start.45 = (bf16[128,2048]{1,0:T(8,128)(2,1)}, bf16[128,2048]{1,0:T(8,128)(2,1)}, u32[]{:S(2)}, u32[]{:S(2)}) collective-permute-start(bf16[128,2048]{1,0:T(8,128)(2,1)} %convert_element_type.550), channel_id=1, source_target_pairs={{0,17},{1,16},{16,1},{17,0},{2,19},{3,18},{18,3},{19,2},{4,21},{5,... | collective-permute-start | bytes 1572872 | tf_op jit(solution)/shard_map/ppermute | solution.py:25
  403.3 39.9 %collective-permute-start.44 = (bf16[128,2048]{1,0:T(8,128)(2,1)}, bf16[128,2048]{1,0:T(8,128)(2,1)}, u32[]{:S(2)}, u32[]{:S(2)}) collective-permute-start(bf16[128,2048]{1,0:T(8,128)(2,1)} %convert_element_type.550), channel_id=1, source_target_pairs={{0,16},{1,17},{16,0},{17,1},{2,18},{3,19},{18,2},{19,3},{4,20},{5,... | collective-permute-start | bytes 1572872 | tf_op jit(solution)/shard_map/ppermute | solution.py:25
  412.7 31.7 %collective-permute-start.43 = (bf16[128,2048]{1,0:T(8,128)(2,1)}, bf16[128,2048]{1,0:T(8,128)(2,1)}, u32[]{:S(2)}, u32[]{:S(2)}) collective-permute-start(bf16[128,2048]{1,0:T(8,128)(2,1)} %convert_element_type.550), channel_id=1, source_target_pairs={{0,1},{1,0},{16,17},{17,16},{2,3},{3,2},{18,19},{19,18},{4,5},{5,4... | collective-permute-start | bytes 1572872 | tf_op jit(solution)/shard_map/ppermute | solution.py:25
  452.6 207.4 %reduce-scatter.7.cloned.1.call-start = ((), (), s32[]{:S(2)}) async-start(), calls=%async_computation.12 | async-start | bytes 9437184 | tf_op jit(solution)/shard_map/reduce_scatter | solution.py:371
  480.3 320.9 %reduce-scatter.15.cloned.1.call-start = ((), (), s32[]{:S(2)}) async-start(), calls=%async_computation.16 | async-start | bytes 2621440 | tf_op jit(solution)/shard_map/reduce_scatter | solution.py:365
  527.1 22.8 %collective-permute-start.53 = (bf16[128,2048]{1,0:T(8,128)(2,1)S(1)}, bf16[128,2048]{1,0:T(8,128)(2,1)S(1)}, u32[]{:S(2)}, u32[]{:S(2)}) collective-permute-start(bf16[128,2048]{1,0:T(8,128)(2,1)S(1)} %fusion.137), channel_id=1, source_target_pairs={{0,16},{1,17},{16,0},{17,1},{2,18},{3,19},{18,2},{19,3},{4,20},{5,... | collective-permute-start | bytes 1572872 | tf_op jit(solution)/shard_map/ppermute | solution.py:25
  578.1 25.3 %collective-permute-start.55 = (bf16[128,2048]{1,0:T(8,128)(2,1)}, bf16[128,2048]{1,0:T(8,128)(2,1)}, u32[]{:S(2)}, u32[]{:S(2)}) collective-permute-start(bf16[128,2048]{1,0:T(8,128)(2,1)} %get-tuple-element.166), channel_id=1, source_target_pairs={{0,1},{1,0},{16,17},{17,16},{2,3},{3,2},{18,19},{19,18},{4,5},{5,4... | collective-permute-start | bytes 1572872 | tf_op jit(solution)/shard_map/ppermute | solution.py:25
  579.5 23.9 %collective-permute-start.57 = (bf16[128,2048]{1,0:T(8,128)(2,1)}, bf16[128,2048]{1,0:T(8,128)(2,1)}, u32[]{:S(2)}, u32[]{:S(2)}) collective-permute-start(bf16[128,2048]{1,0:T(8,128)(2,1)} %get-tuple-element.167), channel_id=1, source_target_pairs={{0,17},{1,16},{16,1},{17,0},{2,19},{3,18},{18,3},{19,2},{4,21},{5,... | collective-permute-start | bytes 1572872 | tf_op jit(solution)/shard_map/ppermute | solution.py:25
  581.0 23.6 %collective-permute-start.56 = (bf16[128,2048]{1,0:T(8,128)(2,1)}, bf16[128,2048]{1,0:T(8,128)(2,1)}, u32[]{:S(2)}, u32[]{:S(2)}) collective-permute-start(bf16[128,2048]{1,0:T(8,128)(2,1)} %get-tuple-element.168), channel_id=1, source_target_pairs={{0,16},{1,17},{16,0},{17,1},{2,18},{3,19},{18,2},{19,3},{4,20},{5,... | collective-permute-start | bytes 1572872 | tf_op jit(solution)/shard_map/ppermute | solution.py:25
  608.7 38.7 %collective-permute-start.93 = (bf16[1024,1024]{1,0:T(8,128)(2,1)S(1)}, bf16[1024,1024]{1,0:T(8,128)(2,1)S(1)}, u32[]{:S(2)}, u32[]{:S(2)}) collective-permute-start(bf16[1024,1024]{1,0:T(8,128)(2,1)S(1)} %pad_maximum_fusion.11), channel_id=1, source_target_pairs={{0,2},{2,0},{4,6},{6,4},{8,10},{10,8},{12,14},{14,12},{1,3},{3,1},... | collective-permute-start | bytes 6291464 | tf_op jit(solution)/shard_map/ppermute | solution.py:29
  610.3 24.2 %collective-permute-start.58 = (bf16[1024,256]{1,0:T(8,128)(2,1)S(1)}, bf16[1024,256]{1,0:T(8,128)(2,1)S(1)}, u32[]{:S(2)}, u32[]{:S(2)}) collective-permute-start(bf16[1024,256]{1,0:T(8,128)(2,1)S(1)} %get-tuple-element.163), channel_id=1, source_target_pairs={{0,1},{1,0},{16,17},{17,16},{2,3},{3,2},{18,19},{19,18},{4,5},{5,4... | collective-permute-start | bytes 1572872 | tf_op jit(solution)/shard_map/ppermute | solution.py:25
  611.8 22.7 %collective-permute-start.60 = (bf16[1024,256]{1,0:T(8,128)(2,1)S(1)}, bf16[1024,256]{1,0:T(8,128)(2,1)S(1)}, u32[]{:S(2)}, u32[]{:S(2)}) collective-permute-start(bf16[1024,256]{1,0:T(8,128)(2,1)S(1)} %get-tuple-element.164), channel_id=1, source_target_pairs={{0,17},{1,16},{16,1},{17,0},{2,19},{3,18},{18,3},{19,2},{4,21},{5,... | collective-permute-start | bytes 1572872 | tf_op jit(solution)/shard_map/ppermute | solution.py:25
  649.8 262.6 %reduce-scatter.11.cloned.1.call-start = ((), (), s32[]{:S(2)}) async-start(), calls=%async_computation.14 | async-start | bytes 9437184 | tf_op jit(solution)/shard_map/reduce_scatter | solution.py:375
  657.3 23.2 %collective-permute-start.67 = (bf16[128,2048]{1,0:T(8,128)(2,1)S(1)}, bf16[128,2048]{1,0:T(8,128)(2,1)}, u32[]{:S(2)}, u32[]{:S(2)}) collective-permute-start(bf16[128,2048]{1,0:T(8,128)(2,1)S(1)} %add_convert_fusion.2), channel_id=1, source_target_pairs={{0,16},{1,17},{16,0},{17,1},{2,18},{3,19},{18,2},{19,3},{4,20},{5,... | collective-permute-start | bytes 1572872 | tf_op jit(solution)/shard_map/ppermute | solution.py:25
  690.4 296.1 %reduce-scatter.17.cloned.1.call-start = ((), (), s32[]{:S(2)}) async-start(), calls=%async_computation.17 | async-start | bytes 9437184 | tf_op jit(solution)/shard_map/reduce_scatter | solution.py:371
  722.8 292.0 %reduce-scatter.13.cloned.1.call-start = ((), (), s32[]{:S(2)}) async-start(), calls=%async_computation.15 | async-start | bytes 2621440 | tf_op jit(solution)/shard_map/reduce_scatter | solution.py:365
  734.0 29.4 %collective-permute-start.109 = (bf16[64,256]{1,0:T(8,128)(2,1)S(1)}, bf16[64,256]{1,0:T(8,128)(2,1)S(1)}, u32[]{:S(2)}, u32[]{:S(2)}) collective-permute-start(bf16[64,256]{1,0:T(8,128)(2,1)S(1)} %get-tuple-element.201), channel_id=1, source_target_pairs={{0,4},{2,6},{12,8},{14,10},{1,5},{3,7},{13,9},{15,11},{16,20},{18,... | collective-permute-start | bytes 98312 | tf_op jit(solution)/shard_map/ppermute | solution.py:268
  775.5 22.9 %collective-permute-start.71 = (bf16[128,2048]{1,0:T(8,128)(2,1)S(1)}, bf16[128,2048]{1,0:T(8,128)(2,1)S(1)}, u32[]{:S(2)}, u32[]{:S(2)}) collective-permute-start(bf16[128,2048]{1,0:T(8,128)(2,1)S(1)} %fusion.102), channel_id=1, source_target_pairs={{0,1},{1,0},{16,17},{17,16},{2,3},{3,2},{18,19},{19,18},{4,5},{5,4... | collective-permute-start | bytes 1572872 | tf_op jit(solution)/shard_map/ppermute | solution.py:25
  838.0 35.0 %collective-permute-start.77 = (bf16[1024,256]{1,0:T(8,128)(2,1)S(1)}, bf16[1024,256]{1,0:T(8,128)(2,1)S(1)}, u32[]{:S(2)}, u32[]{:S(2)}) collective-permute-start(bf16[1024,256]{1,0:T(8,128)(2,1)S(1)} %get-tuple-element.157), channel_id=1, source_target_pairs={{0,1},{1,0},{16,17},{17,16},{2,3},{3,2},{18,19},{19,18},{4,5},{5,4... | collective-permute-start | bytes 1572872 | tf_op jit(solution)/shard_map/ppermute | solution.py:25
  839.1 39.1 %collective-permute-start.79 = (bf16[1024,256]{1,0:T(8,128)(2,1)S(1)}, bf16[1024,256]{1,0:T(8,128)(2,1)S(1)}, u32[]{:S(2)}, u32[]{:S(2)}) collective-permute-start(bf16[1024,256]{1,0:T(8,128)(2,1)S(1)} %get-tuple-element.158), channel_id=1, source_target_pairs={{0,17},{1,16},{16,1},{17,0},{2,19},{3,18},{18,3},{19,2},{4,21},{5,... | collective-permute-start | bytes 1572872 | tf_op jit(solution)/shard_map/ppermute | solution.py:25
  841.9 37.0 %collective-permute-start.78 = (bf16[1024,256]{1,0:T(8,128)(2,1)S(1)}, bf16[1024,256]{1,0:T(8,128)(2,1)S(1)}, u32[]{:S(2)}, u32[]{:S(2)}) collective-permute-start(bf16[1024,256]{1,0:T(8,128)(2,1)S(1)} %get-tuple-element.159), channel_id=1, source_target_pairs={{0,16},{1,17},{16,0},{17,1},{2,18},{3,19},{18,2},{19,3},{4,20},{5,... | collective-permute-start | bytes 1572872 | tf_op jit(solution)/shard_map/ppermute | solution.py:25
  843.4 45.5 %collective-permute-start.74 = (bf16[128,2048]{1,0:T(8,128)(2,1)S(1)}, bf16[128,2048]{1,0:T(8,128)(2,1)S(1)}, u32[]{:S(2)}, u32[]{:S(2)}) collective-permute-start(bf16[128,2048]{1,0:T(8,128)(2,1)S(1)} %get-tuple-element.160), channel_id=1, source_target_pairs={{0,1},{1,0},{16,17},{17,16},{2,3},{3,2},{18,19},{19,18},{4,5},{5,4... | collective-permute-start | bytes 1572872 | tf_op jit(solution)/shard_map/ppermute | solution.py:25
  844.5 44.4 %collective-permute-start.76 = (bf16[128,2048]{1,0:T(8,128)(2,1)S(1)}, bf16[128,2048]{1,0:T(8,128)(2,1)S(1)}, u32[]{:S(2)}, u32[]{:S(2)}) collective-permute-start(bf16[128,2048]{1,0:T(8,128)(2,1)S(1)} %get-tuple-element.161), channel_id=1, source_target_pairs={{0,17},{1,16},{16,1},{17,0},{2,19},{3,18},{18,3},{19,2},{4,21},{5,... | collective-permute-start | bytes 1572872 | tf_op jit(solution)/shard_map/ppermute | solution.py:25
  878.2 28.8 %collective-permute-start.84 = (bf16[128,2048]{1,0:T(8,128)(2,1)S(1)}, bf16[128,2048]{1,0:T(8,128)(2,1)}, u32[]{:S(2)}, u32[]{:S(2)}) collective-permute-start(bf16[128,2048]{1,0:T(8,128)(2,1)S(1)} %copy-done.86), channel_id=1, source_target_pairs={{0,1},{1,0},{16,17},{17,16},{2,3},{3,2},{18,19},{19,18},{4,5},{5,4... | collective-permute-start | bytes 1572872 | tf_op jit(solution)/shard_map/ppermute | solution.py:25
  878.9 33.5 %collective-permute-start.86 = (bf16[128,2048]{1,0:T(8,128)(2,1)S(1)}, bf16[128,2048]{1,0:T(8,128)(2,1)}, u32[]{:S(2)}, u32[]{:S(2)}) collective-permute-start(bf16[128,2048]{1,0:T(8,128)(2,1)S(1)} %copy-done.85), channel_id=1, source_target_pairs={{0,17},{1,16},{16,1},{17,0},{2,19},{3,18},{18,3},{19,2},{4,21},{5,... | collective-permute-start | bytes 1572872 | tf_op jit(solution)/shard_map/ppermute | solution.py:25
  899.1 35.1 %collective-permute-start.90 = (bf16[2048,256]{1,0:T(8,128)(2,1)}, bf16[2048,256]{1,0:T(8,128)(2,1)}, u32[]{:S(2)}, u32[]{:S(2)}) collective-permute-start(bf16[2048,256]{1,0:T(8,128)(2,1)} %reduce-scatter.9.cloned.1.call-done), channel_id=1, source_target_pairs={{0,16},{1,17},{2,18},{3,19},{4,20},{5,21},{6,22},{7,23},{8,24},{9,... | collective-permute-start | bytes 3145736 | tf_op jit(solution)/shard_map/ppermute | solution.py:534
  907.0 49.7 %collective-permute-start.89 = (bf16[256,2048]{1,0:T(8,128)(2,1)}, bf16[256,2048]{1,0:T(8,128)(2,1)}, u32[]{:S(2)}, u32[]{:S(2)}) collective-permute-start(bf16[256,2048]{1,0:T(8,128)(2,1)} %reduce-scatter.7.cloned.1.call-done), channel_id=1, source_target_pairs={{0,16},{1,17},{2,18},{3,19},{4,20},{5,21},{6,22},{7,23},{8,24},{9,... | collective-permute-start | bytes 3145736 | tf_op jit(solution)/shard_map/ppermute | solution.py:534
  912.4 45.3 %collective-permute-start.91 = (bf16[2048,256]{1,0:T(8,128)(2,1)}, bf16[2048,256]{1,0:T(8,128)(2,1)}, u32[]{:S(2)}, u32[]{:S(2)}) collective-permute-start(bf16[2048,256]{1,0:T(8,128)(2,1)} %reduce-scatter.11.cloned.1.call-done), channel_id=1, source_target_pairs={{16,0},{17,1},{18,2},{19,3},{20,4},{21,5},{22,6},{23,7},{24,8},{25... | collective-permute-start | bytes 3145736 | tf_op jit(solution)/shard_map/ppermute | solution.py:534
  914.4 75.2 %collective-permute-start.112 = (bf16[64,256]{1,0:T(8,128)(2,1)S(1)}, bf16[64,256]{1,0:T(8,128)(2,1)}, u32[]{:S(2)}, u32[]{:S(2)}) collective-permute-start(bf16[64,256]{1,0:T(8,128)(2,1)S(1)} %fusion.150), channel_id=1, source_target_pairs={{0,16},{1,17},{2,18},{3,19},{4,20},{5,21},{6,22},{7,23},{8,24},{9,... | collective-permute-start | bytes 98312 | tf_op jit(solution)/shard_map/ppermute | solution.py:534
  924.3 34.7 %collective-permute-start.97 = (bf16[128,256]{1,0:T(8,128)(2,1)S(1)}, bf16[128,256]{1,0:T(8,128)(2,1)S(1)}, u32[]{:S(2)}, u32[]{:S(2)}) collective-permute-start(bf16[128,256]{1,0:T(8,128)(2,1)S(1)} %fusion.141), channel_id=1, source_target_pairs={{0,17},{1,16},{16,1},{17,0},{2,19},{3,18},{18,3},{19,2},{4,21},{5,... | collective-permute-start | bytes 196616 | tf_op jit(solution)/shard_map/ppermute | solution.py:25
  934.3 27.6 %collective-permute-start.96 = (bf16[128,256]{1,0:T(8,128)(2,1)S(1)}, bf16[128,256]{1,0:T(8,128)(2,1)S(1)}, u32[]{:S(2)}, u32[]{:S(2)}) collective-permute-start(bf16[128,256]{1,0:T(8,128)(2,1)S(1)} %fusion.141), channel_id=1, source_target_pairs={{0,16},{1,17},{16,0},{17,1},{2,18},{3,19},{18,2},{19,3},{4,20},{5,... | collective-permute-start | bytes 196616 | tf_op jit(solution)/shard_map/ppermute | solution.py:25
  986.5 23.9 %collective-permute-start.113 = (bf16[256,2048]{1,0:T(8,128)(2,1)}, bf16[256,2048]{1,0:T(8,128)(2,1)S(1)}, u32[]{:S(2)}, u32[]{:S(2)}) collective-permute-start(bf16[256,2048]{1,0:T(8,128)(2,1)} %reduce-scatter.17.cloned.1.call-done), channel_id=1, source_target_pairs={{16,0},{17,1},{18,2},{19,3},{20,4},{21,5},{22,6},{23,7},{24,8},{25... | collective-permute-start | bytes 3145736 | tf_op jit(solution)/shard_map/ppermute | solution.py:534
  (208 other events, 2875.1 us)
Sparse Core Ops, SparseCore 0:
  25.9 49.6 all-gather.6
  77.7 86.4 all-gather.8
  166.5 80.9 all-gather.10
  248.9 45.3 all-gather.12
  296.3 80.8 all-gather.16
  378.6 81.0 all-gather.14
  462.0 87.7 reduce-scatter.8
  552.1 87.9 reduce-scatter.6
  649.9 42.7 reduce-scatter.14
  694.9 91.0 reduce-scatter.10
  788.4 87.7 reduce-scatter.16
  957.8 46.1 reduce-scatter.12
